TPU v7x, 128 devices: a whole 4x4x4 slice. The times are simulated.
128 devices in a mesh: gx: 16 (over y, x), gy: 8 (over z, core).
Axes of the slice: x: 4, y: 4, z: 4, core: 2. Of those that a mesh axis runs over, the one named last changes fastest.
Arguments:
- right_side: float32 [8, 64, 64, 256], P(None, 'gx', 'gy'), may hold values from -6 to 6
- fine_ids: int32 [64, 64, 256], P('gx', 'gy'), may hold values from 0 to 255, as said below
- coarse_diag: float32 [32, 16, 64], P('gx', 'gy'), as said below
- coarse_links: float32 [6, 32, 16, 64], P(None, 'gx', 'gy'), as said below
- coarse_ids: int32 [32, 16, 64], P('gx', 'gy'), may hold values from 0 to 2047, as said below
- coarsest_inverse: float32 [2048, 2048], P(('gx', 'gy')), as said below
Outputs:
- solution: float32 [8, 64, 64, 256], P(None, 'gx', 'gy')
Inputs may be any that keep to these rules, and one draw needn't show every extreme that they name: `fine_ids`: each cell names an aggregate within its device's tile whose local coordinates differ by at most one along each dimension from (cell's local first coordinate // 2, local second coordinate // 4, third coordinate // 4). `coarse_diag`: each entry exceeds the sum of the six couplings of its aggregate. `coarse_links`: the lower coupling of an aggregate along a dimension equals the upper coupling of the aggregate below it; couplings past the grid's ends are zero. `coarse_ids`: names a coarsest unknown for each aggregate. `coarsest_inverse`: symmetric.
All inputs are finite; a program needn't handle non-finite values.
Results may differ from a plain program's by a relative error of at most 0.00013.
Values sent between devices are 32-bit elements; how exact they have to be, the bound alone decides.
No kernel may reach another device: no remote copies, remote signals or barrier semaphores. Data moves between devices by JAX's collectives and lax.ppermute only.
A program may use at most 256 MiB of HBM per device.

v0:
```python
import math

import jax
import jax.numpy as jnp
from jax import lax
from jax.sharding import PartitionSpec as P

DEGREE = 3


prolong_weight = 1.0 / 9.0
fine_low = 2.0 / 30.0
fine_high = 2.0
coarse_low = 0.19
coarse_high = 1.9


def extended(block, sides, width):
    for axis, dim in sides:
        count = lax.axis_size(axis)
        forward = [(i, i + 1) for i in range(count - 1)]
        backward = [(target, source) for source, target in forward]
        low = lax.ppermute(
            lax.slice_in_dim(block, block.shape[dim] - width, None, axis=dim), axis, forward
        )
        high = lax.ppermute(lax.slice_in_dim(block, 0, width, axis=dim), axis, backward)
        block = jnp.concatenate([low, block, high], axis=dim)
    return block


def stencil(padded):
    center = padded[:, 1:-1, 1:-1, :]
    along = jnp.pad(center, ((0, 0), (0, 0), (0, 0), (1, 1)))
    beside = padded[:, 2:, 1:-1, :] + padded[:, :-2, 1:-1, :]
    beside = beside + padded[:, 1:-1, 2:, :] + padded[:, 1:-1, :-2, :]
    beside = beside + along[:, :, :, 2:] + along[:, :, :, :-2]
    return 6.0 * center - beside


def chebyshev(operator, inverse_diag, target, guess, low, high):
    theta = (high + low) / 2.0
    delta = (high - low) / 2.0
    sigma = theta / delta
    rho_old = 1.0 / sigma
    if guess is None:
        residual = target
        iterate = jnp.zeros_like(target)
    else:
        residual = target - operator(guess)
        iterate = guess
    update = inverse_diag * residual / theta
    iterate = iterate + update
    for step in range(DEGREE - 1):
        residual = residual - operator(update)
        rho_new = 1.0 / (2.0 * sigma - rho_old)
        update = rho_new * rho_old * update + 2.0 * rho_new / delta * inverse_diag * residual
        iterate = iterate + update
        rho_old = rho_new
    return iterate


def fine_apply(field):
    padded = extended(field, (("gx", 1), ("gy", 2)), 1)
    return stencil(padded)


def fine_smooth(target, guess):
    return chebyshev(fine_apply, 1.0 / 6.0, target, guess, fine_low, fine_high)


def block_codes(fine_ids, agg_shape):
    agg_x, agg_y, agg_z = agg_shape
    tile_shape = fine_ids.shape
    home_x = lax.broadcasted_iota(jnp.int32, tile_shape, 0) // (tile_shape[0] // agg_x)
    home_y = lax.broadcasted_iota(jnp.int32, tile_shape, 1) // (tile_shape[1] // agg_y)
    home_z = lax.broadcasted_iota(jnp.int32, tile_shape, 2) // (tile_shape[2] // agg_z)
    own_x = fine_ids // (agg_y * agg_z)
    own_y = fine_ids // agg_z % agg_y
    own_z = fine_ids % agg_z
    return (own_x - home_x + 1) * 9 + (own_y - home_y + 1) * 3 + (own_z - home_z + 1)


def all_offsets():
    listing = []
    for step_x in (-1, 0, 1):
        for step_y in (-1, 0, 1):
            for step_z in (-1, 0, 1):
                listing.append(
                    ((step_x + 1) * 9 + (step_y + 1) * 3 + (step_z + 1), step_x, step_y, step_z)
                )
    return listing


def shift_grid(grid, step_x, step_y, step_z):
    padded = jnp.pad(grid, ((0, 0), (1, 1), (1, 1), (1, 1)))
    return padded[
        :,
        1 + step_x : 1 + step_x + grid.shape[1],
        1 + step_y : 1 + step_y + grid.shape[2],
        1 + step_z : 1 + step_z + grid.shape[3],
    ]


def pool_cells(field, agg_shape):
    agg_x, agg_y, agg_z = agg_shape
    rows = field.shape[0]
    ratio_x = field.shape[1] // agg_x
    ratio_y = field.shape[2] // agg_y
    ratio_z = field.shape[3] // agg_z
    blocks = field.reshape(rows, agg_x, ratio_x, agg_y, ratio_y, agg_z, ratio_z)
    return jnp.sum(blocks, axis=(2, 4, 6))


def spread_cells(grid, field_shape):
    rows, agg_x, agg_y, agg_z = grid.shape
    ratio_x = field_shape[1] // agg_x
    ratio_y = field_shape[2] // agg_y
    ratio_z = field_shape[3] // agg_z
    wide = jnp.broadcast_to(
        grid[:, :, None, :, None, :, None], (rows, agg_x, ratio_x, agg_y, ratio_y, agg_z, ratio_z)
    )
    return wide.reshape(field_shape)


def restrict_cells(field, codes, agg_shape):
    total_grid = jnp.zeros((field.shape[0],) + agg_shape, jnp.float32)
    for code_num, step_x, step_y, step_z in all_offsets():
        pooled = pool_cells(jnp.where(codes[None] == code_num, field, 0.0), agg_shape)
        total_grid = total_grid + shift_grid(pooled, -step_x, -step_y, -step_z)
    return total_grid


def lift_cells(grid, codes, field_shape):
    lifted = jnp.zeros(field_shape, jnp.float32)
    for code_num, step_x, step_y, step_z in all_offsets():
        spread = spread_cells(shift_grid(grid, step_x, step_y, step_z), field_shape)
        lifted = lifted + jnp.where(codes[None] == code_num, spread, 0.0)
    return lifted


def block_width(aggregates):
    return math.gcd(aggregates, 512)


def sum_to_unknowns(values, level_ids, total_count):
    rows, aggregates = values.shape
    width = block_width(aggregates)
    count = aggregates // width
    value_blocks = values.reshape(rows, count, width).transpose(1, 0, 2)
    id_blocks = level_ids.reshape(count, width)
    columns = lax.broadcasted_iota(jnp.int32, (1, total_count), 1)

    def sum_one_block(carry, pieces):
        block_values, block_ids = pieces
        onehot = (block_ids[:, None] == columns).astype(jnp.float32)
        return (carry + jnp.dot(block_values, onehot, precision=lax.Precision.HIGHEST), None)

    start = jnp.zeros((rows, total_count), jnp.float32)
    result, unused = lax.scan(sum_one_block, start, (value_blocks, id_blocks))
    return result


def read_unknowns(values, level_ids):
    rows, total_count = values.shape
    aggregates = level_ids.shape[0]
    width = block_width(aggregates)
    count = aggregates // width
    id_blocks = level_ids.reshape(count, width)
    columns = lax.broadcasted_iota(jnp.int32, (1, total_count), 1)

    def read_one_block(block_ids):
        onehot = (block_ids[:, None] == columns).astype(jnp.float32)
        return lax.dot_general(
            values, onehot, (((1,), (1,)), ((), ())), precision=lax.Precision.HIGHEST
        )

    picked = lax.map(read_one_block, id_blocks)
    return picked.transpose(1, 0, 2).reshape(rows, aggregates)


def coarse_apply(vector, coarse_diag, coarse_links):
    padded = extended(vector, (("gx", 1), ("gy", 2)), 1)
    along = jnp.pad(vector, ((0, 0), (0, 0), (0, 0), (1, 1)))
    linked = coarse_links[0] * padded[:, :-2, 1:-1, :] + coarse_links[1] * padded[:, 2:, 1:-1, :]
    linked = (
        linked
        + coarse_links[2] * padded[:, 1:-1, :-2, :]
        + coarse_links[3] * padded[:, 1:-1, 2:, :]
    )
    linked = linked + coarse_links[4] * along[:, :, :, :-2] + coarse_links[5] * along[:, :, :, 2:]
    return coarse_diag * vector - linked


def local(right_side, fine_ids, coarse_diag, coarse_links, coarse_ids, coarsest_inverse):
    rhs_count = right_side.shape[0]
    agg_shape = coarse_diag.shape
    grid_shape = (rhs_count,) + agg_shape
    codes = block_codes(fine_ids, agg_shape)
    level_ids = coarse_ids.reshape(-1)
    coarse_inv_diag = 1.0 / coarse_diag

    def coarse_op(vector):
        return coarse_apply(vector, coarse_diag, coarse_links)

    pre_fine = fine_smooth(right_side, None)
    fine_residual = right_side - fine_apply(pre_fine)
    applied = fine_apply(fine_residual)
    smoothed = fine_residual - prolong_weight * applied
    coarse_target = restrict_cells(smoothed, codes, agg_shape)
    pre_coarse = chebyshev(coarse_op, coarse_inv_diag, coarse_target, None, coarse_low, coarse_high)
    coarse_residual = coarse_target - coarse_op(pre_coarse)
    total_count = coarsest_inverse.shape[1]
    partial_value = sum_to_unknowns(coarse_residual.reshape(rhs_count, -1), level_ids, total_count)
    summed = lax.psum(partial_value, ("gx", "gy"))
    own_part = jnp.dot(summed, coarsest_inverse.T, precision=lax.Precision.HIGHEST)
    coarsest = lax.all_gather(own_part, ("gx", "gy"), axis=1, tiled=True)
    start = pre_coarse + read_unknowns(coarsest, level_ids).reshape(grid_shape)
    post_coarse = chebyshev(
        coarse_op, coarse_inv_diag, coarse_target, start, coarse_low, coarse_high
    )
    lifted = lift_cells(post_coarse, codes, right_side.shape)
    corrected = pre_fine + (lifted - prolong_weight * fine_apply(lifted))
    return fine_smooth(right_side, corrected)


def solution(mesh):
    return jax.shard_map(
        local,
        mesh=mesh,
        in_specs=(
            P(None, "gx", "gy", None),
            P("gx", "gy", None),
            P("gx", "gy", None),
            P(None, "gx", "gy", None),
            P("gx", "gy", None),
            P(("gx", "gy"), None),
        ),
        out_specs=P(None, "gx", "gy", None),
        check_vma=False,
    )
```

profile of v0, /device:TPU:9, one launch (start us, length us, event | category | flops | bytes accessed | tf_op | source)
XLA Modules:
  0.0 959.5 jit_solution(16324235649655375959)
XLA Ops:
  6.5 3.6 copy.721
  18.7 4.3 collective-permute-start
  30.9 5.2 collective-permute-start.3
  46.2 4.3 copy.731
  53.4 11.5 %multiply_add_fusion.1 = (f32[8,4,8,256]{0,3,2,1:T(8,128)S(1)}, f32[8,4,8,256]{0,3,2,1:T(8,128)}) fusion(f32[8,4,8,256]{0,3,2,1:T(8,128)} %copy.739, f32[8,4,8,256]{0,3,2,1:T(8,128)} %copy.721, f32[8,4,8,256]{0,3,2,1:T(8,128)} %copy.737, f32[8,4,8,256]{0,3,2,1:T(8,128)} %copy.736, f32[8,4,8,256]{0,3,2,1:T(8,128)} %copy-done.5), kind=kLoop, calls=%fused_computation.17 | loop fusion | flops 393216 | bytes 1835008 | tf_op jit(solution)/shard_map/add | solution.py:56
  70.6 5.2 collective-permute-start.4
  83.7 4.5 collective-permute-start.7
  93.0 4.3 copy.747
  100.2 9.6 %add_add_fusion.1 = f32[8,4,8,256]{0,3,2,1:T(8,128)S(1)} fusion(f32[8,4,8,256]{0,3,2,1:T(8,128)} %get-tuple-element.52, f32[8,4,8,256]{0,3,2,1:T(8,128)} %copy.752, f32[8,4,8,256]{0,3,2,1:T(8,128)} %copy-done.6, f32[8,4,8,256]{0,3,2,1:T(8,128)} %copy.721), kind=kLoop, calls=%fused_computation.16 | loop fusion | flops 720896 | bytes 1310720 | tf_op jit(solution)/shard_map/add | solution.py:57
  112.6 3.5 collective-permute-start.9
  116.1 5.0 collective-permute-start.8
  128.6 4.5 collective-permute-start.11
  138.0 4.3 copy.760
  145.3 9.0 subtract_subtract_fusion.2
  160.8 3.5 collective-permute-start.13
  164.3 4.5 collective-permute-start.12
  176.7 4.5 collective-permute-start.15
  186.0 4.3 copy.774
  193.2 10.4 %broadcast_select_fusion.26 = (f32[8,4,8,256]{0,3,2,1:T(8,128)}, f32[8,4,8,256]{0,3,2,1:T(8,128)}) fusion(pred[4,8,256]{2,1,0:T(8,128)(4,1)S(1)} %get-tuple-element.49, f32[8,4,8,256]{0,3,2,1:T(8,128)} %copy-done.9, f32[8,4,8,256]{0,3,2,1:T(8,128)} %copy.779), kind=kLoop, calls=%fused_computation.48 | loop fusion | flops 458752 | bytes 1056768 | tf_op jit(solution)/shard_map/jit(_where)/select_n | solution.py:128
  207.1 14.2 %broadcast_select_fusion.24 = (f32[8,4,8,256]{0,3,2,1:T(8,128)}, f32[8,4,8,256]{0,3,2,1:T(8,128)}, f32[8,4,8,256]{0,3,2,1:T(8,128)}, f32[8,4,8,256]{0,3,2,1:T(8,...) fusion(f32[8,4,8,256]{0,3,2,1:T(8,128)} %get-tuple-element.48, ...), kind=kLoop, calls=%fused_computation.46 | loop fusion | flops 524288 | bytes 2424832 | tf_op jit(solution)/shard_map/jit(_where)/select_n | solution.py:128
  224.7 3.3 reduce_sum.251
  228.1 3.3 reduce_sum.250
  231.5 3.3 reduce_sum.249
  235.0 3.3 reduce_sum.248
  238.4 3.3 reduce_sum.247
  241.8 3.3 reduce_sum.246
  248.8 30.0 %broadcast_select_fusion.25 = (f32[8,4,8,256]{0,3,2,1:T(8,128)}, f32[8,4,8,256]{0,3,2,1:T(8,128)}, f32[8,4,8,256]{0,3,2,1:T(8,128)}, f32[8,4,8,256]{0,3,2,1:T(8,...) fusion(f32[8,4,8,256]{0,3,2,1:T(8,128)} %get-tuple-element.48, ...), kind=kLoop, calls=%fused_computation.47 | loop fusion | flops 1179648 | bytes 5128192 | tf_op jit(solution)/shard_map/jit(_where)/select_n | solution.py:128
  309.6 3.5 reduce_sum.260
  333.7 3.4 reduce_sum.253
  340.7 3.5 collective-permute-start.16
  344.2 4.5 collective-permute-start.17
  349.5 4.5 collective-permute-start.18
  359.2 3.4 collective-permute-start.20
  362.6 4.5 collective-permute-start.21
  375.9 3.4 collective-permute-start.24
  379.3 4.5 collective-permute-start.25
  394.1 139.9 %all-reduce.43.cloned.1.call-done = f32[8,2048]{1,0:T(8,128)} async-done(((f32[8,2048]{1,0:T(8,128)}), f32[8,2048]{1,0:T(8,128)}) %all-reduce.43.cloned.1.call-update) | async-done | bytes 65552 | tf_op jit(solution)/shard_map/psum | solution.py:214
  535.0 32.5 %all-gather = f32[128,16,8]{1,2,0:T(8,128)S(1)} all-gather(f32[1,16,8]{1,2,0:T(8,128)S(1)} %convolution_bitcast_fusion), channel_id=1, replica_groups=mesh['gx'=16,'gy'=8] {'gx','gy'}, dimensions={0}, use_global_device_ids=true | all-gather | bytes 66048 | tf_op jit(solution)/shard_map/all_gather | solution.py:216
  571.2 5.3 collective-permute-start.29
  577.3 3.8 collective-permute-start.30
  588.1 6.0 collective-permute-start.33
  605.3 5.6 collective-permute-start.37
  701.9 60.1 %select_add_fusion = f32[8,4,8,256]{0,3,2,1:T(8,128)S(1)} fusion(f32[8,4,8,256]{0,3,2,1:T(8,128)} %bitcast.100, f32[8,4,8,256]{0,3,2,1:T(8,128)} %bitcast.101, f32[8,4,8,256]{0,3,2,1:T(8,128)} %bitcast.103, f32[8,4,8,256]{0,3,2,1:T(8,128)} %bitcast.104, f32[8,4,8,256]{0,3,2,1:T(8,128)} %bitcast.105, f32[8,4,8,256]{0,3,2,1:T(8,128)} %bitcast.107, ...), kind=kLoop, calls=%fused_computation.13 | loop fusion | flops 3473408 | bytes 7561216 | tf_op jit(solution)/shard_map/add | solution.py:137
  764.6 6.0 collective-permute-start.40
  773.2 4.8 collective-permute-done.41
  784.2 3.4 collective-permute-start.43
  792.4 4.3 copy.844
  799.6 8.2 subtract_add_fusion
  812.4 3.4 collective-permute-start.45
  816.2 3.4 collective-permute-done.45
  825.8 4.8 collective-permute-start.47
  835.6 4.3 copy.857
  842.9 10.7 %broadcast_multiply_fusion = (f32[8,4,8,256]{0,3,2,1:T(8,128)S(1)}, f32[8,4,8,256]{0,3,2,1:T(8,128)}) fusion(f32[8,4,8,256]{0,3,2,1:T(8,128)} %copy.721, f32[8,4,8,256]{0,3,2,1:T(8,128)} %copy.862, f32[8,4,8,256]{0,3,2,1:T(8,128)} %copy-done.3), kind=kLoop, calls=%fused_computation.49 | loop fusion | flops 393216 | bytes 1310720 | tf_op jit(solution)/shard_map/div | solution.py:51
  858.3 3.4 collective-permute-start.49
  862.1 3.4 collective-permute-done.49
  871.7 4.8 collective-permute-start.51
  881.2 4.3 copy.871
  888.4 7.3 multiply_add_fusion
  900.5 3.4 collective-permute-start.53
  904.2 3.4 collective-permute-done.53
  913.9 4.8 collective-permute-start.55
  923.7 4.3 copy.884
  931.0 17.9 %add_add_fusion = f32[8,4,8,256]{0,3,2,1:T(8,128)} fusion(f32[8,4,8,256]{0,3,2,1:T(8,128)} %copy.889, f32[8,4,8,256]{0,3,2,1:T(8,128)} %copy-done.8, f32[8,4,8,256]{0,3,2,1:T(8,128)} %copy-done.3, f32[8,4,8,256]{0,3,2,1:T(8,128)} %copy-done.4, f32[8,4,8,256]{0,3,2,1:T(8,128)} %get-tuple-element.24, f32[8,4,8,256]{0,3,2,1:T(8,128)} %copy.876), kind=kLoop, calls=%fused_computation.8 | loop fusion | flops 1048576 | bytes 1835008 | tf_op jit(solution)/shard_map/add | solution.py:57
  948.9 3.5 copy.890
  (471 shorter events, 371.0 us)
Async XLA Ops:
  6.5 527.5 %copy-start = (f32[16,2048]{1,0:T(8,128)S(1)}, f32[16,2048]{1,0:T(8,128)}, u32[]{:S(2)}) copy-start(f32[16,2048]{1,0:T(8,128)} %param.11) | copy-start | bytes 393220
  6.5 527.5 %all-reduce.43.cloned.1.call-start = ((), (), s32[]{:S(2)}) async-start(), calls=%async_computation | async-start | bytes 131072 | tf_op jit(solution)/shard_map/psum | solution.py:214
  15.2 9.4 collective-permute-start.1
  18.7 5.6 collective-permute-start
  30.9 19.6 %collective-permute-start.3 = (f32[8,6,1,256]{3,0,2,1:T(8,128)S(1)}, f32[8,6,1,256]{3,0,2,1:T(8,128)S(1)}, u32[]{:S(2)}, u32[]{:S(2)}) collective-permute-start(f32[8,6,1,256]{3,0,2,1:T(8,128)S(1)} %copy.733), channel_id=1, source_target_pairs={{0,1},{1,2},{2,3},{3,4},{4,5},{5,6},{6,7},{8,9},{9,10},{10,11},{11... | collective-permute-start | bytes 147464 | tf_op jit(solution)/shard_map/ppermute | solution.py:23
  36.1 14.4 %collective-permute-start.2 = (f32[8,6,1,256]{3,0,2,1:T(8,128)S(1)}, f32[8,6,1,256]{3,0,2,1:T(8,128)S(1)}, u32[]{:S(2)}, u32[]{:S(2)}) collective-permute-start(f32[8,6,1,256]{3,0,2,1:T(8,128)S(1)} %copy.730), channel_id=1, source_target_pairs={{1,0},{2,1},{3,2},{4,3},{5,4},{6,5},{7,6},{9,8},{10,9},{11,10},{12... | collective-permute-start | bytes 147464 | tf_op jit(solution)/shard_map/ppermute | solution.py:26
  67.8 9.7 %collective-permute-start.5 = (f32[8,1,8,256]{3,2,1,0:T(8,128)S(1)}, f32[8,1,8,256]{3,2,1,0:T(8,128)S(1)}, u32[]{:S(2)}, u32[]{:S(2)}) collective-permute-start(f32[8,1,8,256]{3,2,1,0:T(8,128)S(1)} %copy.742), channel_id=1, source_target_pairs={{0,8},{8,16},{16,24},{24,32},{32,40},{40,48},{48,56},{56,64},{64,7... | collective-permute-start | bytes 196616 | tf_op jit(solution)/shard_map/ppermute | solution.py:23
  70.6 6.5 collective-permute-start.4
  83.7 13.6 %collective-permute-start.7 = (f32[8,6,1,256]{3,0,2,1:T(8,128)S(1)}, f32[8,6,1,256]{3,0,2,1:T(8,128)S(1)}, u32[]{:S(2)}, u32[]{:S(2)}) collective-permute-start(f32[8,6,1,256]{3,0,2,1:T(8,128)S(1)} %copy.749), channel_id=1, source_target_pairs={{0,1},{1,2},{2,3},{3,4},{4,5},{5,6},{6,7},{8,9},{9,10},{10,11},{11... | collective-permute-start | bytes 147464 | tf_op jit(solution)/shard_map/ppermute | solution.py:23
  88.2 9.1 collective-permute-start.6
  112.6 9.7 %collective-permute-start.9 = (f32[8,1,8,256]{3,2,1,0:T(8,128)S(1)}, f32[8,1,8,256]{3,2,1,0:T(8,128)S(1)}, u32[]{:S(2)}, u32[]{:S(2)}) collective-permute-start(f32[8,1,8,256]{3,2,1,0:T(8,128)S(1)} %copy.755), channel_id=1, source_target_pairs={{0,8},{8,16},{16,24},{24,32},{32,40},{40,48},{48,56},{56,64},{64,7... | collective-permute-start | bytes 196616 | tf_op jit(solution)/shard_map/ppermute | solution.py:23
  116.1 5.8 collective-permute-start.8
  128.6 13.7 %collective-permute-start.11 = (f32[8,6,1,256]{3,0,2,1:T(8,128)S(1)}, f32[8,6,1,256]{3,0,2,1:T(8,128)S(1)}, u32[]{:S(2)}, u32[]{:S(2)}) collective-permute-start(f32[8,6,1,256]{3,0,2,1:T(8,128)S(1)} %copy.762), channel_id=1, source_target_pairs={{0,1},{1,2},{2,3},{3,4},{4,5},{5,6},{6,7},{8,9},{9,10},{10,11},{11... | collective-permute-start | bytes 147464 | tf_op jit(solution)/shard_map/ppermute | solution.py:23
  133.1 9.2 collective-permute-start.10
  160.8 9.7 %collective-permute-start.13 = (f32[8,1,8,256]{3,2,1,0:T(8,128)S(1)}, f32[8,1,8,256]{3,2,1,0:T(8,128)S(1)}, u32[]{:S(2)}, u32[]{:S(2)}) collective-permute-start(f32[8,1,8,256]{3,2,1,0:T(8,128)S(1)} %copy.769), channel_id=1, source_target_pairs={{0,8},{8,16},{16,24},{24,32},{32,40},{40,48},{48,56},{56,64},{64,7... | collective-permute-start | bytes 196616 | tf_op jit(solution)/shard_map/ppermute | solution.py:23
  164.3 5.8 collective-permute-start.12
  169.0 79.6 %copy-start.45 = (pred[4,8,256]{2,1,0:T(8,128)(4,1)}, pred[4,8,256]{2,1,0:T(8,128)(4,1)S(1)}, u32[]{:S(2)}) copy-start(pred[4,8,256]{2,1,0:T(8,128)(4,1)S(1)} %get-tuple-element.141) | copy-start | bytes 24580
  169.0 79.6 %copy-start.46 = (pred[4,8,256]{2,1,0:T(8,128)(4,1)}, pred[4,8,256]{2,1,0:T(8,128)(4,1)S(1)}, u32[]{:S(2)}) copy-start(pred[4,8,256]{2,1,0:T(8,128)(4,1)S(1)} %get-tuple-element.142) | copy-start | bytes 24580
  169.0 79.6 %copy-start.48 = (pred[4,8,256]{2,1,0:T(8,128)(4,1)}, pred[4,8,256]{2,1,0:T(8,128)(4,1)S(1)}, u32[]{:S(2)}) copy-start(pred[4,8,256]{2,1,0:T(8,128)(4,1)S(1)} %get-tuple-element.144) | copy-start | bytes 24580
  169.0 79.6 %copy-start.49 = (pred[4,8,256]{2,1,0:T(8,128)(4,1)}, pred[4,8,256]{2,1,0:T(8,128)(4,1)S(1)}, u32[]{:S(2)}) copy-start(pred[4,8,256]{2,1,0:T(8,128)(4,1)S(1)} %get-tuple-element.145) | copy-start | bytes 24580
  169.0 79.6 %copy-start.50 = (pred[4,8,256]{2,1,0:T(8,128)(4,1)}, pred[4,8,256]{2,1,0:T(8,128)(4,1)S(1)}, u32[]{:S(2)}) copy-start(pred[4,8,256]{2,1,0:T(8,128)(4,1)S(1)} %get-tuple-element.146) | copy-start | bytes 24580
  169.1 79.6 %copy-start.51 = (pred[4,8,256]{2,1,0:T(8,128)(4,1)}, pred[4,8,256]{2,1,0:T(8,128)(4,1)S(1)}, u32[]{:S(2)}) copy-start(pred[4,8,256]{2,1,0:T(8,128)(4,1)S(1)} %get-tuple-element.147) | copy-start | bytes 24580
  176.7 13.6 %collective-permute-start.15 = (f32[8,6,1,256]{3,0,2,1:T(8,128)S(1)}, f32[8,6,1,256]{3,0,2,1:T(8,128)S(1)}, u32[]{:S(2)}, u32[]{:S(2)}) collective-permute-start(f32[8,6,1,256]{3,0,2,1:T(8,128)S(1)} %copy.776), channel_id=1, source_target_pairs={{0,1},{1,2},{2,3},{3,4},{4,5},{5,6},{6,7},{8,9},{9,10},{10,11},{11... | collective-permute-start | bytes 147464 | tf_op jit(solution)/shard_map/ppermute | solution.py:23
  181.2 9.1 collective-permute-start.14
  340.7 8.1 collective-permute-start.16
  344.2 5.3 collective-permute-start.17
  349.5 6.4 collective-permute-start.18
  354.0 5.1 collective-permute-start.19
  359.2 8.0 collective-permute-start.20
  362.6 5.3 collective-permute-start.21
  367.9 4.7 collective-permute-start.22
  370.7 5.1 collective-permute-start.23
  375.9 8.0 collective-permute-start.24
  379.3 5.3 collective-permute-start.25
  384.6 4.8 collective-permute-start.26
  387.4 5.1 collective-permute-start.27
  569.1 7.4 collective-permute-start.28
  571.2 6.1 collective-permute-start.29
  577.3 5.7 collective-permute-start.30
  581.0 5.1 collective-permute-start.31
  586.2 8.0 collective-permute-start.32
  588.1 6.8 collective-permute-start.33
  594.9 4.7 collective-permute-start.34
  597.7 5.1 collective-permute-start.35
  602.9 8.0 collective-permute-start.36
  605.3 6.3 collective-permute-start.37
  611.6 5.1 collective-permute-start.38
  614.4 5.1 collective-permute-start.39
  764.6 8.3 collective-permute-start.40
  770.9 7.1 collective-permute-start.41
  784.2 12.5 %collective-permute-start.43 = (f32[8,6,1,256]{3,0,2,1:T(8,128)S(1)}, f32[8,6,1,256]{3,0,2,1:T(8,128)S(1)}, u32[]{:S(2)}, u32[]{:S(2)}) collective-permute-start(f32[8,6,1,256]{3,0,2,1:T(8,128)S(1)} %copy.846), channel_id=1, source_target_pairs={{0,1},{1,2},{2,3},{3,4},{4,5},{5,6},{6,7},{8,9},{9,10},{10,11},{11... | collective-permute-start | bytes 147464 | tf_op jit(solution)/shard_map/ppermute | solution.py:23
  787.6 9.1 collective-permute-start.42
  810.2 5.6 collective-permute-start.44
  812.4 7.1 collective-permute-start.45
  825.8 14.1 %collective-permute-start.47 = (f32[8,6,1,256]{3,0,2,1:T(8,128)S(1)}, f32[8,6,1,256]{3,0,2,1:T(8,128)S(1)}, u32[]{:S(2)}, u32[]{:S(2)}) collective-permute-start(f32[8,6,1,256]{3,0,2,1:T(8,128)S(1)} %copy.859), channel_id=1, source_target_pairs={{0,1},{1,2},{2,3},{3,4},{4,5},{5,6},{6,7},{8,9},{9,10},{10,11},{11... | collective-permute-start | bytes 147464 | tf_op jit(solution)/shard_map/ppermute | solution.py:23
  830.6 9.3 collective-permute-start.46
  856.1 5.6 collective-permute-start.48
  858.3 7.1 collective-permute-start.49
  871.7 13.9 %collective-permute-start.51 = (f32[8,6,1,256]{3,0,2,1:T(8,128)S(1)}, f32[8,6,1,256]{3,0,2,1:T(8,128)S(1)}, u32[]{:S(2)}, u32[]{:S(2)}) collective-permute-start(f32[8,6,1,256]{3,0,2,1:T(8,128)S(1)} %copy.873), channel_id=1, source_target_pairs={{0,1},{1,2},{2,3},{3,4},{4,5},{5,6},{6,7},{8,9},{9,10},{10,11},{11... | collective-permute-start | bytes 147464 | tf_op jit(solution)/shard_map/ppermute | solution.py:23
  876.5 9.1 collective-permute-start.50
  898.2 5.6 collective-permute-start.52
  900.5 7.1 collective-permute-start.53
  913.9 14.2 %collective-permute-start.55 = (f32[8,6,1,256]{3,0,2,1:T(8,128)S(1)}, f32[8,6,1,256]{3,0,2,1:T(8,128)S(1)}, u32[]{:S(2)}, u32[]{:S(2)}) collective-permute-start(f32[8,6,1,256]{3,0,2,1:T(8,128)S(1)} %copy.886), channel_id=1, source_target_pairs={{0,1},{1,2},{2,3},{3,4},{4,5},{5,6},{6,7},{8,9},{9,10},{10,11},{11... | collective-permute-start | bytes 147464 | tf_op jit(solution)/shard_map/ppermute | solution.py:23
  918.7 9.4 collective-permute-start.54
  (60 other events, 1445.2 us)
Sparse Core Ops, SparseCore 0:
  394.3 139.6 all-reduce.42
where the time goes:
time: 971 us; the launch traced here: 959 us
  other arithmetic  306 us (32%)
  local copies, waits for them, and re-layouts  233 us (24%)
  starting transfers between devices  187 us (19%)
  waiting for transfers between devices  182 us (19%)
  blocking collectives  32.5 us (3%)
  between operations  15.9 us (2%)
    psum x1, waiting for transfers between devices, local(): summed = lax.psum(partial_value, ('gx', 'gy'))  140 us
    ppermute x28, starting transfers between devices, extended(): lax.ppermute(lax.slice_in_dim(block, block.shape[dim] - width, None, axis...  97.7 us
    reduce_sum x27, other arithmetic, pool_cells(): return jnp.sum(blocks, axis=(2, 4, 6))  90.4 us
    ppermute x28, starting transfers between devices, extended(): lax.ppermute(lax.slice_in_dim(block, 0, width, axis=dim), axis, backward)  89 us
    broadcast_in_dim x27, local copies, waits for them, and re-layouts, spread_cells(): jnp.broadcast_to(grid[:, :, None, :, None, :, None], (rows, agg_x, ratio_...  66.2 us
    add x1, other arithmetic, lift_cells(): lifted = lifted + jnp.where(codes[None] == code_num, spread, 0.0)  60.1 us
    select_n x3, other arithmetic, restrict_cells(): jnp.where(codes[None] == code_num, field, 0.0)  54.6 us
    unnamed x136, local copies, waits for them, and re-layouts  41.1 us
  transfers between devices with their start and end apart: 57, of which 21 were waited for; matrix products, arithmetic and copies ran while one was open for 7% of the time, Pallas kernels for 0%

commit v1 on v0

v1 whole, which is shorter than its diff:
```python
import math

import jax
import jax.numpy as jnp
import numpy as np
from jax import lax
from jax.experimental import pallas as pl
from jax.experimental.pallas import tpu as pltpu
from jax.sharding import PartitionSpec as P

F32 = jnp.float32
BF16 = jnp.bfloat16

PROLONG = 1.0 / 9.0


def nodes(low, high):
    theta = (high + low) / 2.0
    delta = (high - low) / 2.0
    reach = delta * math.cos(math.pi / 6.0)
    return (theta + reach, theta - reach, theta)


FINE_NODES = tuple(6.0 * node for node in nodes(2.0 / 30.0, 2.0))
COARSE_NODES = nodes(0.19, 1.9)

RHS, CX, YT, CY, CZ = 8, 4, 8, 8, 256
GX, GY = 16, 8
LANES = 128
NC2 = 2048
HI = NC2 // LANES


def beside_in_row(row):
    sub = lax.broadcasted_iota(jnp.int32, row.shape, 1)
    lane = lax.broadcasted_iota(jnp.int32, row.shape, 2)
    zero_tile = jnp.zeros((1,) + row.shape[1:], F32)
    up = pltpu.roll(row, 1, 1)
    up = jnp.where(sub == 0, jnp.concatenate([zero_tile, up[:-1]], axis=0), up)
    down = pltpu.roll(row, CY - 1, 1)
    down = jnp.where(sub == CY - 1, jnp.concatenate([down[1:], zero_tile], axis=0), down)
    left = jnp.where(lane == 0, 0.0, pltpu.roll(row, 1, 2))
    right = jnp.where(lane == CZ - 1, 0.0, pltpu.roll(row, CZ - 1, 2))
    return (up + down) + (left + right)


def relax(low, row, high, node):
    return (1.0 - 6.0 / node) * row + (1.0 / node) * (low + high + beside_in_row(row))


def row_gate(x, keep_low, keep_high):
    return jnp.where(x < 0, keep_low, jnp.where(x >= CX, keep_high, 1.0))


def beside_grid(grid):
    sub = lax.broadcasted_iota(jnp.int32, grid.shape, 1)
    lane = lax.broadcasted_iota(jnp.int32, grid.shape, 2)
    turned = pltpu.roll(grid, LANES // 2, 2)
    low_y = jnp.where(lane < LANES // 2, pltpu.roll(turned, 1, 1), turned)
    high_y = jnp.where(lane < LANES // 2, turned, pltpu.roll(turned, YT - 1, 1))
    low_z = pltpu.roll(grid, 1, 2)
    high_z = pltpu.roll(grid, LANES - 1, 2)
    del sub
    return low_y, high_y, low_z, high_z


def lower_of(grid):
    return jnp.concatenate([jnp.zeros((1,) + grid.shape[1:], F32), grid[:-1]], axis=0)


def upper_of(grid):
    return jnp.concatenate([grid[1:], jnp.zeros((1,) + grid.shape[1:], F32)], axis=0)


def load_window(coefs_ref, place, rows, before):
    diag, ux, uy, uz, ids = [], [], [], [], []
    for w in range(rows):
        dev = place + (w - before) // 2
        half = (w - before) % 2
        inside = jnp.logical_and(dev >= 0, dev < GX)
        at = jnp.clip(dev, 0, GX - 1)
        diag.append(jnp.where(inside, coefs_ref[at, 0, half], 1.0))
        ux.append(jnp.where(inside, coefs_ref[at, 1, half], 0.0))
        uy.append(jnp.where(inside, coefs_ref[at, 2, half], 0.0))
        uz.append(jnp.where(inside, coefs_ref[at, 3, half], 0.0))
        ids.append(coefs_ref[at, 4, half].astype(jnp.int32))
    diag, ux, uy, uz, ids = (jnp.stack(v, axis=0) for v in (diag, ux, uy, uz, ids))
    low_x = lower_of(ux)
    low_y = beside_grid(uy)[0]
    low_z = beside_grid(uz)[2]
    return (diag, low_x, ux, low_y, uy, low_z, uz), ids


def coarse_apply(grid, coefs):
    diag, lx, ux, ly, uy, lz, uz = coefs
    low_y, high_y, low_z, high_z = beside_grid(grid)
    linked = lx * lower_of(grid) + ux * upper_of(grid)
    linked = linked + ly * low_y + uy * high_y
    linked = linked + lz * low_z + uz * high_z
    return diag * grid - linked


def coarse_smooth(residual, coefs, inverse, with_last):
    total = None
    for k, node in enumerate(COARSE_NODES):
        update = (1.0 / node) * inverse * residual
        total = update if total is None else total + update
        if k < 2 or with_last:
            residual = residual - coarse_apply(update, coefs)
    return total, residual


def split3(value):
    first = value.astype(BF16)
    rest = value - first.astype(F32)
    second = rest.astype(BF16)
    third = (rest - second.astype(F32)).astype(BF16)
    return first, second, third


def down_kernel(place_ref, tl_ref, to_ref, tr_ref, ids_ref, coefs_ref, pool_ref, send_ref, u_ref, a_ref, b_ref):
    place = place_ref[0]
    keep_low = jnp.where(place > 0, 1.0, 0.0).astype(F32)
    keep_high = jnp.where(place < GX - 1, 1.0, 0.0).astype(F32)
    first, second, third = FINE_NODES
    for x in range(CX):
        a_ref[x] = tl_ref[:, x]
        a_ref[CX + x] = to_ref[:, x]
        a_ref[2 * CX + x] = tr_ref[:, x]

    def step(src, dst, reach, node):
        def body(k, carry):
            row = relax(src[k - 1], src[k], src[k + 1], node)
            dst[k] = row * row_gate(k - CX, keep_low, keep_high)
            return carry

        lax.fori_loop(CX - reach, 2 * CX + reach, body, 0)

    step(a_ref, b_ref, 3, first)

    def start_u(k, carry):
        u_ref[k] = (1.0 / first) * a_ref[k + 2] + (1.0 / second) * b_ref[k + 2]
        return carry

    lax.fori_loop(0, 8, start_u, 0)
    step(b_ref, a_ref, 2, second)

    def end_u(k, carry):
        u_ref[k] = u_ref[k] + (1.0 / third) * a_ref[k + 2]
        return carry

    lax.fori_loop(0, 8, end_u, 0)
    step(a_ref, b_ref, 1, third)
    step(b_ref, a_ref, 0, 1.0 / PROLONG)

    shape = (YT, CY, CZ)
    home = lax.broadcasted_iota(jnp.int32, shape, 2) // 4
    codes = []
    for x in range(CX):
        ids = ids_ref[:, x]
        codes.append((ids >> 6) * 3 + ((ids & 63) - home) + 1)
    pooled = []
    for half in range(2):
        parts = []
        for k in range(6):
            total = jnp.zeros(shape, F32)
            for x in range(CX):
                total = total + jnp.where(codes[x] == half * 6 + k, a_ref[CX + x], 0.0)
            parts.append(jnp.sum(total, axis=1))
        pooled.append(jnp.concatenate(parts, axis=1))
    pooled = jnp.concatenate(pooled, axis=0)
    pieces = jnp.concatenate(split3(pooled), axis=0)
    sums = jnp.dot(pieces, pool_ref[...], preferred_element_type=F32)
    rows = 2 * YT
    target = sums[:rows] + sums[rows : 2 * rows] + sums[2 * rows :]
    own = (target[:YT], target[YT:])

    coefs, ids = load_window(coefs_ref, place, 8, 3)
    blank = jnp.zeros((YT, LANES), F32)
    grid = jnp.stack([blank] * 3 + list(own) + [blank] * 3, axis=0)
    unused, residual = coarse_smooth(grid, coefs, 1.0 / coefs[0], True)
    high_of = ids >> 7
    low_of = ids & (LANES - 1)
    high_iota = lax.broadcasted_iota(jnp.int32, (HI, LANES), 0)
    low_iota = lax.broadcasted_iota(jnp.int32, (LANES, LANES), 0)
    counted = jnp.zeros((3 * HI, LANES), F32)
    for w in range(8):
        left, right = [], []
        for k in range(YT):
            picked = jnp.where(high_of[w, k : k + 1] == high_iota, residual[w, k : k + 1], 0.0)
            left.append(jnp.concatenate(split3(picked), axis=0))
            right.append(jnp.where(low_of[w, k : k + 1] == low_iota, 1.0, 0.0).astype(BF16))
        counted = counted + lax.dot_general(
            jnp.concatenate(left, axis=1),
            jnp.concatenate(right, axis=1),
            (((1,), (1,)), ((), ())),
            preferred_element_type=F32,
        )
    counted = counted[:HI] + counted[HI : 2 * HI] + counted[2 * HI :]
    for k in range(GX):
        send_ref[k, 0] = own[0]
        send_ref[k, 1] = own[1]
        send_ref[k, 2] = counted[:8]
        send_ref[k, 3] = counted[8:]


def solve_kernel(got_ref, inverse_ref, send_ref):
    top = got_ref[0, 2]
    bottom = got_ref[0, 3]
    for k in range(1, GX):
        top = top + got_ref[k, 2]
        bottom = bottom + got_ref[k, 3]
    target = jnp.concatenate([top, bottom], axis=0)
    total = jnp.zeros((LANES, LANES), F32)
    for k in range(HI):
        total = total + inverse_ref[:, k * LANES : (k + 1) * LANES] * target[k : k + 1]
    row = jnp.sum(total.T, axis=0, keepdims=True)
    tile = jnp.broadcast_to(row, (8, LANES))
    for k in range(GX):
        send_ref[k] = tile


def lane_take(table, index):
    return jnp.take_along_axis(table, index, axis=1, mode="promise_in_bounds")


def up_kernel(
    place_ref,
    got_ref,
    table_ref,
    coefs_ref,
    idl_ref,
    ido_ref,
    idr_ref,
    u_ref,
    ul_ref,
    ur_ref,
    out_ref,
    post_ref,
    a_ref,
    b_ref,
):
    place = place_ref[0]
    keep_low = jnp.where(place > 0, 1.0, 0.0).astype(F32)
    keep_high = jnp.where(place < GX - 1, 1.0, 0.0).astype(F32)
    rows, before = 16, 7
    coefs, ids = load_window(coefs_ref, place, rows, before)
    target = []
    for w in range(rows):
        dev = place + (w - before) // 2
        inside = jnp.logical_and(dev >= 0, dev < GX)
        at = jnp.clip(dev, 0, GX - 1)
        target.append(jnp.where(inside, got_ref[at, (w - before) % 2], 0.0))
    target = jnp.stack(target, axis=0)
    inverse = 1.0 / coefs[0]
    pre, left_over = coarse_smooth(target, coefs, inverse, True)
    high_of = ids >> 7
    low_of = ids & (LANES - 1)
    lifted_rows = []
    for w in range(rows):
        value = jnp.zeros((YT, LANES), F32)
        for k in range(HI):
            table = jnp.broadcast_to(table_ref[k, 0:1], (YT, LANES))
            value = jnp.where(high_of[w] == k, lane_take(table, low_of[w]), value)
        lifted_rows.append(value)
    coarsest = jnp.stack(lifted_rows, axis=0)
    left_over = left_over - coarse_apply(coarsest, coefs)
    update, unused = coarse_smooth(left_over, coefs, inverse, False)
    post = pre + coarsest + update
    for k in range(6):
        gate = keep_low if k < 2 else (keep_high if k >= 4 else None)
        row = post[k + 5]
        post_ref[k] = row if gate is None else row * gate

    for slab, id_ref in enumerate((idl_ref, ido_ref, idr_ref)):

        def lift(x, carry, slab=slab, id_ref=id_ref):
            for k in range(YT):
                table0 = jnp.broadcast_to(post_ref[2 * slab, k : k + 1], (CY, LANES))
                table1 = jnp.broadcast_to(post_ref[2 * slab + 1, k : k + 1], (CY, LANES))
                for part in range(2):
                    lanes = slice(part * LANES, (part + 1) * LANES)
                    cell = id_ref[k, x, :, lanes]
                    low = cell & (LANES - 1)
                    value = jnp.where(cell >= LANES, lane_take(table1, low), lane_take(table0, low))
                    a_ref[slab * CX + x, k, :, lanes] = value
            return carry

        lax.fori_loop(0, CX, lift, 0)

    def step(src, dst, reach, node, add):
        def body(k, carry):
            row = relax(src[k - 1], src[k], src[k + 1], node)
            row = row * row_gate(k - CX, keep_low, keep_high)
            if add:
                row = row + u_ref[k - 2]
            dst[k] = row
            return carry

        lax.fori_loop(CX - reach, 2 * CX + reach, body, 0)

    step(a_ref, b_ref, 2, 1.0 / PROLONG, True)
    for at, edge, gate in ((1, ul_ref, keep_low), (2 * CX + 2, ur_ref, keep_high)):
        row = relax(a_ref[at - 1], a_ref[at], a_ref[at + 1], 1.0 / PROLONG)
        b_ref[at] = row * gate + edge[...]
    first, second, third = FINE_NODES
    step(b_ref, a_ref, 2, first, False)
    step(a_ref, b_ref, 1, second, False)
    for x in range(CX):
        k = CX + x
        out_ref[:, x] = relax(b_ref[k - 1], b_ref[k], b_ref[k + 1], third) + u_ref[k - 2]


def pool_matrix():
    cell = np.arange(CZ)
    out = np.zeros((2, 3, CZ, LANES), np.float32)
    for half in range(2):
        for shift in range(3):
            at = cell // 4 + shift - 1
            ok = (at >= 0) & (at < 64)
            out[half, shift, cell[ok], half * 64 + at[ok]] = 1.0
    return out.reshape(6 * CZ, LANES)


def call(kernel, out_shape, scratch, flops, scalars=0):
    def spec(k):
        return pl.BlockSpec(memory_space=pltpu.SMEM if k < scalars else pltpu.VMEM)

    def run(*args):
        return pl.pallas_call(
            kernel,
            out_shape=out_shape,
            in_specs=[spec(k) for k in range(len(args))],
            out_specs=jax.tree.map(lambda _: pl.BlockSpec(memory_space=pltpu.VMEM), out_shape),
            scratch_shapes=scratch,
            compiler_params=pltpu.CompilerParams(vmem_limit_bytes=40 * 1024 * 1024),
            cost_estimate=pl.CostEstimate(flops=flops, bytes_accessed=2**20, transcendentals=0),
        )(*args)

    return run


def shape_of(*dims):
    return jax.ShapeDtypeStruct(dims, F32)


def to_all(value, axis, count):
    return lax.all_to_all(jnp.broadcast_to(value[None], (count,) + value.shape), axis, 0, 0, tiled=True)


def beside(value_up, value_down):
    forward = [(k, k + 1) for k in range(GX - 1)]
    backward = [(b, a) for a, b in forward]
    return lax.ppermute(value_up, "gx", forward), lax.ppermute(value_down, "gx", backward)


def local(right_side, fine_ids, coarse_diag, coarse_links, coarse_ids, coarsest_inverse):
    place = lax.axis_index("gx").astype(jnp.int32).reshape(1)
    own = lax.all_to_all(right_side, "gy", 0, 0, tiled=True)
    low, high = beside(own, own)

    coefs = jnp.stack(
        [coarse_diag, coarse_links[1], coarse_links[3], coarse_links[5], coarse_ids.astype(F32)], axis=0
    ).reshape(5, 2, LANES)
    coefs = to_all(coefs, "gy", GY).transpose(1, 2, 0, 3)
    coefs = to_all(coefs, "gx", GX)
    ids = to_all(fine_ids, "gy", GY)
    id_low, id_high = beside(ids, ids)
    inverse = to_all(coarsest_inverse, "gy", GY).reshape(LANES, NC2)

    pool = jnp.asarray(pool_matrix(), BF16)
    field = (3 * CX, YT, CY, CZ)
    send, u = call(
        down_kernel,
        [shape_of(GX, 4, YT, LANES), shape_of(8, YT, CY, CZ)],
        [pltpu.VMEM(field, F32), pltpu.VMEM(field, F32)],
        10**7,
        1,
    )(place, low, own, high, ids, coefs, pool)
    got = lax.all_to_all(send, "gx", 0, 0, tiled=True)
    u_low, u_high = beside(u[3], u[4])
    send = call(solve_kernel, shape_of(GX, 8, LANES), [], 10**6)(got, inverse)
    table = lax.all_to_all(send, "gx", 0, 0, tiled=True)
    out = call(
        up_kernel,
        shape_of(YT, CX, CY, CZ),
        [pltpu.VMEM((6, YT, LANES), F32), pltpu.VMEM(field, F32), pltpu.VMEM(field, F32)],
        10**7,
        1,
    )(place, got, table, coefs, id_low, ids, id_high, u, u_low, u_high)
    return lax.all_to_all(out, "gy", 0, 0, tiled=True)


def solution(mesh):
    return jax.shard_map(
        local,
        mesh=mesh,
        in_specs=(
            P(None, "gx", "gy", None),
            P("gx", "gy", None),
            P("gx", "gy", None),
            P(None, "gx", "gy", None),
            P("gx", "gy", None),
            P(("gx", "gy"), None),
        ),
        out_specs=P(None, "gx", "gy", None),
        check_vma=False,
    )
```

time: 971 us -> 130 us (0.13)
  the two profiles are of different devices: /device:TPU:9 before, /device:TPU:1 now
where the time goes in v1:
time: 130 us; the launch traced here: 129 us
  blocking collectives  48.2 us (37%)
  starting transfers between devices  34.9 us (27%)
  waiting for transfers between devices  28.4 us (22%)
  Pallas kernels  11.4 us (9%)
  local copies, waits for them, and re-layouts  5.89 us (5%)
    all_to_all x3, starting transfers between devices, to_all(): lax.all_to_all(jnp.broadcast_to(value[None], (count,) + value.shape), axi...  18.1 us
    all_to_all x1, blocking collectives, local(): got = lax.all_to_all(send, 'gx', 0, 0, tiled=True)  14.3 us
    all_to_all x3, waiting for transfers between devices, to_all(): lax.all_to_all(jnp.broadcast_to(value[None], (count,) + value.shape), axi...  12.8 us
    all_to_all x1, blocking collectives, local(): return lax.all_to_all(out, 'gy', 0, 0, tiled=True)  11.9 us
    pallas_call x3, Pallas kernels, run(): pl.pallas_call(kernel, out_shape=out_shape, in_specs=[spec(k) for k in ra...  11.4 us
    all_to_all x1, blocking collectives, to_all(): lax.all_to_all(jnp.broadcast_to(value[None], (count,) + value.shape), axi...  11.4 us
    all_to_all x1, blocking collectives, local(): own = lax.all_to_all(right_side, 'gy', 0, 0, tiled=True)  10.7 us
    ppermute x3, starting transfers between devices, beside(): lax.ppermute(value_up, 'gx', forward)  9.46 us
  transfers between devices with their start and end apart: 10, of which 5 were waited for; matrix products, arithmetic and copies ran while one was open for 0% of the time, Pallas kernels for 1%

profile of v1, /device:TPU:1, one launch (start us, length us, event | category | flops | bytes accessed | tf_op | source)
XLA Modules:
  0.0 129.0 jit_solution(2394750644810935703)
XLA Ops:
  0.0 0.8 stack.15
  0.8 0.7 fusion
  1.5 0.1 stack.16
  1.6 0.1 stack.17
  1.6 0.0 copy-start.3
  1.6 0.1 stack.18
  1.7 0.6 copy-done.3
  2.3 0.1 stack.19
  2.5 11.4 %all_to_all.40 = f32[8,5,2,128]{3,2,1,0:T(2,128)S(1)} all-to-all(f32[8,5,2,128]{3,2,1,0:T(2,128)S(1)} %broadcast_in_dim.12), channel_id=1, replica_groups=mesh['gx'=16,'gy'=8] {'gy'}, dimensions={0} | all-to-all | bytes 81920 | tf_op jit(solution)/shard_map/all_to_all | solution.py:348
  13.8 0.0 copy-start.2
  13.8 10.7 %all_to_all.41.to_ref = f32[8,4,8,256]{3,2,1,0:T(8,128)S(1)} all-to-all(f32[8,4,8,256]{3,2,1,0:T(8,128)} %param.7), channel_id=1, replica_groups=mesh['gx'=16,'gy'=8] {'gy'}, dimensions={0} | all-to-all | bytes 524288 | tf_op jit(solution)/shard_map/all_to_all | solution.py:359
  24.5 0.0 copy-done.2
  24.5 0.7 broadcast_in_dim.10
  25.2 4.4 %all-to-all-start.1 = ((s32[8,4,8,256]{3,2,1,0:T(8,128)}), s32[8,4,8,256]{3,2,1,0:T(8,128)S(1)}, u32[]{:S(2)}, u32[]{:S(2)}) async-start(s32[8,4,8,256]{3,2,1,0:T(8,128)} %broadcast_in_dim.10), calls=%async_computation.1 | async-start | bytes 524288 | tf_op jit(solution)/shard_map/all_to_all | solution.py:348
  29.6 6.5 %all-to-all-done.1.ids_ref.ido_ref = s32[8,4,8,256]{3,2,1,0:T(8,128)S(1)} async-done(((s32[8,4,8,256]{3,2,1,0:T(8,128)}), s32[8,4,8,256]{3,2,1,0:T(8,128)S(1)}, u32[]{:S(2)}, u32[]{:S(2)}) %all-to-all-start.1) | async-done | bytes 262176 | tf_op jit(solution)/shard_map/all_to_all | solution.py:348
  36.1 0.9 broadcast_in_dim.13
  37.0 0.0 copy-start
  37.0 6.9 %all-to-all-start.3 = ((f32[16,5,2,8,128]{4,3,2,1,0:T(8,128)}), f32[16,5,2,8,128]{4,3,2,1,0:T(8,128)S(1)}, u32[]{:S(2)}, u32[]{:S(2)}) async-start(f32[16,5,2,8,128]{4,3,2,1,0:T(8,128)} %broadcast_in_dim.13), calls=%async_computation.3 | async-start | bytes 1310720 | tf_op jit(solution)/shard_map/all_to_all | solution.py:348
  43.9 3.3 %collective-permute-start = (f32[8,4,8,256]{3,2,1,0:T(8,128)S(1)}, f32[8,4,8,256]{3,2,1,0:T(8,128)S(1)}, u32[]{:S(2)}, u32[]{:S(2)}) collective-permute-start(f32[8,4,8,256]{3,2,1,0:T(8,128)S(1)} %all_to_all.41.to_ref), channel_id=1, source_target_pairs={{0,8},{8,16},{16,24},{24,32},{32,40},{40,48},{48,56},{56,64},{64,7... | collective-permute-start | bytes 786440 | tf_op jit(solution)/shard_map/ppermute | solution.py:354
  47.2 1.3 %collective-permute-start.1 = (f32[8,4,8,256]{3,2,1,0:T(8,128)S(1)}, f32[8,4,8,256]{3,2,1,0:T(8,128)S(1)}, u32[]{:S(2)}, u32[]{:S(2)}) collective-permute-start(f32[8,4,8,256]{3,2,1,0:T(8,128)S(1)} %all_to_all.41.to_ref), channel_id=1, source_target_pairs={{8,0},{16,8},{24,16},{32,24},{40,32},{48,40},{56,48},{64,56},{72,6... | collective-permute-start | bytes 786440 | tf_op jit(solution)/shard_map/ppermute | solution.py:354
  48.5 7.1 %collective-permute-done.tl_ref = f32[8,4,8,256]{3,2,1,0:T(8,128)S(1)} collective-permute-done((f32[8,4,8,256]{3,2,1,0:T(8,128)S(1)}, f32[8,4,8,256]{3,2,1,0:T(8,128)S(1)}, u32[]{:S(2)}, u32[]{:S(2)}) %collective-permute-start) | collective-permute-done | bytes 262176 | tf_op jit(solution)/shard_map/ppermute | solution.py:354
  55.6 2.0 %collective-permute-done.1.tr_ref = f32[8,4,8,256]{3,2,1,0:T(8,128)S(1)} collective-permute-done((f32[8,4,8,256]{3,2,1,0:T(8,128)S(1)}, f32[8,4,8,256]{3,2,1,0:T(8,128)S(1)}, u32[]{:S(2)}, u32[]{:S(2)}) %collective-permute-start.1) | collective-permute-done | bytes 262176 | tf_op jit(solution)/shard_map/ppermute | solution.py:354
  57.6 0.0 all-to-all-done.3.coefs_ref
  57.6 0.0 copy-done
  57.6 5.2 %shard_map.73 = (f32[16,4,8,128]{3,2,1,0:T(8,128)S(1)}, f32[8,8,8,256]{3,2,1,0:T(8,128)S(1)}) custom-call(s32[1]{0:T(128)} %bitcast.place_ref, f32[8,4,8,256]{3,2,1,0:T(8,128)S(1)} %collective-permute-done.tl_ref, f32[8,4,8,256]{3,2,1,0:T(8,128)S(1)} %all_to_all.41.to_ref, f32[8,4,8,256]{3,2,1,0:T(8,128)S(1)} %collective-permute-done.1.tr_ref, ...), custom_call_target="tpu_custom_call" | custom-call | flops 10000000 | bytes 1048576 | tf_op jit(solution)/shard_map/pallas_call | solution.py:330
  62.8 0.0 copy-start.1
  62.8 14.3 %all_to_all.42.got_ref = f32[16,4,8,128]{3,2,1,0:T(8,128)S(1)} all-to-all(f32[16,4,8,128]{3,2,1,0:T(8,128)S(1)} %get-tuple-element.7), channel_id=1, replica_groups=mesh['gx'=16,'gy'=8] {'gx'}, dimensions={0} | all-to-all | bytes 524288 | tf_op jit(solution)/shard_map/all_to_all | solution.py:380
  77.1 0.0 copy-done.1
  77.1 1.1 broadcast_in_dim.14
  78.2 6.8 %all-to-all-start.5 = ((f32[8,16,2048]{2,1,0:T(8,128)}), f32[8,16,2048]{2,1,0:T(8,128)S(1)}, u32[]{:S(2)}, u32[]{:S(2)}) async-start(f32[8,16,2048]{2,1,0:T(8,128)} %broadcast_in_dim.14), calls=%async_computation.5 | async-start | bytes 2097152 | tf_op jit(solution)/shard_map/all_to_all | solution.py:348
  85.0 2.2 %collective-permute-start.2 = (s32[8,4,8,256]{3,2,1,0:T(8,128)S(1)}, s32[8,4,8,256]{3,2,1,0:T(8,128)S(1)}, u32[]{:S(2)}, u32[]{:S(2)}) collective-permute-start(s32[8,4,8,256]{3,2,1,0:T(8,128)S(1)} %all-to-all-done.1.ids_ref.ido_ref), channel_id=1, source_target_pairs={{0,8},{8,16},{16,24},{24,32},{32,40},{40,48},{48,56},{56,64},{64,7... | collective-permute-start | bytes 786440 | tf_op jit(solution)/shard_map/ppermute | solution.py:354
  87.2 1.3 %collective-permute-start.3 = (s32[8,4,8,256]{3,2,1,0:T(8,128)S(1)}, s32[8,4,8,256]{3,2,1,0:T(8,128)S(1)}, u32[]{:S(2)}, u32[]{:S(2)}) collective-permute-start(s32[8,4,8,256]{3,2,1,0:T(8,128)S(1)} %all-to-all-done.1.ids_ref.ido_ref), channel_id=1, source_target_pairs={{8,0},{16,8},{24,16},{32,24},{40,32},{48,40},{56,48},{64,56},{72,6... | collective-permute-start | bytes 786440 | tf_op jit(solution)/shard_map/ppermute | solution.py:354
  88.5 4.0 %collective-permute-start.4 = (f32[8,8,256]{2,1,0:T(8,128)S(1)}, f32[8,8,256]{2,1,0:T(8,128)S(1)}, u32[]{:S(2)}, u32[]{:S(2)}) collective-permute-start(f32[8,8,256]{2,1,0:T(8,128)S(1)} %get-tuple-element.10), channel_id=1, source_target_pairs={{0,8},{8,16},{16,24},{24,32},{32,40},{40,48},{48,56},{56,64},{64,7... | collective-permute-start | bytes 196616 | tf_op jit(solution)/shard_map/ppermute | solution.py:354
  92.5 1.3 %collective-permute-start.5 = (f32[8,8,256]{2,1,0:T(8,128)S(1)}, f32[8,8,256]{2,1,0:T(8,128)S(1)}, u32[]{:S(2)}, u32[]{:S(2)}) collective-permute-start(f32[8,8,256]{2,1,0:T(8,128)S(1)} %get-tuple-element.9), channel_id=1, source_target_pairs={{8,0},{16,8},{24,16},{32,24},{40,32},{48,40},{56,48},{64,56},{72,6... | collective-permute-start | bytes 196616 | tf_op jit(solution)/shard_map/ppermute | solution.py:354
  93.8 6.3 %all-to-all-done.5 = f32[8,16,2048]{2,1,0:T(8,128)S(1)} async-done(((f32[8,16,2048]{2,1,0:T(8,128)}), f32[8,16,2048]{2,1,0:T(8,128)S(1)}, u32[]{:S(2)}, u32[]{:S(2)}) %all-to-all-start.5) | async-done | bytes 1048608 | tf_op jit(solution)/shard_map/all_to_all | solution.py:348
  100.1 0.8 shard_map.74
  100.9 3.5 %all-to-all-start.6 = ((f32[16,8,128]{2,1,0:T(8,128)}), f32[16,8,128]{2,1,0:T(8,128)S(1)}, u32[]{:S(2)}, u32[]{:S(2)}) async-start(f32[16,8,128]{2,1,0:T(8,128)} %shard_map.74), calls=%async_computation.6 | async-start | bytes 131072 | tf_op jit(solution)/shard_map/all_to_all | solution.py:383
  104.5 0.0 collective-permute-done.2.idl_ref
  104.5 0.0 collective-permute-done.3.idr_ref
  104.5 0.0 collective-permute-done.4.ul_ref
  104.5 0.0 collective-permute-done.5.ur_ref
  104.5 6.5 %all-to-all-done.6.table_ref = f32[16,8,128]{2,1,0:T(8,128)S(1)} async-done(((f32[16,8,128]{2,1,0:T(8,128)}), f32[16,8,128]{2,1,0:T(8,128)S(1)}, u32[]{:S(2)}, u32[]{:S(2)}) %all-to-all-start.6) | async-done | bytes 65568 | tf_op jit(solution)/shard_map/all_to_all | solution.py:383
  110.9 5.5 %shard_map.75 = f32[8,4,8,256]{3,2,1,0:T(8,128)S(1)} custom-call(s32[1]{0:T(128)} %bitcast.place_ref, f32[16,4,8,128]{3,2,1,0:T(8,128)S(1)} %all_to_all.42.got_ref, f32[16,8,128]{2,1,0:T(8,128)S(1)} %all-to-all-done.6.table_ref, f32[16,5,2,8,128]{4,3,2,1,0:T(8,128)S(1)} %all-to-all-done.3.coefs_ref, s32[8,4,8,256]{3,2,1,0:T(8,128)S(1)} %collective-permute-done.2.idl_ref, ...), custom_call_target="tpu_custom_call" | custom-call | flops 10000000 | bytes 1048576 | tf_op jit(solution)/shard_map/pallas_call | solution.py:330
  116.4 11.9 %all_to_all.43 = f32[8,4,8,256]{3,2,1,0:T(8,128)S(1)} all-to-all(f32[8,4,8,256]{3,2,1,0:T(8,128)S(1)} %shard_map.75), channel_id=1, replica_groups=mesh['gx'=16,'gy'=8] {'gy'}, dimensions={0} | all-to-all | bytes 524288 | tf_op jit(solution)/shard_map/all_to_all | solution.py:391
  128.3 0.7 copy.14
  (9 shorter events, 0.1 us)
Async XLA Ops:
  1.6 0.7 copy-start.3
  13.8 10.7 %copy-start.2 = (s32[4,8,256]{2,1,0:T(8,128)S(1)}, s32[4,8,256]{2,1,0:T(8,128)}, u32[]{:S(2)}) copy-start(s32[4,8,256]{2,1,0:T(8,128)} %param.8) | copy-start | bytes 98308
  25.2 10.9 %all-to-all-start.1 = ((s32[8,4,8,256]{3,2,1,0:T(8,128)}), s32[8,4,8,256]{3,2,1,0:T(8,128)S(1)}, u32[]{:S(2)}, u32[]{:S(2)}) async-start(s32[8,4,8,256]{3,2,1,0:T(8,128)} %broadcast_in_dim.10), calls=%async_computation.1 | async-start | bytes 524288 | tf_op jit(solution)/shard_map/all_to_all | solution.py:348
  37.0 20.6 %copy-start = (bf16[1536,128]{1,0:T(8,128)(2,1)S(1)}, bf16[1536,128]{1,0:T(8,128)(2,1)}, u32[]{:S(2)}) copy-start(bf16[1536,128]{1,0:T(8,128)(2,1)} %constant.8.clone.pool_ref) | copy-start | bytes 1179652
  37.0 20.6 %all-to-all-start.3 = ((f32[16,5,2,8,128]{4,3,2,1,0:T(8,128)}), f32[16,5,2,8,128]{4,3,2,1,0:T(8,128)S(1)}, u32[]{:S(2)}, u32[]{:S(2)}) async-start(f32[16,5,2,8,128]{4,3,2,1,0:T(8,128)} %broadcast_in_dim.13), calls=%async_computation.3 | async-start | bytes 1310720 | tf_op jit(solution)/shard_map/all_to_all | solution.py:348
  43.9 11.7 %collective-permute-start = (f32[8,4,8,256]{3,2,1,0:T(8,128)S(1)}, f32[8,4,8,256]{3,2,1,0:T(8,128)S(1)}, u32[]{:S(2)}, u32[]{:S(2)}) collective-permute-start(f32[8,4,8,256]{3,2,1,0:T(8,128)S(1)} %all_to_all.41.to_ref), channel_id=1, source_target_pairs={{0,8},{8,16},{16,24},{24,32},{32,40},{40,48},{48,56},{56,64},{64,7... | collective-permute-start | bytes 786440 | tf_op jit(solution)/shard_map/ppermute | solution.py:354
  47.2 10.4 %collective-permute-start.1 = (f32[8,4,8,256]{3,2,1,0:T(8,128)S(1)}, f32[8,4,8,256]{3,2,1,0:T(8,128)S(1)}, u32[]{:S(2)}, u32[]{:S(2)}) collective-permute-start(f32[8,4,8,256]{3,2,1,0:T(8,128)S(1)} %all_to_all.41.to_ref), channel_id=1, source_target_pairs={{8,0},{16,8},{24,16},{32,24},{40,32},{48,40},{56,48},{64,56},{72,6... | collective-permute-start | bytes 786440 | tf_op jit(solution)/shard_map/ppermute | solution.py:354
  62.8 14.3 %copy-start.1 = (f32[16,2048]{1,0:T(8,128)S(1)}, f32[16,2048]{1,0:T(8,128)}, u32[]{:S(2)}) copy-start(f32[16,2048]{1,0:T(8,128)} %param.12) | copy-start | bytes 393220
  78.2 21.9 %all-to-all-start.5 = ((f32[8,16,2048]{2,1,0:T(8,128)}), f32[8,16,2048]{2,1,0:T(8,128)S(1)}, u32[]{:S(2)}, u32[]{:S(2)}) async-start(f32[8,16,2048]{2,1,0:T(8,128)} %broadcast_in_dim.14), calls=%async_computation.5 | async-start | bytes 2097152 | tf_op jit(solution)/shard_map/all_to_all | solution.py:348
  85.0 19.4 %collective-permute-start.2 = (s32[8,4,8,256]{3,2,1,0:T(8,128)S(1)}, s32[8,4,8,256]{3,2,1,0:T(8,128)S(1)}, u32[]{:S(2)}, u32[]{:S(2)}) collective-permute-start(s32[8,4,8,256]{3,2,1,0:T(8,128)S(1)} %all-to-all-done.1.ids_ref.ido_ref), channel_id=1, source_target_pairs={{0,8},{8,16},{16,24},{24,32},{32,40},{40,48},{48,56},{56,64},{64,7... | collective-permute-start | bytes 786440 | tf_op jit(solution)/shard_map/ppermute | solution.py:354
  87.2 17.2 %collective-permute-start.3 = (s32[8,4,8,256]{3,2,1,0:T(8,128)S(1)}, s32[8,4,8,256]{3,2,1,0:T(8,128)S(1)}, u32[]{:S(2)}, u32[]{:S(2)}) collective-permute-start(s32[8,4,8,256]{3,2,1,0:T(8,128)S(1)} %all-to-all-done.1.ids_ref.ido_ref), channel_id=1, source_target_pairs={{8,0},{16,8},{24,16},{32,24},{40,32},{48,40},{56,48},{64,56},{72,6... | collective-permute-start | bytes 786440 | tf_op jit(solution)/shard_map/ppermute | solution.py:354
  88.5 15.9 %collective-permute-start.4 = (f32[8,8,256]{2,1,0:T(8,128)S(1)}, f32[8,8,256]{2,1,0:T(8,128)S(1)}, u32[]{:S(2)}, u32[]{:S(2)}) collective-permute-start(f32[8,8,256]{2,1,0:T(8,128)S(1)} %get-tuple-element.10), channel_id=1, source_target_pairs={{0,8},{8,16},{16,24},{24,32},{32,40},{40,48},{48,56},{56,64},{64,7... | collective-permute-start | bytes 196616 | tf_op jit(solution)/shard_map/ppermute | solution.py:354
  92.5 11.9 %collective-permute-start.5 = (f32[8,8,256]{2,1,0:T(8,128)S(1)}, f32[8,8,256]{2,1,0:T(8,128)S(1)}, u32[]{:S(2)}, u32[]{:S(2)}) collective-permute-start(f32[8,8,256]{2,1,0:T(8,128)S(1)} %get-tuple-element.9), channel_id=1, source_target_pairs={{8,0},{16,8},{24,16},{32,24},{40,32},{48,40},{56,48},{64,56},{72,6... | collective-permute-start | bytes 196616 | tf_op jit(solution)/shard_map/ppermute | solution.py:354
  100.9 10.0 %all-to-all-start.6 = ((f32[16,8,128]{2,1,0:T(8,128)}), f32[16,8,128]{2,1,0:T(8,128)S(1)}, u32[]{:S(2)}, u32[]{:S(2)}) async-start(f32[16,8,128]{2,1,0:T(8,128)} %shard_map.74), calls=%async_computation.6 | async-start | bytes 131072 | tf_op jit(solution)/shard_map/all_to_all | solution.py:383

commit v2 on v1

v2 whole, which is shorter than its diff:
```python
import math

import jax
import jax.numpy as jnp
from jax import lax
from jax.experimental import pallas as pl
from jax.experimental.pallas import tpu as pltpu
from jax.sharding import PartitionSpec as P

F32 = jnp.float32
BF16 = jnp.bfloat16

PROLONG = 1.0 / 9.0


def nodes(low, high):
    theta = (high + low) / 2.0
    delta = (high - low) / 2.0
    reach = delta * math.cos(math.pi / 6.0)
    return (theta + reach, theta - reach, theta)


FINE_NODES = tuple(6.0 * node for node in nodes(2.0 / 30.0, 2.0))
COARSE_NODES = nodes(0.19, 1.9)

RHS, CX, YT, CY, CZ = 8, 4, 8, 8, 256
GX, GY = 16, 8
LANES = 128
NC2 = 2048
HI = NC2 // LANES


def beside_in_row(row):
    sub = lax.broadcasted_iota(jnp.int32, row.shape, 1)
    lane = lax.broadcasted_iota(jnp.int32, row.shape, 2)
    zero_tile = jnp.zeros((1,) + row.shape[1:], F32)
    up = pltpu.roll(row, 1, 1)
    up = jnp.where(sub == 0, jnp.concatenate([zero_tile, up[:-1]], axis=0), up)
    down = pltpu.roll(row, CY - 1, 1)
    down = jnp.where(sub == CY - 1, jnp.concatenate([down[1:], zero_tile], axis=0), down)
    left = jnp.where(lane == 0, 0.0, pltpu.roll(row, 1, 2))
    right = jnp.where(lane == CZ - 1, 0.0, pltpu.roll(row, CZ - 1, 2))
    return (up + down) + (left + right)


def relax(low, row, high, node):
    return (1.0 - 6.0 / node) * row + (1.0 / node) * (low + high + beside_in_row(row))


def beside_grid(grid):
    sub = lax.broadcasted_iota(jnp.int32, grid.shape, 1)
    lane = lax.broadcasted_iota(jnp.int32, grid.shape, 2)
    turned = pltpu.roll(grid, LANES // 2, 2)
    low_y = jnp.where(lane < LANES // 2, pltpu.roll(turned, 1, 1), turned)
    high_y = jnp.where(lane < LANES // 2, turned, pltpu.roll(turned, YT - 1, 1))
    low_z = pltpu.roll(grid, 1, 2)
    high_z = pltpu.roll(grid, LANES - 1, 2)
    del sub
    return low_y, high_y, low_z, high_z


def lower_of(grid):
    return jnp.concatenate([jnp.zeros((1,) + grid.shape[1:], F32), grid[:-1]], axis=0)


def upper_of(grid):
    return jnp.concatenate([grid[1:], jnp.zeros((1,) + grid.shape[1:], F32)], axis=0)


NAX = 2 * GX
WINDOW = 10
FIELDS = 5


def with_lower(diag, ux, uy, uz):
    return (diag, lower_of(ux), ux, beside_grid(uy)[0], uy, beside_grid(uz)[2], uz, 1.0 / diag)


def coarse_apply(grid, coefs, below=None, above=None):
    diag, lx, ux, ly, uy, lz, uz = coefs[:7]
    low_y, high_y, low_z, high_z = beside_grid(grid)
    low_x = lower_of(grid) if below is None else jnp.concatenate([below[None], grid[:-1]], axis=0)
    high_x = upper_of(grid) if above is None else jnp.concatenate([grid[1:], above[None]], axis=0)
    linked = lx * low_x + ux * high_x
    linked = linked + ly * low_y + uy * high_y
    linked = linked + lz * low_z + uz * high_z
    return diag * grid - linked


def coarse_smooth(residual, coefs, with_last):
    total = None
    for k, node in enumerate(COARSE_NODES):
        update = (1.0 / node) * coefs[7] * residual
        total = update if total is None else total + update
        if k < 2 or with_last:
            residual = residual - coarse_apply(update, coefs)
    return total, residual


def split3(value):
    first = value.astype(BF16)
    rest = value - first.astype(F32)
    second = rest.astype(BF16)
    third = (rest - second.astype(F32)).astype(BF16)
    return first, second, third


def tiles_kernel(ids_ref, diag_ref, links_ref, coarse_ids_ref, out_ref, id_buf, diag_buf, link_buf, cid_buf, sems):
    pairs = ((ids_ref, id_buf), (diag_ref, diag_buf), (links_ref, link_buf), (coarse_ids_ref, cid_buf))
    copies = [pltpu.make_async_copy(src, dst, sems.at[k]) for k, (src, dst) in enumerate(pairs)]
    for copy in copies:
        copy.start()
    for copy in copies:
        copy.wait()
    fields = (
        diag_buf[...],
        link_buf[1],
        link_buf[3],
        link_buf[5],
        cid_buf[...].astype(F32),
    )
    rows = [
        jnp.concatenate([field[half, k : k + 1] for half in range(2) for k in range(2)], axis=1)
        for field in fields
    ]
    rows.append(jnp.zeros((3, CZ), F32))
    for x in range(CX):
        out_ref[x] = id_buf[x].astype(F32)
    out_ref[CX] = jnp.concatenate(rows, axis=0)


SHARED = 3 * CX + 1


def share_kernel(mine_ref, low_ref, high_ref, out_ref):
    out_ref[0 : CX + 1] = mine_ref[...]
    out_ref[CX + 1 : 2 * CX + 1] = low_ref[...]
    out_ref[2 * CX + 1 :] = high_ref[...]


def shared_tile(near_ref, far_ref, chip, core, j, tile):
    k = lax.rem(chip + 4 - j // 2, 4)
    return jnp.where(core == j % 2, near_ref[k, tile], far_ref[k, tile])


def shared_ids(near_ref, far_ref, chip, core, tile):
    rows = [shared_tile(near_ref, far_ref, chip, core, j, tile) for j in range(GY)]
    return jnp.stack(rows, axis=0).astype(jnp.int32)


def pool_matrix():
    lane = lax.broadcasted_iota(jnp.int32, (CZ, LANES), 1)
    gap = lane - lax.broadcasted_iota(jnp.int32, (CZ, LANES), 0) // 4
    parts = []
    for half in range(2):
        for shift in range(-1, 2):
            hit = jnp.logical_and(gap == half * 64 + shift, lane // 64 == half)
            parts.append(jnp.where(hit, 1.0, 0.0).astype(BF16))
    return jnp.concatenate(parts, axis=0)


EDGE = 4
ROWS = CX + 2 * EDGE
U_EDGE = 2


def relax_rows(src, dst, reach, node, keep_low, keep_high, plus=None):
    for k in range(EDGE - reach, EDGE + CX + reach):
        row = relax(src[k - 1], src[k], src[k + 1], node)
        if k < EDGE:
            row = row * keep_low
        elif k >= EDGE + CX:
            row = row * keep_high
        dst[k] = row if plus is None else row + plus[k - EDGE + U_EDGE]


def down_kernel(where_ref, tl_ref, to_ref, tr_ref, smooth_ref, u_ref, up_ref, down_ref, a_ref, b_ref):
    place = where_ref[0]
    keep_low = jnp.where(place > 0, 1.0, 0.0).astype(F32)
    keep_high = jnp.where(place < GX - 1, 1.0, 0.0).astype(F32)
    gates = keep_low, keep_high
    first, second, third = FINE_NODES
    for x in range(CX):
        a_ref[x] = tl_ref[:, x] * keep_low
        a_ref[EDGE + x] = to_ref[:, x]
        a_ref[EDGE + CX + x] = tr_ref[:, x] * keep_high

    relax_rows(a_ref, b_ref, 3, first, *gates)
    shift = EDGE - U_EDGE
    for k in range(CX + 2 * U_EDGE):
        u_ref[k] = (1.0 / first) * a_ref[k + shift] + (1.0 / second) * b_ref[k + shift]
    relax_rows(b_ref, a_ref, 2, second, *gates)
    for k in range(CX + 2 * U_EDGE):
        u_ref[k] = u_ref[k] + (1.0 / third) * a_ref[k + shift]
    up_ref[...] = u_ref[U_EDGE + 1]
    down_ref[...] = u_ref[U_EDGE + 2]
    relax_rows(a_ref, b_ref, 1, third, *gates)
    for x in range(CX):
        k = EDGE + x
        smooth_ref[x] = relax(b_ref[k - 1], b_ref[k], b_ref[k + 1], 1.0 / PROLONG)


def pool_kernel(where_ref, smooth_ref, near_ref, far_ref, send_ref, tile_ref):
    chip, core = where_ref[1], where_ref[2]
    shape = (YT, CY, CZ)
    home = lax.broadcasted_iota(jnp.int32, shape, 2) // 4
    codes = []
    for x in range(CX):
        ids = shared_ids(near_ref, far_ref, chip, core, x)
        codes.append((ids >> 6) * 3 + ((ids & 63) - home) + 1)
    pooled = []
    for half in range(2):
        parts = []
        for k in range(6):
            total = jnp.zeros(shape, F32)
            for x in range(CX):
                total = total + jnp.where(codes[x] == half * 6 + k, smooth_ref[x], 0.0)
            parts.append(jnp.sum(total, axis=1))
        pooled.append(jnp.concatenate(parts, axis=1))
    pooled = jnp.concatenate(pooled, axis=0)
    pieces = jnp.concatenate(split3(pooled), axis=0)
    sums = jnp.dot(pieces, pool_matrix(), preferred_element_type=F32)
    rows = 2 * YT
    target = sums[:rows] + sums[rows : 2 * rows] + sums[2 * rows :]
    tiles = [target[:YT], target[YT:]]
    for j in range(GY):
        tile_ref[j] = shared_tile(near_ref, far_ref, chip, core, j, CX)
    for k in range(FIELDS):
        for half in range(2):
            tiles.append(tile_ref[:, k, half * LANES : (half + 1) * LANES])
    for i in range(GX):
        for k, tile in enumerate(tiles):
            send_ref[i, k] = tile


def solve_kernel(where_ref, got_ref, near_ref, far_ref, send_ref, window_ref, full_ref, total_ref):
    def grid(k):
        return jnp.stack([got_ref[x // 2, 2 * k + x % 2] for x in range(NAX)], axis=0)

    coefs = with_lower(grid(1), grid(2), grid(3), grid(4))
    pre, residual = coarse_smooth(grid(0), coefs, True)
    for k, value in enumerate((*coefs, pre, residual)):
        full_ref[k] = value
    place = where_ref[0]
    for k in range(10):
        for w in range(WINDOW):
            x = 2 * place + w - 4
            row = full_ref[k, jnp.clip(x, 0, NAX - 1)]
            if not 4 <= w < 6:
                row = jnp.where(jnp.logical_and(x >= 0, x < NAX), row, 1.0 if k in (0, 7) else 0.0)
            window_ref[k, w] = row
    ids = grid(5).astype(jnp.int32)
    high_of = ids >> 7
    low_of = ids & (LANES - 1)
    high_iota = lax.broadcasted_iota(jnp.int32, (HI, LANES), 0)
    low_iota = lax.broadcasted_iota(jnp.int32, (LANES, LANES), 0)
    counted = jnp.zeros((3 * HI, LANES), F32)
    for x in range(NAX):
        left, right = [], []
        for k in range(YT):
            picked = jnp.where(high_of[x, k : k + 1] == high_iota, residual[x, k : k + 1], 0.0)
            left.append(jnp.concatenate(split3(picked), axis=0))
            right.append(jnp.where(low_of[x, k : k + 1] == low_iota, 1.0, 0.0).astype(BF16))
        counted = counted + lax.dot_general(
            jnp.concatenate(left, axis=1),
            jnp.concatenate(right, axis=1),
            (((1,), (1,)), ((), ())),
            preferred_element_type=F32,
        )
    target = counted[:HI] + counted[HI : 2 * HI] + counted[2 * HI :]
    chip, core = where_ref[1], where_ref[2]
    for ref, side in ((near_ref, core), (far_ref, 1 - core)):
        for k in range(4):
            total = jnp.zeros((HI, LANES), F32)
            for h in range(HI):
                total = total + ref[k, :, h * LANES : (h + 1) * LANES] * target[h : h + 1]
            at = lax.rem(chip + 4 - k, 4) * 2 + side
            total_ref[pl.ds(pl.multiple_of(at * HI, HI), HI)] = total
    row = jnp.sum(total_ref[...].T, axis=0, keepdims=True)
    tile = jnp.broadcast_to(row, (8, LANES))
    for i in range(GX):
        send_ref[i] = tile


def lane_take(table, index):
    return jnp.take_along_axis(table, index, axis=1, mode="promise_in_bounds")


def up_kernel(
    where_ref,
    table_ref,
    window_ref,
    got_ref,
    near_ref,
    far_ref,
    u_ref,
    ul_ref,
    ur_ref,
    out_ref,
    post_ref,
    a_ref,
    b_ref,
):
    place, chip, core = where_ref[0], where_ref[1], where_ref[2]
    keep_low = jnp.where(place > 0, 1.0, 0.0).astype(F32)
    keep_high = jnp.where(place < GX - 1, 1.0, 0.0).astype(F32)
    coefs = tuple(window_ref[k] for k in range(8))
    picked = []
    for w in range(-5, 7):
        unknown = got_ref[jnp.clip(place + w // 2, 0, GX - 1), 2 * FIELDS + w % 2].astype(jnp.int32)
        high_of = unknown >> 7
        low_of = unknown & (LANES - 1)
        value = jnp.zeros((YT, LANES), F32)
        for k in range(HI):
            table = jnp.broadcast_to(table_ref[k, 0:1], (YT, LANES))
            value = jnp.where(high_of == k, lane_take(table, low_of), value)
        picked.append(value)
    coarsest = jnp.stack(picked[1:-1], axis=0)
    rest = window_ref[9] - coarse_apply(coarsest, coefs, picked[0], picked[-1])
    update, unused = coarse_smooth(rest, coefs, False)
    post = window_ref[8] + coarsest + update
    for k in range(6):
        gate = keep_low if k < 2 else (keep_high if k >= 4 else None)
        row = post[k + 2]
        post_ref[k] = row if gate is None else row * gate

    for slab, first_tile in ((0, CX + 1), (1, 0), (2, 2 * CX + 1)):
        for x in range(CX):
            ids = shared_ids(near_ref, far_ref, chip, core, first_tile + x)
            for k in range(YT):
                table0 = jnp.broadcast_to(post_ref[2 * slab, k : k + 1], (CY, LANES))
                table1 = jnp.broadcast_to(post_ref[2 * slab + 1, k : k + 1], (CY, LANES))
                for part in range(2):
                    lanes = slice(part * LANES, (part + 1) * LANES)
                    cell = ids[k, :, lanes]
                    low = cell & (LANES - 1)
                    value = jnp.where(cell >= LANES, lane_take(table1, low), lane_take(table0, low))
                    a_ref[slab * CX + x, k, :, lanes] = value

    gates = keep_low, keep_high
    first, second, third = FINE_NODES
    relax_rows(a_ref, b_ref, 2, 1.0 / PROLONG, *gates, plus=u_ref)
    for k, u, gate in ((EDGE - 3, ul_ref, keep_low), (EDGE + CX + 2, ur_ref, keep_high)):
        b_ref[k] = (relax(a_ref[k - 1], a_ref[k], a_ref[k + 1], 1.0 / PROLONG) + u[...]) * gate
    relax_rows(b_ref, a_ref, 2, first, *gates)
    relax_rows(a_ref, b_ref, 1, second, *gates)
    for x in range(CX):
        k = EDGE + x
        out_ref[:, x] = relax(b_ref[k - 1], b_ref[k], b_ref[k + 1], third) + u_ref[U_EDGE + x]


def call(kernel, out_shape, scratch, flops, scalars=0, inputs=pltpu.VMEM, limit=24):
    def spec(k):
        return pl.BlockSpec(memory_space=pltpu.SMEM if k < scalars else inputs)

    def run(*args):
        return pl.pallas_call(
            kernel,
            out_shape=out_shape,
            in_specs=[spec(k) for k in range(len(args))],
            out_specs=jax.tree.map(lambda _: pl.BlockSpec(memory_space=pltpu.VMEM), out_shape),
            scratch_shapes=scratch,
            compiler_params=pltpu.CompilerParams(vmem_limit_bytes=limit * 1024 * 1024),
            cost_estimate=pl.CostEstimate(flops=flops, bytes_accessed=2**20, transcendentals=0),
        )(*args)

    return run


def shape_of(*dims):
    return jax.ShapeDtypeStruct(dims, F32)


def shifted(value, step):
    return lax.ppermute(value, "gx", [(k, (k + step) % GX) for k in range(GX)])


FINE_FLOPS = 3 * 10**10


def round_chips(value):
    return [lax.ppermute(value, "gy", [(j, (j + 2 * k) % GY) for j in range(GY)]) for k in range(1, 4)]


def other_core(value):
    return lax.ppermute(value, "gy", [(j, j ^ 1) for j in range(GY)])


def local(right_side, fine_ids, coarse_diag, coarse_links, coarse_ids, coarsest_inverse):
    row = lax.axis_index("gy")
    place = jnp.stack([lax.axis_index("gx"), row // 2, row % 2]).astype(jnp.int32)
    cells = lax.all_to_all(right_side, "gy", 0, 0, tiled=True)
    low, high = shifted(cells, 1), shifted(cells, -1)

    arguments = (fine_ids, coarse_diag, coarse_links, coarse_ids)
    tiles = call(
        tiles_kernel,
        pltpu.VMEM((CX + 1, CY, CZ), F32),
        [
            pltpu.VMEM((CX, CY, CZ), jnp.int32),
            pltpu.VMEM((2, 2, 64), F32),
            pltpu.VMEM((6, 2, 2, 64), F32),
            pltpu.VMEM((2, 2, 64), jnp.int32),
            pltpu.SemaphoreType.DMA((4,)),
        ],
        10**8,
        inputs=pltpu.HBM,
    )(*(pltpu.with_memory_space_constraint(value, pltpu.HBM) for value in arguments))
    shared = call(share_kernel, pltpu.VMEM((SHARED, CY, CZ), F32), [], 10**8)(
        tiles, shifted(tiles[:CX], 1), shifted(tiles[:CX], -1)
    )
    near = jnp.stack([shared, *round_chips(shared)], axis=0)
    far = other_core(near)

    field = (ROWS, YT, CY, CZ)
    smooth, u, going_up, going_down = call(
        down_kernel,
        [
            pltpu.VMEM((CX, YT, CY, CZ), F32),
            pltpu.VMEM((CX + 2 * U_EDGE, YT, CY, CZ), F32),
            pltpu.VMEM((YT, CY, CZ), F32),
            pltpu.VMEM((YT, CY, CZ), F32),
        ],
        [pltpu.VMEM(field, F32), pltpu.VMEM(field, F32)],
        FINE_FLOPS,
        1,
    )(place, low, cells, high)
    send = call(
        pool_kernel,
        pltpu.VMEM((GX, 2 + 2 * FIELDS, YT, LANES), F32),
        [pltpu.VMEM((GY, CY, CZ), F32)],
        2 * 10**9,
        1,
    )(place, smooth, near, far)
    send, inverse = lax.optimization_barrier((send, coarsest_inverse))
    inverse_near = jnp.stack([inverse, *round_chips(inverse)], axis=0)
    inverse_far = other_core(inverse_near)
    u_low, u_high = shifted(going_up, 1), shifted(going_down, -1)
    got = lax.all_to_all(send, "gx", 0, 0, tiled=True)
    send, window = call(
        solve_kernel,
        [pltpu.VMEM((GX, 8, LANES), F32), pltpu.VMEM((10, WINDOW, YT, LANES), F32)],
        [pltpu.VMEM((10, NAX, YT, LANES), F32), pltpu.VMEM((LANES, LANES), F32)],
        3 * 10**9,
        1,
    )(place, got, inverse_near, inverse_far)
    table = lax.all_to_all(send, "gx", 0, 0, tiled=True)
    out = call(
        up_kernel,
        pltpu.VMEM((YT, CX, CY, CZ), F32),
        [pltpu.VMEM((6, YT, LANES), F32), pltpu.VMEM(field, F32), pltpu.VMEM(field, F32)],
        4 * 10**9,
        1,
    )(place, table, window, got, near, far, u, u_low, u_high)
    return lax.all_to_all(out, "gy", 0, 0, tiled=True)


def solution(mesh):
    return jax.shard_map(
        local,
        mesh=mesh,
        in_specs=(
            P(None, "gx", "gy", None),
            P("gx", "gy", None),
            P("gx", "gy", None),
            P(None, "gx", "gy", None),
            P("gx", "gy", None),
            P(("gx", "gy"), None),
        ),
        out_specs=P(None, "gx", "gy", None),
        check_vma=False,
    )
```

time: 130 us -> 90 us (0.69)
  blocking collectives: 48.2 us -> 15.3 us
  waiting for transfers between devices: 28.4 us -> 20.2 us
  starting transfers between devices: 34.9 us -> 39.3 us
  local copies, waits for them, and re-layouts: 5.89 us -> 1.76 us
    all_to_all x3 -> x0, blocking collectives: 36.3 us -> none  [the longest x1 14.3 us: local(): got = lax.all_to_all(send, 'gx', 0, 0, tiled=True)]
    ppermute x6 -> x14, starting transfers between devices: 13.3 us -> 23.9 us  [the longest x6 14.7 us: shifted(): return lax.ppermute(value, 'gx', [(k, (k + step) % GX) for k in range(GX)])]
    all_to_all x3 -> x2, waiting for transfers between devices: 12.8 us -> 4.29 us  [the longest x1 3.68 us: local(): got = lax.all_to_all(send, 'gx', 0, 0, tiled=True)]
    all_to_all x3 -> x2, starting transfers between devices: 18.1 us -> 11.4 us  [the longest x1 6.81 us: local(): cells = lax.all_to_all(right_side, 'gy', 0, 0, tiled=True)]
    all_to_all x1, blocking collectives: 11.9 us -> 15.3 us  [local(): return lax.all_to_all(out, 'gy', 0, 0, tiled=True)]
    broadcast_in_dim x4 -> x0, local copies, waits for them, and re-layouts: 2.72 us -> none  [to_all(): jnp.broadcast_to(value[None], (count,) + value.shape)]
    pallas_call x3 -> x6, Pallas kernels: 11.4 us -> 12.6 us  [run(): pl.pallas_call(kernel, out_shape=out_shape, in_specs=[spec(k) for k in ra...]
    ppermute x6 -> x14, waiting for transfers between devices: 9.12 us -> 9.4 us  [the longest x6 8.84 us: round_chips(): lax.ppermute(value, 'gy', [(j, (j + 2 * k) % GY) for j in range(GY)])]
  transfers between devices with their start and end apart: 10 -> 17, of which waited for: 5 -> 8; matrix products, arithmetic and copies ran while one was open for 0% -> 0% of each run, Pallas kernels for 1% -> 8%
where the time goes in v2:
time: 90 us; the launch traced here: 89.4 us
  starting transfers between devices  39.3 us (44%)
  waiting for transfers between devices  20.2 us (22%)
  blocking collectives  15.3 us (17%)
  Pallas kernels  12.6 us (14%)
  local copies, waits for them, and re-layouts  1.76 us (2%)
    all_to_all x1, blocking collectives, local(): return lax.all_to_all(out, 'gy', 0, 0, tiled=True)  15.3 us
    ppermute x6, starting transfers between devices, shifted(): return lax.ppermute(value, 'gx', [(k, (k + step) % GX) for k in range(GX)])  14.7 us
    pallas_call x6, Pallas kernels, run(): pl.pallas_call(kernel, out_shape=out_shape, in_specs=[spec(k) for k in ra...  12.6 us
    ppermute x6, waiting for transfers between devices, round_chips(): lax.ppermute(value, 'gy', [(j, (j + 2 * k) % GY) for j in range(GY)])  8.84 us
    all_to_all x1, starting transfers between devices, local(): cells = lax.all_to_all(right_side, 'gy', 0, 0, tiled=True)  6.81 us
    all_to_all x1, waiting for transfers between devices, local(): table = lax.all_to_all(send, 'gx', 0, 0, tiled=True)  6.49 us
    ppermute x6, starting transfers between devices, round_chips(): lax.ppermute(value, 'gy', [(j, (j + 2 * k) % GY) for j in range(GY)])  5.29 us
    all_to_all x1, starting transfers between devices, local(): got = lax.all_to_all(send, 'gx', 0, 0, tiled=True)  4.63 us
  transfers between devices with their start and end apart: 17, of which 8 were waited for; matrix products, arithmetic and copies ran while one was open for 0% of the time, Pallas kernels for 8%

profile of v2, /device:TPU:1, one launch (start us, length us, event | category | flops | bytes accessed | tf_op | source)
XLA Modules:
  0.0 89.4 jit_solution(11142064404253247598)
XLA Ops:
  0.0 6.8 %all-to-all-start = ((f32[8,4,8,256]{3,2,1,0:T(8,128)}), f32[8,4,8,256]{3,2,1,0:T(8,128)S(1)}, u32[]{:S(2)}, u32[]{:S(2)}) async-start(f32[8,4,8,256]{3,2,1,0:T(8,128)} %param.6), calls=%async_computation | async-start | bytes 524288 | tf_op jit(solution)/shard_map/all_to_all | solution.py:392
  6.8 0.9 shard_map.65.mine_ref
  7.7 5.0 %collective-permute-start.3 = (f32[4,8,256]{2,1,0:T(8,128)S(1)}, f32[4,8,256]{2,1,0:T(8,128)S(1)}, u32[]{:S(2)}, u32[]{:S(2)}) collective-permute-start(f32[4,8,256]{2,1,0:T(8,128)S(1)} %slice.5), channel_id=1, source_target_pairs={{0,120},{8,0},{16,8},{24,16},{32,24},{40,32},{48,40},{56,48},{64,5... | collective-permute-start | bytes 98312 | tf_op jit(solution)/shard_map/ppermute | solution.py:375
  12.7 0.0 collective-permute-start.2
  12.7 0.6 all-to-all-done.to_ref
  13.3 4.9 %collective-permute-start.1 = (f32[8,4,8,256]{3,2,1,0:T(8,128)S(1)}, f32[8,4,8,256]{3,2,1,0:T(8,128)S(1)}, u32[]{:S(2)}, u32[]{:S(2)}) collective-permute-start(f32[8,4,8,256]{3,2,1,0:T(8,128)S(1)} %all-to-all-done.to_ref), channel_id=1, source_target_pairs={{0,120},{8,0},{16,8},{24,16},{32,24},{40,32},{48,40},{56,48},{64,5... | collective-permute-start | bytes 786440 | tf_op jit(solution)/shard_map/ppermute | solution.py:375
  18.2 0.0 collective-permute-start
  18.3 0.0 collective-permute-done.3.high_ref
  18.3 0.5 collective-permute-done.2.low_ref
  18.8 2.7 %collective-permute-start.6 = (f32[13,8,256]{2,1,0:T(8,128)S(1)}, f32[13,8,256]{2,1,0:T(8,128)S(1)}, u32[]{:S(2)}, u32[]{:S(2)}) collective-permute-start(f32[13,8,256]{2,1,0:T(8,128)S(1)} %shard_map.66), channel_id=1, source_target_pairs={{0,6},{1,7},{2,0},{3,1},{4,2},{5,3},{6,4},{7,5},{8,14},{9,15},{10,... | collective-permute-start | bytes 319496 | tf_op jit(solution)/shard_map/ppermute | solution.py:382
  21.5 0.6 collective-permute-start.5
  22.1 0.6 collective-permute-start.4
  22.6 0.1 pad_add_fusion.where_ref
  22.7 0.5 collective-permute-done.6
  23.2 3.6 %collective-permute-done.5 = f32[13,8,256]{2,1,0:T(8,128)S(1)} collective-permute-done((f32[13,8,256]{2,1,0:T(8,128)S(1)}, f32[13,8,256]{2,1,0:T(8,128)S(1)}, u32[]{:S(2)}, u32[]{:S(2)}) %collective-permute-start.5) | collective-permute-done | bytes 106528 | tf_op jit(solution)/shard_map/ppermute | solution.py:382
  26.8 1.1 %collective-permute-done.4 = f32[13,8,256]{2,1,0:T(8,128)S(1)} collective-permute-done((f32[13,8,256]{2,1,0:T(8,128)S(1)}, f32[13,8,256]{2,1,0:T(8,128)S(1)}, u32[]{:S(2)}, u32[]{:S(2)}) %collective-permute-start.4) | collective-permute-done | bytes 106528 | tf_op jit(solution)/shard_map/ppermute | solution.py:382
  28.0 3.0 %collective-permute-start.7 = (f32[4,13,8,256]{3,2,1,0:T(8,128)S(1)}, f32[4,13,8,256]{3,2,1,0:T(8,128)S(1)}, u32[]{:S(2)}, u32[]{:S(2)}) collective-permute-start(f32[4,13,8,256]{3,2,1,0:T(8,128)S(1)} %pad_maximum_fusion.1.near_ref), channel_id=1, source_target_pairs={{0,1},{1,0},{2,3},{3,2},{4,5},{5,4},{6,7},{7,6},{8,9},{9,8},{10,11... | collective-permute-start | bytes 1277960 | tf_op jit(solution)/shard_map/ppermute | solution.py:386
  31.0 0.0 collective-permute-done.1.tr_ref
  31.0 0.0 collective-permute-done.tl_ref
  31.0 1.7 %shard_map.64 = (f32[4,8,8,256]{3,2,1,0:T(8,128)S(1)}, f32[8,8,8,256]{3,2,1,0:T(8,128)S(1)}, f32[8,8,256]{2,1,0:T(8,128)S(1)}, f32[8,8,256]{2,1,0:T(8,128)S(1)}) custom-call(s32[3]{0:T(128)S(1)} %pad_add_fusion.where_ref, f32[8,4,8,256]{3,2,1,0:T(8,128)S(1)} %collective-permute-done.tl_ref, f32[8,4,8,256]{3,2,1,0:T(8,128)S(1)} %all-to-all-done.to_ref, ...), custom_call_target="tpu_custom_call" | custom-call | flops 30000001024 | bytes 1048576 | tf_op jit(solution)/shard_map/pallas_call | solution.py:357
  32.7 0.0 copy-start
  32.8 0.0 collective-permute-done.7.far_ref
  32.8 0.0 copy-start.2
  32.8 2.4 %shard_map.67 = f32[16,12,8,128]{3,2,1,0:T(8,128)} custom-call(s32[3]{0:T(128)S(1)} %pad_add_fusion.where_ref, f32[4,8,8,256]{3,2,1,0:T(8,128)S(1)} %get-tuple-element.13.smooth_ref, f32[4,13,8,256]{3,2,1,0:T(8,128)S(1)} %pad_maximum_fusion.1.near_ref, f32[4,13,8,256]{3,2,1,0:T(8,128)S(1)} %collective-permute-done.7.far_ref), custom_call_target="tpu_custom_call" | custom-call | flops 2000000000 | bytes 1048576 | tf_op jit(solution)/shard_map/pallas_call | solution.py:357
  35.1 0.0 copy-done
  35.1 0.0 copy-done.2
  35.1 0.3 collective-permute-start.10
  35.4 0.6 collective-permute-start.9
  36.0 0.6 collective-permute-start.8
  36.6 4.6 %all-to-all-start.1 = ((f32[16,12,8,128]{3,2,1,0:T(8,128)}), f32[16,12,8,128]{3,2,1,0:T(8,128)S(1)}, u32[]{:S(2)}, u32[]{:S(2)}) async-start(f32[16,12,8,128]{3,2,1,0:T(8,128)} %shard_map.67), calls=%async_computation.1 | async-start | bytes 1572864 | tf_op jit(solution)/shard_map/all_to_all | solution.py:439
  41.2 0.0 collective-permute-done.10
  41.3 0.0 collective-permute-done.9
  41.3 3.6 %collective-permute-done.8 = f32[16,2048]{1,0:T(8,128)S(1)} collective-permute-done((f32[16,2048]{1,0:T(8,128)S(1)}, f32[16,2048]{1,0:T(8,128)S(1)}, u32[]{:S(2)}, u32[]{:S(2)}) %collective-permute-start.8) | collective-permute-done | bytes 131104 | tf_op jit(solution)/shard_map/ppermute | solution.py:382
  44.9 0.9 collective-permute-start.11
  45.8 0.0 collective-permute-start.12
  45.8 4.8 %collective-permute-start.13 = (f32[8,8,256]{2,1,0:T(8,128)S(1)}, f32[8,8,256]{2,1,0:T(8,128)S(1)}, u32[]{:S(2)}, u32[]{:S(2)}) collective-permute-start(f32[8,8,256]{2,1,0:T(8,128)S(1)} %get-tuple-element.20), channel_id=1, source_target_pairs={{0,120},{8,0},{16,8},{24,16},{32,24},{40,32},{48,40},{56,48},{64,5... | collective-permute-start | bytes 196616 | tf_op jit(solution)/shard_map/ppermute | solution.py:375
  50.6 0.0 collective-permute-done.11.far_ref
  50.6 3.7 %all-to-all-done.1.got_ref = f32[16,12,8,128]{3,2,1,0:T(8,128)S(1)} async-done(((f32[16,12,8,128]{3,2,1,0:T(8,128)}), f32[16,12,8,128]{3,2,1,0:T(8,128)S(1)}, u32[]{:S(2)}, u32[]{:S(2)}) %all-to-all-start.1) | async-done | bytes 786464 | tf_op jit(solution)/shard_map/all_to_all | solution.py:439
  54.3 4.4 %shard_map.68 = (f32[16,8,128]{2,1,0:T(8,128)}, f32[10,10,8,128]{3,2,1,0:T(8,128)S(1)}) custom-call(s32[3]{0:T(128)S(1)} %pad_add_fusion.where_ref, f32[16,12,8,128]{3,2,1,0:T(8,128)S(1)} %all-to-all-done.1.got_ref, f32[4,16,2048]{2,1,0:T(8,128)S(1)} %pad_maximum_fusion.near_ref, f32[4,16,2048]{2,1,0:T(8,128)S(1)} %collective-permute-done.11.far_ref), custom_call_target="tpu_custom_call" | custom-call | flops 3000000000 | bytes 1048576 | tf_op jit(solution)/shard_map/pallas_call | solution.py:357
  58.6 4.0 %all-to-all-start.2 = ((f32[16,8,128]{2,1,0:T(8,128)}), f32[16,8,128]{2,1,0:T(8,128)S(1)}, u32[]{:S(2)}, u32[]{:S(2)}) async-start(f32[16,8,128]{2,1,0:T(8,128)} %get-tuple-element.16), calls=%async_computation.2 | async-start | bytes 131072 | tf_op jit(solution)/shard_map/all_to_all | solution.py:447
  62.6 0.0 collective-permute-done.12.ul_ref
  62.6 0.0 collective-permute-done.13.ur_ref
  62.6 6.5 %all-to-all-done.2.table_ref = f32[16,8,128]{2,1,0:T(8,128)S(1)} async-done(((f32[16,8,128]{2,1,0:T(8,128)}), f32[16,8,128]{2,1,0:T(8,128)S(1)}, u32[]{:S(2)}, u32[]{:S(2)}) %all-to-all-start.2) | async-done | bytes 65568 | tf_op jit(solution)/shard_map/all_to_all | solution.py:447
  69.1 0.0 copy-start.1
  69.1 1.0 %copy-done.1 = f32[8,8,8,256]{3,2,1,0:T(8,128)S(1)} copy-done((f32[8,8,8,256]{3,2,1,0:T(8,128)S(1)}, f32[8,8,8,256]{3,2,1,0:T(8,128)}, u32[]{:S(2)}) %copy-start.1) | copy-done | bytes 524312
  70.2 3.3 %shard_map.69 = f32[8,4,8,256]{3,2,1,0:T(8,128)S(1)} custom-call(s32[3]{0:T(128)S(1)} %pad_add_fusion.where_ref, f32[16,8,128]{2,1,0:T(8,128)S(1)} %all-to-all-done.2.table_ref, f32[10,10,8,128]{3,2,1,0:T(8,128)S(1)} %get-tuple-element.17.window_ref, f32[16,12,8,128]{3,2,1,0:T(8,128)S(1)} %all-to-all-done.1.got_ref, ...), custom_call_target="tpu_custom_call" | custom-call | flops 4000000000 | bytes 1048576 | tf_op jit(solution)/shard_map/pallas_call | solution.py:357
  73.5 15.3 %all_to_all.20 = f32[8,4,8,256]{3,2,1,0:T(8,128)S(1)} all-to-all(f32[8,4,8,256]{3,2,1,0:T(8,128)S(1)} %shard_map.69), channel_id=1, replica_groups=mesh['gx'=16,'gy'=8] {'gy'}, dimensions={0} | all-to-all | bytes 524288 | tf_op jit(solution)/shard_map/all_to_all | solution.py:455
  88.7 0.7 copy.8
  (4 shorter events, 0.1 us)
Async XLA Ops:
  0.0 13.3 %all-to-all-start = ((f32[8,4,8,256]{3,2,1,0:T(8,128)}), f32[8,4,8,256]{3,2,1,0:T(8,128)S(1)}, u32[]{:S(2)}, u32[]{:S(2)}) async-start(f32[8,4,8,256]{3,2,1,0:T(8,128)} %param.6), calls=%async_computation | async-start | bytes 524288 | tf_op jit(solution)/shard_map/all_to_all | solution.py:392
  7.7 10.5 %collective-permute-start.3 = (f32[4,8,256]{2,1,0:T(8,128)S(1)}, f32[4,8,256]{2,1,0:T(8,128)S(1)}, u32[]{:S(2)}, u32[]{:S(2)}) collective-permute-start(f32[4,8,256]{2,1,0:T(8,128)S(1)} %slice.5), channel_id=1, source_target_pairs={{0,120},{8,0},{16,8},{24,16},{32,24},{40,32},{48,40},{56,48},{64,5... | collective-permute-start | bytes 98312 | tf_op jit(solution)/shard_map/ppermute | solution.py:375
  12.7 6.1 %collective-permute-start.2 = (f32[4,8,256]{2,1,0:T(8,128)S(1)}, f32[4,8,256]{2,1,0:T(8,128)S(1)}, u32[]{:S(2)}, u32[]{:S(2)}) collective-permute-start(f32[4,8,256]{2,1,0:T(8,128)S(1)} %slice.5), channel_id=1, source_target_pairs={{0,8},{8,16},{16,24},{24,32},{32,40},{40,48},{48,56},{56,64},{64,7... | collective-permute-start | bytes 98312 | tf_op jit(solution)/shard_map/ppermute | solution.py:375
  13.3 17.7 %collective-permute-start.1 = (f32[8,4,8,256]{3,2,1,0:T(8,128)S(1)}, f32[8,4,8,256]{3,2,1,0:T(8,128)S(1)}, u32[]{:S(2)}, u32[]{:S(2)}) collective-permute-start(f32[8,4,8,256]{3,2,1,0:T(8,128)S(1)} %all-to-all-done.to_ref), channel_id=1, source_target_pairs={{0,120},{8,0},{16,8},{24,16},{32,24},{40,32},{48,40},{56,48},{64,5... | collective-permute-start | bytes 786440 | tf_op jit(solution)/shard_map/ppermute | solution.py:375
  18.2 12.8 %collective-permute-start = (f32[8,4,8,256]{3,2,1,0:T(8,128)S(1)}, f32[8,4,8,256]{3,2,1,0:T(8,128)S(1)}, u32[]{:S(2)}, u32[]{:S(2)}) collective-permute-start(f32[8,4,8,256]{3,2,1,0:T(8,128)S(1)} %all-to-all-done.to_ref), channel_id=1, source_target_pairs={{0,8},{8,16},{16,24},{24,32},{32,40},{40,48},{48,56},{56,64},{64,7... | collective-permute-start | bytes 786440 | tf_op jit(solution)/shard_map/ppermute | solution.py:375
  18.8 4.4 %collective-permute-start.6 = (f32[13,8,256]{2,1,0:T(8,128)S(1)}, f32[13,8,256]{2,1,0:T(8,128)S(1)}, u32[]{:S(2)}, u32[]{:S(2)}) collective-permute-start(f32[13,8,256]{2,1,0:T(8,128)S(1)} %shard_map.66), channel_id=1, source_target_pairs={{0,6},{1,7},{2,0},{3,1},{4,2},{5,3},{6,4},{7,5},{8,14},{9,15},{10,... | collective-permute-start | bytes 319496 | tf_op jit(solution)/shard_map/ppermute | solution.py:382
  21.5 5.4 %collective-permute-start.5 = (f32[13,8,256]{2,1,0:T(8,128)S(1)}, f32[13,8,256]{2,1,0:T(8,128)S(1)}, u32[]{:S(2)}, u32[]{:S(2)}) collective-permute-start(f32[13,8,256]{2,1,0:T(8,128)S(1)} %shard_map.66), channel_id=1, source_target_pairs={{0,4},{1,5},{2,6},{3,7},{4,0},{5,1},{6,2},{7,3},{8,12},{9,13},{10,... | collective-permute-start | bytes 319496 | tf_op jit(solution)/shard_map/ppermute | solution.py:382
  22.1 5.9 %collective-permute-start.4 = (f32[13,8,256]{2,1,0:T(8,128)S(1)}, f32[13,8,256]{2,1,0:T(8,128)S(1)}, u32[]{:S(2)}, u32[]{:S(2)}) collective-permute-start(f32[13,8,256]{2,1,0:T(8,128)S(1)} %shard_map.66), channel_id=1, source_target_pairs={{0,2},{1,3},{2,4},{3,5},{4,6},{5,7},{6,0},{7,1},{8,10},{9,11},{10,... | collective-permute-start | bytes 319496 | tf_op jit(solution)/shard_map/ppermute | solution.py:382
  28.0 4.7 %collective-permute-start.7 = (f32[4,13,8,256]{3,2,1,0:T(8,128)S(1)}, f32[4,13,8,256]{3,2,1,0:T(8,128)S(1)}, u32[]{:S(2)}, u32[]{:S(2)}) collective-permute-start(f32[4,13,8,256]{3,2,1,0:T(8,128)S(1)} %pad_maximum_fusion.1.near_ref), channel_id=1, source_target_pairs={{0,1},{1,0},{2,3},{3,2},{4,5},{5,4},{6,7},{7,6},{8,9},{9,8},{10,11... | collective-permute-start | bytes 1277960 | tf_op jit(solution)/shard_map/ppermute | solution.py:386
  32.7 2.4 %copy-start = (f32[8,8,8,256]{3,2,1,0:T(8,128)}, f32[8,8,8,256]{3,2,1,0:T(8,128)S(1)}, u32[]{:S(2)}) copy-start(f32[8,8,8,256]{3,2,1,0:T(8,128)S(1)} %get-tuple-element.18.u_ref) | copy-start | bytes 1572868
  32.8 2.4 %copy-start.2 = (f32[16,2048]{1,0:T(8,128)S(1)}, f32[16,2048]{1,0:T(8,128)}, u32[]{:S(2)}) copy-start(f32[16,2048]{1,0:T(8,128)} %param.11) | copy-start | bytes 393220
  35.1 6.1 %collective-permute-start.10 = (f32[16,2048]{1,0:T(8,128)S(1)}, f32[16,2048]{1,0:T(8,128)S(1)}, u32[]{:S(2)}, u32[]{:S(2)}) collective-permute-start(f32[16,2048]{1,0:T(8,128)S(1)} %copy-done.2), channel_id=1, source_target_pairs={{0,6},{1,7},{2,0},{3,1},{4,2},{5,3},{6,4},{7,5},{8,14},{9,15},{10,... | collective-permute-start | bytes 393224 | tf_op jit(solution)/shard_map/ppermute | solution.py:382
  35.4 5.8 %collective-permute-start.9 = (f32[16,2048]{1,0:T(8,128)S(1)}, f32[16,2048]{1,0:T(8,128)S(1)}, u32[]{:S(2)}, u32[]{:S(2)}) collective-permute-start(f32[16,2048]{1,0:T(8,128)S(1)} %copy-done.2), channel_id=1, source_target_pairs={{0,4},{1,5},{2,6},{3,7},{4,0},{5,1},{6,2},{7,3},{8,12},{9,13},{10,... | collective-permute-start | bytes 393224 | tf_op jit(solution)/shard_map/ppermute | solution.py:382
  36.0 8.8 %collective-permute-start.8 = (f32[16,2048]{1,0:T(8,128)S(1)}, f32[16,2048]{1,0:T(8,128)S(1)}, u32[]{:S(2)}, u32[]{:S(2)}) collective-permute-start(f32[16,2048]{1,0:T(8,128)S(1)} %copy-done.2), channel_id=1, source_target_pairs={{0,2},{1,3},{2,4},{3,5},{4,6},{5,7},{6,0},{7,1},{8,10},{9,11},{10,... | collective-permute-start | bytes 393224 | tf_op jit(solution)/shard_map/ppermute | solution.py:382
  36.6 17.6 %all-to-all-start.1 = ((f32[16,12,8,128]{3,2,1,0:T(8,128)}), f32[16,12,8,128]{3,2,1,0:T(8,128)S(1)}, u32[]{:S(2)}, u32[]{:S(2)}) async-start(f32[16,12,8,128]{3,2,1,0:T(8,128)} %shard_map.67), calls=%async_computation.1 | async-start | bytes 1572864 | tf_op jit(solution)/shard_map/all_to_all | solution.py:439
  44.9 5.7 %collective-permute-start.11 = (f32[4,16,2048]{2,1,0:T(8,128)S(1)}, f32[4,16,2048]{2,1,0:T(8,128)S(1)}, u32[]{:S(2)}, u32[]{:S(2)}) collective-permute-start(f32[4,16,2048]{2,1,0:T(8,128)S(1)} %pad_maximum_fusion.near_ref), channel_id=1, source_target_pairs={{0,1},{1,0},{2,3},{3,2},{4,5},{5,4},{6,7},{7,6},{8,9},{9,8},{10,11... | collective-permute-start | bytes 1572872 | tf_op jit(solution)/shard_map/ppermute | solution.py:386
  45.8 16.8 %collective-permute-start.12 = (f32[8,8,256]{2,1,0:T(8,128)S(1)}, f32[8,8,256]{2,1,0:T(8,128)S(1)}, u32[]{:S(2)}, u32[]{:S(2)}) collective-permute-start(f32[8,8,256]{2,1,0:T(8,128)S(1)} %get-tuple-element.19), channel_id=1, source_target_pairs={{0,8},{8,16},{16,24},{24,32},{32,40},{40,48},{48,56},{56,64},{64,7... | collective-permute-start | bytes 196616 | tf_op jit(solution)/shard_map/ppermute | solution.py:375
  45.8 16.9 %collective-permute-start.13 = (f32[8,8,256]{2,1,0:T(8,128)S(1)}, f32[8,8,256]{2,1,0:T(8,128)S(1)}, u32[]{:S(2)}, u32[]{:S(2)}) collective-permute-start(f32[8,8,256]{2,1,0:T(8,128)S(1)} %get-tuple-element.20), channel_id=1, source_target_pairs={{0,120},{8,0},{16,8},{24,16},{32,24},{40,32},{48,40},{56,48},{64,5... | collective-permute-start | bytes 196616 | tf_op jit(solution)/shard_map/ppermute | solution.py:375
  58.6 10.5 %all-to-all-start.2 = ((f32[16,8,128]{2,1,0:T(8,128)}), f32[16,8,128]{2,1,0:T(8,128)S(1)}, u32[]{:S(2)}, u32[]{:S(2)}) async-start(f32[16,8,128]{2,1,0:T(8,128)} %get-tuple-element.16), calls=%async_computation.2 | async-start | bytes 131072 | tf_op jit(solution)/shard_map/all_to_all | solution.py:447
  69.1 1.0 %copy-start.1 = (f32[8,8,8,256]{3,2,1,0:T(8,128)S(1)}, f32[8,8,8,256]{3,2,1,0:T(8,128)}, u32[]{:S(2)}) copy-start(f32[8,8,8,256]{3,2,1,0:T(8,128)} %copy-done) | copy-start | bytes 1572868

commit v3 on v2

--- a/solution.py
+++ b/solution.py
@@ -225,23 +225,33 @@
     tiles = [target[:YT], target[YT:]]
     for j in range(GY):
         tile_ref[j] = shared_tile(near_ref, far_ref, chip, core, j, CX)
+    halves = [
+        tile_ref[:, k, half * LANES : (half + 1) * LANES] for k in range(FIELDS) for half in range(2)
+    ]
     for k in range(FIELDS):
-        for half in range(2):
-            tiles.append(tile_ref[:, k, half * LANES : (half + 1) * LANES])
+        tiles.append(jnp.where(core == 0, halves[k], halves[FIELDS + k]))
     for i in range(GX):
         for k, tile in enumerate(tiles):
             send_ref[i, k] = tile
 
 
-def solve_kernel(where_ref, got_ref, near_ref, far_ref, send_ref, window_ref, full_ref, total_ref):
+def solve_kernel(
+    where_ref, got_ref, other_ref, near_ref, far_ref, send_ref, window_ref, ids_ref, full_ref, total_ref
+):
+    place, chip, core = where_ref[0], where_ref[1], where_ref[2]
+
     def grid(k):
-        return jnp.stack([got_ref[x // 2, 2 * k + x % 2] for x in range(NAX)], axis=0)
-
-    coefs = with_lower(grid(1), grid(2), grid(3), grid(4))
-    pre, residual = coarse_smooth(grid(0), coefs, True)
+        rows = []
+        for x in range(NAX):
+            side, at = divmod(2 * k + x % 2, FIELDS)
+            rows.append(jnp.where(core == side, got_ref[x // 2, 2 + at], other_ref[x // 2, at]))
+        return jnp.stack(rows, axis=0)
+
+    coefs = with_lower(grid(0), grid(1), grid(2), grid(3))
+    target = jnp.stack([got_ref[x // 2, x % 2] for x in range(NAX)], axis=0)
+    pre, residual = coarse_smooth(target, coefs, True)
     for k, value in enumerate((*coefs, pre, residual)):
         full_ref[k] = value
-    place = where_ref[0]
     for k in range(10):
         for w in range(WINDOW):
             x = 2 * place + w - 4
@@ -249,7 +259,11 @@
             if not 4 <= w < 6:
                 row = jnp.where(jnp.logical_and(x >= 0, x < NAX), row, 1.0 if k in (0, 7) else 0.0)
             window_ref[k, w] = row
-    ids = grid(5).astype(jnp.int32)
+    ids = grid(4)
+    full_ref[10] = ids
+    for w in range(WINDOW + 2):
+        ids_ref[w] = full_ref[10, jnp.clip(2 * place + w - 5, 0, NAX - 1)].astype(jnp.int32)
+    ids = ids.astype(jnp.int32)
     high_of = ids >> 7
     low_of = ids & (LANES - 1)
     high_iota = lax.broadcasted_iota(jnp.int32, (HI, LANES), 0)
@@ -268,7 +282,6 @@
             preferred_element_type=F32,
         )
     target = counted[:HI] + counted[HI : 2 * HI] + counted[2 * HI :]
-    chip, core = where_ref[1], where_ref[2]
     for ref, side in ((near_ref, core), (far_ref, 1 - core)):
         for k in range(4):
             total = jnp.zeros((HI, LANES), F32)
@@ -290,24 +303,28 @@
     where_ref,
     table_ref,
     window_ref,
-    got_ref,
+    ids_ref,
     near_ref,
     far_ref,
-    u_ref,
+    u_hbm,
     ul_ref,
     ur_ref,
     out_ref,
     post_ref,
     a_ref,
     b_ref,
+    u_ref,
+    u_sem,
 ):
+    u_copy = pltpu.make_async_copy(u_hbm, u_ref, u_sem)
+    u_copy.start()
     place, chip, core = where_ref[0], where_ref[1], where_ref[2]
     keep_low = jnp.where(place > 0, 1.0, 0.0).astype(F32)
     keep_high = jnp.where(place < GX - 1, 1.0, 0.0).astype(F32)
     coefs = tuple(window_ref[k] for k in range(8))
     picked = []
-    for w in range(-5, 7):
-        unknown = got_ref[jnp.clip(place + w // 2, 0, GX - 1), 2 * FIELDS + w % 2].astype(jnp.int32)
+    for w in range(WINDOW + 2):
+        unknown = ids_ref[w]
         high_of = unknown >> 7
         low_of = unknown & (LANES - 1)
         value = jnp.zeros((YT, LANES), F32)
@@ -339,6 +356,7 @@
 
     gates = keep_low, keep_high
     first, second, third = FINE_NODES
+    u_copy.wait()
     relax_rows(a_ref, b_ref, 2, 1.0 / PROLONG, *gates, plus=u_ref)
     for k, u, gate in ((EDGE - 3, ul_ref, keep_low), (EDGE + CX + 2, ur_ref, keep_high)):
         b_ref[k] = (relax(a_ref[k - 1], a_ref[k], a_ref[k + 1], 1.0 / PROLONG) + u[...]) * gate
@@ -349,9 +367,9 @@
         out_ref[:, x] = relax(b_ref[k - 1], b_ref[k], b_ref[k + 1], third) + u_ref[U_EDGE + x]
 
 
-def call(kernel, out_shape, scratch, flops, scalars=0, inputs=pltpu.VMEM, limit=24):
+def call(kernel, out_shape, scratch, flops, scalars=0, spaces=None):
     def spec(k):
-        return pl.BlockSpec(memory_space=pltpu.SMEM if k < scalars else inputs)
+        return pl.BlockSpec(memory_space=pltpu.SMEM if k < scalars else (spaces or {}).get(k, pltpu.VMEM))
 
     def run(*args):
         return pl.pallas_call(
@@ -360,17 +378,13 @@
             in_specs=[spec(k) for k in range(len(args))],
             out_specs=jax.tree.map(lambda _: pl.BlockSpec(memory_space=pltpu.VMEM), out_shape),
             scratch_shapes=scratch,
-            compiler_params=pltpu.CompilerParams(vmem_limit_bytes=limit * 1024 * 1024),
+            compiler_params=pltpu.CompilerParams(vmem_limit_bytes=24 * 1024 * 1024),
             cost_estimate=pl.CostEstimate(flops=flops, bytes_accessed=2**20, transcendentals=0),
         )(*args)
 
     return run
 
 
-def shape_of(*dims):
-    return jax.ShapeDtypeStruct(dims, F32)
-
-
 def shifted(value, step):
     return lax.ppermute(value, "gx", [(k, (k + step) % GX) for k in range(GX)])
 
@@ -378,8 +392,8 @@
 FINE_FLOPS = 3 * 10**10
 
 
-def round_chips(value):
-    return [lax.ppermute(value, "gy", [(j, (j + 2 * k) % GY) for j in range(GY)]) for k in range(1, 4)]
+def chip_below(value, step):
+    return lax.ppermute(value, "gy", [(j, (j + 2 * step) % GY) for j in range(GY)])
 
 
 def other_core(value):
@@ -404,12 +418,15 @@
             pltpu.SemaphoreType.DMA((4,)),
         ],
         10**8,
-        inputs=pltpu.HBM,
+        0,
+        dict.fromkeys(range(4), pltpu.HBM),
     )(*(pltpu.with_memory_space_constraint(value, pltpu.HBM) for value in arguments))
     shared = call(share_kernel, pltpu.VMEM((SHARED, CY, CZ), F32), [], 10**8)(
         tiles, shifted(tiles[:CX], 1), shifted(tiles[:CX], -1)
     )
-    near = jnp.stack([shared, *round_chips(shared)], axis=0)
+    inverse = [coarsest_inverse, chip_below(coarsest_inverse, 1), None, chip_below(coarsest_inverse, 3)]
+    shared, inverse[1], inverse[3] = lax.optimization_barrier((shared, inverse[1], inverse[3]))
+    near = jnp.stack([shared, *(chip_below(shared, k) for k in range(1, 4))], axis=0)
     far = other_core(near)
 
     field = (ROWS, YT, CY, CZ)
@@ -427,31 +444,44 @@
     )(place, low, cells, high)
     send = call(
         pool_kernel,
-        pltpu.VMEM((GX, 2 + 2 * FIELDS, YT, LANES), F32),
+        pltpu.VMEM((GX, 2 + FIELDS, YT, LANES), F32),
         [pltpu.VMEM((GY, CY, CZ), F32)],
         2 * 10**9,
         1,
     )(place, smooth, near, far)
-    send, inverse = lax.optimization_barrier((send, coarsest_inverse))
-    inverse_near = jnp.stack([inverse, *round_chips(inverse)], axis=0)
+    send, inverse[0] = lax.optimization_barrier((send, inverse[0]))
+    inverse[2] = chip_below(inverse[0], 2)
+    inverse_near = jnp.stack(inverse, axis=0)
     inverse_far = other_core(inverse_near)
     u_low, u_high = shifted(going_up, 1), shifted(going_down, -1)
     got = lax.all_to_all(send, "gx", 0, 0, tiled=True)
-    send, window = call(
+    got, u_low, u_high = lax.optimization_barrier((got, u_low, u_high))
+    send, window, unknowns = call(
         solve_kernel,
-        [pltpu.VMEM((GX, 8, LANES), F32), pltpu.VMEM((10, WINDOW, YT, LANES), F32)],
-        [pltpu.VMEM((10, NAX, YT, LANES), F32), pltpu.VMEM((LANES, LANES), F32)],
+        [
+            pltpu.VMEM((GX, 8, LANES), F32),
+            pltpu.VMEM((10, WINDOW, YT, LANES), F32),
+            pltpu.VMEM((WINDOW + 2, YT, LANES), jnp.int32),
+        ],
+        [pltpu.VMEM((11, NAX, YT, LANES), F32), pltpu.VMEM((LANES, LANES), F32)],
         3 * 10**9,
         1,
-    )(place, got, inverse_near, inverse_far)
+    )(place, got, other_core(got[:, 2:]), inverse_near, inverse_far)
     table = lax.all_to_all(send, "gx", 0, 0, tiled=True)
     out = call(
         up_kernel,
         pltpu.VMEM((YT, CX, CY, CZ), F32),
-        [pltpu.VMEM((6, YT, LANES), F32), pltpu.VMEM(field, F32), pltpu.VMEM(field, F32)],
+        [
+            pltpu.VMEM((6, YT, LANES), F32),
+            pltpu.VMEM(field, F32),
+            pltpu.VMEM(field, F32),
+            pltpu.VMEM((CX + 2 * U_EDGE, YT, CY, CZ), F32),
+            pltpu.SemaphoreType.DMA,
+        ],
         4 * 10**9,
         1,
-    )(place, table, window, got, near, far, u, u_low, u_high)
+        {6: pltpu.HBM},
+    )(place, table, window, unknowns, near, far, pltpu.with_memory_space_constraint(u, pltpu.HBM), u_low, u_high)
     return lax.all_to_all(out, "gy", 0, 0, tiled=True)
 
 

time: 90 us -> 86.3 us (0.959)
  waiting for transfers between devices: 20.2 us -> 13.9 us
  blocking collectives: 15.3 us -> 21.2 us
  starting transfers between devices: 39.3 us -> 37.6 us
  local copies, waits for them, and re-layouts: 1.76 us -> 0.74 us
    all_to_all x0 -> x1, blocking collectives: none -> 9.97 us  [local(): table = lax.all_to_all(send, 'gx', 0, 0, tiled=True)]
    all_to_all x1 -> x0, waiting for transfers between devices: 6.49 us -> none  [local(): table = lax.all_to_all(send, 'gx', 0, 0, tiled=True)]
    ppermute x6, waiting for transfers between devices: 0.56 us -> 5.91 us  [shifted(): return lax.ppermute(value, 'gx', [(k, (k + step) % GX) for k in range(GX)])]
    all_to_all x1, blocking collectives: 15.3 us -> 11.2 us  [local(): return lax.all_to_all(out, 'gy', 0, 0, tiled=True)]
    all_to_all x1 -> x0, starting transfers between devices: 3.99 us -> none  [local(): table = lax.all_to_all(send, 'gx', 0, 0, tiled=True)]
    all_to_all x1, waiting for transfers between devices: 3.68 us -> 0.01 us  [local(): got = lax.all_to_all(send, 'gx', 0, 0, tiled=True)]
    ppermute x6, waiting for transfers between devices: 8.84 us -> 6.68 us  [chip_below(): lax.ppermute(value, 'gy', [(j, (j + 2 * step) % GY) for j in range(GY)])]
    ppermute x2 -> x3, starting transfers between devices: 3.89 us -> 5.63 us  [other_core(): return lax.ppermute(value, 'gy', [(j, j ^ 1) for j in range(GY)])]
  transfers between devices with their start and end apart: 17 -> 17, of which waited for: 8 -> 7; matrix products, arithmetic and copies ran while one was open for 0% -> 0% of each run, Pallas kernels for 8% -> 3%
where the time goes in v3:
time: 86.3 us; the launch traced here: 85.8 us
  starting transfers between devices  37.6 us (44%)
  blocking collectives  21.2 us (25%)
  waiting for transfers between devices  13.9 us (16%)
  Pallas kernels  12.1 us (14%)
    ppermute x6, starting transfers between devices, shifted(): return lax.ppermute(value, 'gx', [(k, (k + step) % GX) for k in range(GX)])  14.6 us
    pallas_call x6, Pallas kernels, run(): pl.pallas_call(kernel, out_shape=out_shape, in_specs=[spec(k) for k in ra...  12.1 us
    all_to_all x1, blocking collectives, local(): return lax.all_to_all(out, 'gy', 0, 0, tiled=True)  11.2 us
    all_to_all x1, blocking collectives, local(): table = lax.all_to_all(send, 'gx', 0, 0, tiled=True)  9.97 us
    all_to_all x1, starting transfers between devices, local(): cells = lax.all_to_all(right_side, 'gy', 0, 0, tiled=True)  6.95 us
    ppermute x6, waiting for transfers between devices, chip_below(): lax.ppermute(value, 'gy', [(j, (j + 2 * step) % GY) for j in range(GY)])  6.68 us
    ppermute x6, waiting for transfers between devices, shifted(): return lax.ppermute(value, 'gx', [(k, (k + step) % GX) for k in range(GX)])  5.91 us
    ppermute x6, starting transfers between devices, chip_below(): lax.ppermute(value, 'gy', [(j, (j + 2 * step) % GY) for j in range(GY)])  5.89 us
  transfers between devices with their start and end apart: 17, of which 7 were waited for; matrix products, arithmetic and copies ran while one was open for 0% of the time, Pallas kernels for 3%

profile of v3, /device:TPU:1, one launch (start us, length us, event | category | flops | bytes accessed | tf_op | source)
XLA Modules:
  0.0 85.8 jit_solution(11727903087460367279)
XLA Ops:
  0.0 0.0 copy-start.1
  0.0 6.9 %all-to-all-start = ((f32[8,4,8,256]{3,2,1,0:T(8,128)}), f32[8,4,8,256]{3,2,1,0:T(8,128)S(1)}, u32[]{:S(2)}, u32[]{:S(2)}) async-start(f32[8,4,8,256]{3,2,1,0:T(8,128)} %param.6), calls=%async_computation | async-start | bytes 524288 | tf_op jit(solution)/shard_map/all_to_all | solution.py:406
  6.9 0.0 copy-done.1
  7.0 1.4 %collective-permute-start.4 = (f32[16,2048]{1,0:T(8,128)S(1)}, f32[16,2048]{1,0:T(8,128)S(1)}, u32[]{:S(2)}, u32[]{:S(2)}) collective-permute-start(f32[16,2048]{1,0:T(8,128)S(1)} %copy-done.1), channel_id=1, source_target_pairs={{0,2},{1,3},{2,4},{3,5},{4,6},{5,7},{6,0},{7,1},{8,10},{9,11},{10,... | collective-permute-start | bytes 393224 | tf_op jit(solution)/shard_map/ppermute | solution.py:396
  8.3 1.3 %collective-permute-start.5 = (f32[16,2048]{1,0:T(8,128)S(1)}, f32[16,2048]{1,0:T(8,128)S(1)}, u32[]{:S(2)}, u32[]{:S(2)}) collective-permute-start(f32[16,2048]{1,0:T(8,128)S(1)} %copy-done.1), channel_id=1, source_target_pairs={{0,6},{1,7},{2,0},{3,1},{4,2},{5,3},{6,4},{7,5},{8,14},{9,15},{10,... | collective-permute-start | bytes 393224 | tf_op jit(solution)/shard_map/ppermute | solution.py:396
  9.6 0.9 %shard_map.65.mine_ref = f32[5,8,256]{2,1,0:T(8,128)S(1)} custom-call(s32[4,8,256]{2,1,0:T(8,128)} %ids_ref.1, f32[2,2,64]{2,1,0:T(2,128)} %diag_ref.1, f32[6,2,2,64]{3,2,1,0:T(2,128)} %links_ref.1, s32[2,2,64]{2,1,0:T(2,128)} %coarse_ids_ref.1), custom_call_target="tpu_custom_call" | custom-call | flops 100000000 | bytes 1048576 | tf_op jit(solution)/shard_map/pallas_call | solution.py:375
  10.5 5.0 %collective-permute-start.3 = (f32[4,8,256]{2,1,0:T(8,128)S(1)}, f32[4,8,256]{2,1,0:T(8,128)S(1)}, u32[]{:S(2)}, u32[]{:S(2)}) collective-permute-start(f32[4,8,256]{2,1,0:T(8,128)S(1)} %slice.9), channel_id=1, source_target_pairs={{0,120},{8,0},{16,8},{24,16},{32,24},{40,32},{48,40},{56,48},{64,5... | collective-permute-start | bytes 98312 | tf_op jit(solution)/shard_map/ppermute | solution.py:389
  15.5 0.0 collective-permute-start.2
  15.5 0.0 all-to-all-done.to_ref
  15.5 4.8 %collective-permute-start.1 = (f32[8,4,8,256]{3,2,1,0:T(8,128)S(1)}, f32[8,4,8,256]{3,2,1,0:T(8,128)S(1)}, u32[]{:S(2)}, u32[]{:S(2)}) collective-permute-start(f32[8,4,8,256]{3,2,1,0:T(8,128)S(1)} %all-to-all-done.to_ref), channel_id=1, source_target_pairs={{0,120},{8,0},{16,8},{24,16},{32,24},{40,32},{48,40},{56,48},{64,5... | collective-permute-start | bytes 786440 | tf_op jit(solution)/shard_map/ppermute | solution.py:389
  20.3 0.0 collective-permute-done.3.high_ref
  20.3 0.0 collective-permute-start
  20.3 1.3 %collective-permute-done.2.low_ref = f32[4,8,256]{2,1,0:T(8,128)S(1)} collective-permute-done((f32[4,8,256]{2,1,0:T(8,128)S(1)}, f32[4,8,256]{2,1,0:T(8,128)S(1)}, u32[]{:S(2)}, u32[]{:S(2)}) %collective-permute-start.2) | collective-permute-done | bytes 32800 | tf_op jit(solution)/shard_map/ppermute | solution.py:389
  21.6 0.0 collective-permute-done.4
  21.6 0.0 collective-permute-done.5
  21.7 1.4 %collective-permute-start.8 = (f32[13,8,256]{2,1,0:T(8,128)S(1)}, f32[13,8,256]{2,1,0:T(8,128)S(1)}, u32[]{:S(2)}, u32[]{:S(2)}) collective-permute-start(f32[13,8,256]{2,1,0:T(8,128)S(1)} %shard_map.66), channel_id=1, source_target_pairs={{0,6},{1,7},{2,0},{3,1},{4,2},{5,3},{6,4},{7,5},{8,14},{9,15},{10,... | collective-permute-start | bytes 319496 | tf_op jit(solution)/shard_map/ppermute | solution.py:396
  23.1 0.6 collective-permute-start.7
  23.7 0.6 collective-permute-start.6
  24.3 0.1 pad_add_fusion.where_ref
  24.3 1.0 %collective-permute-done.8 = f32[13,8,256]{2,1,0:T(8,128)S(1)} collective-permute-done((f32[13,8,256]{2,1,0:T(8,128)S(1)}, f32[13,8,256]{2,1,0:T(8,128)S(1)}, u32[]{:S(2)}, u32[]{:S(2)}) %collective-permute-start.8) | collective-permute-done | bytes 106528 | tf_op jit(solution)/shard_map/ppermute | solution.py:396
  25.3 3.2 %collective-permute-done.7 = f32[13,8,256]{2,1,0:T(8,128)S(1)} collective-permute-done((f32[13,8,256]{2,1,0:T(8,128)S(1)}, f32[13,8,256]{2,1,0:T(8,128)S(1)}, u32[]{:S(2)}, u32[]{:S(2)}) %collective-permute-start.7) | collective-permute-done | bytes 106528 | tf_op jit(solution)/shard_map/ppermute | solution.py:396
  28.5 1.1 %collective-permute-done.6 = f32[13,8,256]{2,1,0:T(8,128)S(1)} collective-permute-done((f32[13,8,256]{2,1,0:T(8,128)S(1)}, f32[13,8,256]{2,1,0:T(8,128)S(1)}, u32[]{:S(2)}, u32[]{:S(2)}) %collective-permute-start.6) | collective-permute-done | bytes 106528 | tf_op jit(solution)/shard_map/ppermute | solution.py:396
  29.6 3.6 %collective-permute-start.9 = (f32[4,13,8,256]{3,2,1,0:T(8,128)S(1)}, f32[4,13,8,256]{3,2,1,0:T(8,128)S(1)}, u32[]{:S(2)}, u32[]{:S(2)}) collective-permute-start(f32[4,13,8,256]{3,2,1,0:T(8,128)S(1)} %pad_maximum_fusion.1.near_ref), channel_id=1, source_target_pairs={{0,1},{1,0},{2,3},{3,2},{4,5},{5,4},{6,7},{7,6},{8,9},{9,8},{10,11... | collective-permute-start | bytes 1277960 | tf_op jit(solution)/shard_map/ppermute | solution.py:400
  33.2 0.0 collective-permute-done.1.tr_ref
  33.2 0.0 collective-permute-done.tl_ref
  33.2 1.7 %shard_map.64 = (f32[4,8,8,256]{3,2,1,0:T(8,128)S(1)}, f32[8,8,8,256]{3,2,1,0:T(8,128)S(1)}, f32[8,8,256]{2,1,0:T(8,128)S(1)}, f32[8,8,256]{2,1,0:T(8,128)S(1)}) custom-call(s32[3]{0:T(128)S(1)} %pad_add_fusion.where_ref, f32[8,4,8,256]{3,2,1,0:T(8,128)S(1)} %collective-permute-done.tl_ref, f32[8,4,8,256]{3,2,1,0:T(8,128)S(1)} %all-to-all-done.to_ref, ...), custom_call_target="tpu_custom_call" | custom-call | flops 30000001024 | bytes 1048576 | tf_op jit(solution)/shard_map/pallas_call | solution.py:375
  34.9 0.0 copy-start
  34.9 0.0 collective-permute-done.9.far_ref
  34.9 2.2 %shard_map.67 = f32[16,7,8,128]{3,2,1,0:T(8,128)} custom-call(s32[3]{0:T(128)S(1)} %pad_add_fusion.where_ref, f32[4,8,8,256]{3,2,1,0:T(8,128)S(1)} %get-tuple-element.20.smooth_ref, f32[4,13,8,256]{3,2,1,0:T(8,128)S(1)} %pad_maximum_fusion.1.near_ref, f32[4,13,8,256]{3,2,1,0:T(8,128)S(1)} %collective-permute-done.9.far_ref), custom_call_target="tpu_custom_call" | custom-call | flops 2000000000 | bytes 1048576 | tf_op jit(solution)/shard_map/pallas_call | solution.py:375
  37.2 0.0 copy-done
  37.2 0.6 collective-permute-start.13
  37.8 4.6 %all-to-all-start.1 = ((f32[16,7,8,128]{3,2,1,0:T(8,128)}), f32[16,7,8,128]{3,2,1,0:T(8,128)S(1)}, u32[]{:S(2)}, u32[]{:S(2)}) async-start(f32[16,7,8,128]{3,2,1,0:T(8,128)} %shard_map.67), calls=%async_computation.1 | async-start | bytes 917504 | tf_op jit(solution)/shard_map/all_to_all | solution.py:457
  42.3 1.4 %collective-permute-done.13 = f32[16,2048]{1,0:T(8,128)S(1)} collective-permute-done((f32[16,2048]{1,0:T(8,128)S(1)}, f32[16,2048]{1,0:T(8,128)S(1)}, u32[]{:S(2)}, u32[]{:S(2)}) %collective-permute-start.13) | collective-permute-done | bytes 131104 | tf_op jit(solution)/shard_map/ppermute | solution.py:396
  43.8 0.9 %collective-permute-start.14 = (f32[4,16,2048]{2,1,0:T(8,128)S(1)}, f32[4,16,2048]{2,1,0:T(8,128)S(1)}, u32[]{:S(2)}, u32[]{:S(2)}) collective-permute-start(f32[4,16,2048]{2,1,0:T(8,128)S(1)} %pad_maximum_fusion.near_ref), channel_id=1, source_target_pairs={{0,1},{1,0},{2,3},{3,2},{4,5},{5,4},{6,7},{7,6},{8,9},{9,8},{10,11... | collective-permute-start | bytes 1572872 | tf_op jit(solution)/shard_map/ppermute | solution.py:400
  44.7 0.0 collective-permute-start.10
  44.7 4.8 %collective-permute-start.11 = (f32[8,8,256]{2,1,0:T(8,128)S(1)}, f32[8,8,256]{2,1,0:T(8,128)S(1)}, u32[]{:S(2)}, u32[]{:S(2)}) collective-permute-start(f32[8,8,256]{2,1,0:T(8,128)S(1)} %get-tuple-element.24), channel_id=1, source_target_pairs={{0,120},{8,0},{16,8},{24,16},{32,24},{40,32},{48,40},{56,48},{64,5... | collective-permute-start | bytes 196616 | tf_op jit(solution)/shard_map/ppermute | solution.py:389
  49.5 4.6 %collective-permute-done.10.ul_ref = f32[8,8,256]{2,1,0:T(8,128)S(1)} collective-permute-done((f32[8,8,256]{2,1,0:T(8,128)S(1)}, f32[8,8,256]{2,1,0:T(8,128)S(1)}, u32[]{:S(2)}, u32[]{:S(2)}) %collective-permute-start.10) | collective-permute-done | bytes 65568 | tf_op jit(solution)/shard_map/ppermute | solution.py:389
  54.1 0.0 collective-permute-done.11.ur_ref
  54.1 0.0 all-to-all-done.1.got_ref
  54.1 1.2 %collective-permute-start.12 = (f32[16,5,8,128]{3,2,1,0:T(8,128)S(1)}, f32[16,5,8,128]{3,2,1,0:T(8,128)S(1)}, u32[]{:S(2)}, u32[]{:S(2)}) collective-permute-start(f32[16,5,8,128]{3,2,1,0:T(8,128)S(1)} %slice.8), channel_id=1, source_target_pairs={{0,1},{1,0},{2,3},{3,2},{4,5},{5,4},{6,7},{7,6},{8,9},{9,8},{10,11... | collective-permute-start | bytes 983048 | tf_op jit(solution)/shard_map/ppermute | solution.py:400
  55.3 0.0 collective-permute-done.14.far_ref
  55.3 1.3 %collective-permute-done.12.other_ref = f32[16,5,8,128]{3,2,1,0:T(8,128)S(1)} collective-permute-done((f32[16,5,8,128]{3,2,1,0:T(8,128)S(1)}, f32[16,5,8,128]{3,2,1,0:T(8,128)S(1)}, u32[]{:S(2)}, u32[]{:S(2)}) %collective-permute-start.12) | collective-permute-done | bytes 327712 | tf_op jit(solution)/shard_map/ppermute | solution.py:400
  56.6 3.8 %shard_map.68 = (f32[16,8,128]{2,1,0:T(8,128)S(1)}, f32[10,10,8,128]{3,2,1,0:T(8,128)S(1)}, s32[12,8,128]{2,1,0:T(8,128)S(1)}) custom-call(s32[3]{0:T(128)S(1)} %pad_add_fusion.where_ref, f32[16,7,8,128]{3,2,1,0:T(8,128)S(1)} %all-to-all-done.1.got_ref, f32[16,5,8,128]{3,2,1,0:T(8,128)S(1)} %collective-permute-done.12.other_ref, ...), custom_call_target="tpu_custom_call" | custom-call | flops 3000000000 | bytes 1048576 | tf_op jit(solution)/shard_map/pallas_call | solution.py:375
  60.3 10.0 %all_to_all.20.table_ref = f32[16,8,128]{2,1,0:T(8,128)S(1)} all-to-all(f32[16,8,128]{2,1,0:T(8,128)S(1)} %get-tuple-element.29), channel_id=1, replica_groups=mesh['gx'=16,'gy'=8] {'gx'}, dimensions={0} | all-to-all | bytes 131072 | tf_op jit(solution)/shard_map/all_to_all | solution.py:470
  70.3 3.5 %shard_map.69 = f32[8,4,8,256]{3,2,1,0:T(8,128)S(1)} custom-call(s32[3]{0:T(128)S(1)} %pad_add_fusion.where_ref, f32[16,8,128]{2,1,0:T(8,128)S(1)} %all_to_all.20.table_ref, f32[10,10,8,128]{3,2,1,0:T(8,128)S(1)} %get-tuple-element.30.window_ref, s32[12,8,128]{2,1,0:T(8,128)S(1)} %get-tuple-element.31.ids_ref, ...), custom_call_target="tpu_custom_call" | custom-call | flops 4000000000 | bytes 1048576 | tf_op jit(solution)/shard_map/pallas_call | solution.py:375
  73.9 11.2 %all_to_all.21 = f32[8,4,8,256]{3,2,1,0:T(8,128)S(1)} all-to-all(f32[8,4,8,256]{3,2,1,0:T(8,128)S(1)} %shard_map.69), channel_id=1, replica_groups=mesh['gx'=16,'gy'=8] {'gy'}, dimensions={0} | all-to-all | bytes 524288 | tf_op jit(solution)/shard_map/all_to_all | solution.py:485
  85.1 0.7 copy.8
  (5 shorter events, 0.1 us)
Async XLA Ops:
  0.0 7.0 %copy-start.1 = (f32[16,2048]{1,0:T(8,128)S(1)}, f32[16,2048]{1,0:T(8,128)}, u32[]{:S(2)}) copy-start(f32[16,2048]{1,0:T(8,128)} %param.11) | copy-start | bytes 393220
  0.0 15.5 %all-to-all-start = ((f32[8,4,8,256]{3,2,1,0:T(8,128)}), f32[8,4,8,256]{3,2,1,0:T(8,128)S(1)}, u32[]{:S(2)}, u32[]{:S(2)}) async-start(f32[8,4,8,256]{3,2,1,0:T(8,128)} %param.6), calls=%async_computation | async-start | bytes 524288 | tf_op jit(solution)/shard_map/all_to_all | solution.py:406
  7.0 14.7 %collective-permute-start.4 = (f32[16,2048]{1,0:T(8,128)S(1)}, f32[16,2048]{1,0:T(8,128)S(1)}, u32[]{:S(2)}, u32[]{:S(2)}) collective-permute-start(f32[16,2048]{1,0:T(8,128)S(1)} %copy-done.1), channel_id=1, source_target_pairs={{0,2},{1,3},{2,4},{3,5},{4,6},{5,7},{6,0},{7,1},{8,10},{9,11},{10,... | collective-permute-start | bytes 393224 | tf_op jit(solution)/shard_map/ppermute | solution.py:396
  8.3 13.3 %collective-permute-start.5 = (f32[16,2048]{1,0:T(8,128)S(1)}, f32[16,2048]{1,0:T(8,128)S(1)}, u32[]{:S(2)}, u32[]{:S(2)}) collective-permute-start(f32[16,2048]{1,0:T(8,128)S(1)} %copy-done.1), channel_id=1, source_target_pairs={{0,6},{1,7},{2,0},{3,1},{4,2},{5,3},{6,4},{7,5},{8,14},{9,15},{10,... | collective-permute-start | bytes 393224 | tf_op jit(solution)/shard_map/ppermute | solution.py:396
  10.5 9.8 %collective-permute-start.3 = (f32[4,8,256]{2,1,0:T(8,128)S(1)}, f32[4,8,256]{2,1,0:T(8,128)S(1)}, u32[]{:S(2)}, u32[]{:S(2)}) collective-permute-start(f32[4,8,256]{2,1,0:T(8,128)S(1)} %slice.9), channel_id=1, source_target_pairs={{0,120},{8,0},{16,8},{24,16},{32,24},{40,32},{48,40},{56,48},{64,5... | collective-permute-start | bytes 98312 | tf_op jit(solution)/shard_map/ppermute | solution.py:389
  15.5 6.1 %collective-permute-start.2 = (f32[4,8,256]{2,1,0:T(8,128)S(1)}, f32[4,8,256]{2,1,0:T(8,128)S(1)}, u32[]{:S(2)}, u32[]{:S(2)}) collective-permute-start(f32[4,8,256]{2,1,0:T(8,128)S(1)} %slice.9), channel_id=1, source_target_pairs={{0,8},{8,16},{16,24},{24,32},{32,40},{40,48},{48,56},{56,64},{64,7... | collective-permute-start | bytes 98312 | tf_op jit(solution)/shard_map/ppermute | solution.py:389
  15.5 17.7 %collective-permute-start.1 = (f32[8,4,8,256]{3,2,1,0:T(8,128)S(1)}, f32[8,4,8,256]{3,2,1,0:T(8,128)S(1)}, u32[]{:S(2)}, u32[]{:S(2)}) collective-permute-start(f32[8,4,8,256]{3,2,1,0:T(8,128)S(1)} %all-to-all-done.to_ref), channel_id=1, source_target_pairs={{0,120},{8,0},{16,8},{24,16},{32,24},{40,32},{48,40},{56,48},{64,5... | collective-permute-start | bytes 786440 | tf_op jit(solution)/shard_map/ppermute | solution.py:389
  20.3 12.9 %collective-permute-start = (f32[8,4,8,256]{3,2,1,0:T(8,128)S(1)}, f32[8,4,8,256]{3,2,1,0:T(8,128)S(1)}, u32[]{:S(2)}, u32[]{:S(2)}) collective-permute-start(f32[8,4,8,256]{3,2,1,0:T(8,128)S(1)} %all-to-all-done.to_ref), channel_id=1, source_target_pairs={{0,8},{8,16},{16,24},{24,32},{32,40},{40,48},{48,56},{56,64},{64,7... | collective-permute-start | bytes 786440 | tf_op jit(solution)/shard_map/ppermute | solution.py:389
  21.7 3.6 %collective-permute-start.8 = (f32[13,8,256]{2,1,0:T(8,128)S(1)}, f32[13,8,256]{2,1,0:T(8,128)S(1)}, u32[]{:S(2)}, u32[]{:S(2)}) collective-permute-start(f32[13,8,256]{2,1,0:T(8,128)S(1)} %shard_map.66), channel_id=1, source_target_pairs={{0,6},{1,7},{2,0},{3,1},{4,2},{5,3},{6,4},{7,5},{8,14},{9,15},{10,... | collective-permute-start | bytes 319496 | tf_op jit(solution)/shard_map/ppermute | solution.py:396
  23.1 5.4 %collective-permute-start.7 = (f32[13,8,256]{2,1,0:T(8,128)S(1)}, f32[13,8,256]{2,1,0:T(8,128)S(1)}, u32[]{:S(2)}, u32[]{:S(2)}) collective-permute-start(f32[13,8,256]{2,1,0:T(8,128)S(1)} %shard_map.66), channel_id=1, source_target_pairs={{0,4},{1,5},{2,6},{3,7},{4,0},{5,1},{6,2},{7,3},{8,12},{9,13},{10,... | collective-permute-start | bytes 319496 | tf_op jit(solution)/shard_map/ppermute | solution.py:396
  23.7 5.9 %collective-permute-start.6 = (f32[13,8,256]{2,1,0:T(8,128)S(1)}, f32[13,8,256]{2,1,0:T(8,128)S(1)}, u32[]{:S(2)}, u32[]{:S(2)}) collective-permute-start(f32[13,8,256]{2,1,0:T(8,128)S(1)} %shard_map.66), channel_id=1, source_target_pairs={{0,2},{1,3},{2,4},{3,5},{4,6},{5,7},{6,0},{7,1},{8,10},{9,11},{10,... | collective-permute-start | bytes 319496 | tf_op jit(solution)/shard_map/ppermute | solution.py:396
  29.6 5.3 %collective-permute-start.9 = (f32[4,13,8,256]{3,2,1,0:T(8,128)S(1)}, f32[4,13,8,256]{3,2,1,0:T(8,128)S(1)}, u32[]{:S(2)}, u32[]{:S(2)}) collective-permute-start(f32[4,13,8,256]{3,2,1,0:T(8,128)S(1)} %pad_maximum_fusion.1.near_ref), channel_id=1, source_target_pairs={{0,1},{1,0},{2,3},{3,2},{4,5},{5,4},{6,7},{7,6},{8,9},{9,8},{10,11... | collective-permute-start | bytes 1277960 | tf_op jit(solution)/shard_map/ppermute | solution.py:400
  34.9 2.2 %copy-start = (f32[8,8,8,256]{3,2,1,0:T(8,128)}, f32[8,8,8,256]{3,2,1,0:T(8,128)S(1)}, u32[]{:S(2)}) copy-start(f32[8,8,8,256]{3,2,1,0:T(8,128)S(1)} %get-tuple-element.32.u_hbm) | copy-start | bytes 1572868
  37.2 6.6 %collective-permute-start.13 = (f32[16,2048]{1,0:T(8,128)S(1)}, f32[16,2048]{1,0:T(8,128)S(1)}, u32[]{:S(2)}, u32[]{:S(2)}) collective-permute-start(f32[16,2048]{1,0:T(8,128)S(1)} %copy-done.1), channel_id=1, source_target_pairs={{0,4},{1,5},{2,6},{3,7},{4,0},{5,1},{6,2},{7,3},{8,12},{9,13},{10,... | collective-permute-start | bytes 393224 | tf_op jit(solution)/shard_map/ppermute | solution.py:396
  37.8 16.4 %all-to-all-start.1 = ((f32[16,7,8,128]{3,2,1,0:T(8,128)}), f32[16,7,8,128]{3,2,1,0:T(8,128)S(1)}, u32[]{:S(2)}, u32[]{:S(2)}) async-start(f32[16,7,8,128]{3,2,1,0:T(8,128)} %shard_map.67), calls=%async_computation.1 | async-start | bytes 917504 | tf_op jit(solution)/shard_map/all_to_all | solution.py:457
  43.8 11.5 %collective-permute-start.14 = (f32[4,16,2048]{2,1,0:T(8,128)S(1)}, f32[4,16,2048]{2,1,0:T(8,128)S(1)}, u32[]{:S(2)}, u32[]{:S(2)}) collective-permute-start(f32[4,16,2048]{2,1,0:T(8,128)S(1)} %pad_maximum_fusion.near_ref), channel_id=1, source_target_pairs={{0,1},{1,0},{2,3},{3,2},{4,5},{5,4},{6,7},{7,6},{8,9},{9,8},{10,11... | collective-permute-start | bytes 1572872 | tf_op jit(solution)/shard_map/ppermute | solution.py:400
  44.7 9.4 %collective-permute-start.10 = (f32[8,8,256]{2,1,0:T(8,128)S(1)}, f32[8,8,256]{2,1,0:T(8,128)S(1)}, u32[]{:S(2)}, u32[]{:S(2)}) collective-permute-start(f32[8,8,256]{2,1,0:T(8,128)S(1)} %get-tuple-element.23), channel_id=1, source_target_pairs={{0,8},{8,16},{16,24},{24,32},{32,40},{40,48},{48,56},{56,64},{64,7... | collective-permute-start | bytes 196616 | tf_op jit(solution)/shard_map/ppermute | solution.py:389
  44.7 9.4 %collective-permute-start.11 = (f32[8,8,256]{2,1,0:T(8,128)S(1)}, f32[8,8,256]{2,1,0:T(8,128)S(1)}, u32[]{:S(2)}, u32[]{:S(2)}) collective-permute-start(f32[8,8,256]{2,1,0:T(8,128)S(1)} %get-tuple-element.24), channel_id=1, source_target_pairs={{0,120},{8,0},{16,8},{24,16},{32,24},{40,32},{48,40},{56,48},{64,5... | collective-permute-start | bytes 196616 | tf_op jit(solution)/shard_map/ppermute | solution.py:389
  54.1 2.4 %collective-permute-start.12 = (f32[16,5,8,128]{3,2,1,0:T(8,128)S(1)}, f32[16,5,8,128]{3,2,1,0:T(8,128)S(1)}, u32[]{:S(2)}, u32[]{:S(2)}) collective-permute-start(f32[16,5,8,128]{3,2,1,0:T(8,128)S(1)} %slice.8), channel_id=1, source_target_pairs={{0,1},{1,0},{2,3},{3,2},{4,5},{5,4},{6,7},{7,6},{8,9},{9,8},{10,11... | collective-permute-start | bytes 983048 | tf_op jit(solution)/shard_map/ppermute | solution.py:400

commit v4 on v3

--- a/solution.py
+++ b/solution.py
@@ -28,6 +28,7 @@
 LANES = 128
 NC2 = 2048
 HI = NC2 // LANES
+HALF = LANES // 2
 
 
 def beside_in_row(row):
@@ -129,15 +130,6 @@
     out_ref[CX] = jnp.concatenate(rows, axis=0)
 
 
-SHARED = 3 * CX + 1
-
-
-def share_kernel(mine_ref, low_ref, high_ref, out_ref):
-    out_ref[0 : CX + 1] = mine_ref[...]
-    out_ref[CX + 1 : 2 * CX + 1] = low_ref[...]
-    out_ref[2 * CX + 1 :] = high_ref[...]
-
-
 def shared_tile(near_ref, far_ref, chip, core, j, tile):
     k = lax.rem(chip + 4 - j // 2, 4)
     return jnp.where(core == j % 2, near_ref[k, tile], far_ref[k, tile])
@@ -174,16 +166,18 @@
         dst[k] = row if plus is None else row + plus[k - EDGE + U_EDGE]
 
 
-def down_kernel(where_ref, tl_ref, to_ref, tr_ref, smooth_ref, u_ref, up_ref, down_ref, a_ref, b_ref):
+def down_kernel(where_ref, t1_ref, to_ref, t2_ref, far_ref, smooth_ref, u_ref, a_ref, b_ref):
+    del far_ref
     place = where_ref[0]
+    odd = place & 1
     keep_low = jnp.where(place > 0, 1.0, 0.0).astype(F32)
     keep_high = jnp.where(place < GX - 1, 1.0, 0.0).astype(F32)
     gates = keep_low, keep_high
     first, second, third = FINE_NODES
     for x in range(CX):
-        a_ref[x] = tl_ref[:, x] * keep_low
+        a_ref[x] = jnp.where(odd == 1, t1_ref[:, x], t2_ref[:, x]) * keep_low
         a_ref[EDGE + x] = to_ref[:, x]
-        a_ref[EDGE + CX + x] = tr_ref[:, x] * keep_high
+        a_ref[EDGE + CX + x] = jnp.where(odd == 1, t2_ref[:, x], t1_ref[:, x]) * keep_high
 
     relax_rows(a_ref, b_ref, 3, first, *gates)
     shift = EDGE - U_EDGE
@@ -192,22 +186,25 @@
     relax_rows(b_ref, a_ref, 2, second, *gates)
     for k in range(CX + 2 * U_EDGE):
         u_ref[k] = u_ref[k] + (1.0 / third) * a_ref[k + shift]
-    up_ref[...] = u_ref[U_EDGE + 1]
-    down_ref[...] = u_ref[U_EDGE + 2]
     relax_rows(a_ref, b_ref, 1, third, *gates)
     for x in range(CX):
         k = EDGE + x
         smooth_ref[x] = relax(b_ref[k - 1], b_ref[k], b_ref[k + 1], 1.0 / PROLONG)
 
 
-def pool_kernel(where_ref, smooth_ref, near_ref, far_ref, send_ref, tile_ref):
+def pool_kernel(where_ref, smooth_ref, u_ref, near_ref, far_ref, send_ref, first_ref, second_ref, tile_ref):
     chip, core = where_ref[1], where_ref[2]
     shape = (YT, CY, CZ)
     home = lax.broadcasted_iota(jnp.int32, shape, 2) // 4
     codes = []
     for x in range(CX):
         ids = shared_ids(near_ref, far_ref, chip, core, x)
+        first_ref[:, x] = ids.astype(F32)
+        second_ref[:, x] = ids.astype(F32)
         codes.append((ids >> 6) * 3 + ((ids & 63) - home) + 1)
+    odd = where_ref[0] & 1
+    first_ref[:, CX] = u_ref[U_EDGE + 1 + odd]
+    second_ref[:, CX] = u_ref[U_EDGE + 2 - odd]
     pooled = []
     for half in range(2):
         parts = []
@@ -236,8 +233,10 @@
 
 
 def solve_kernel(
-    where_ref, got_ref, other_ref, near_ref, far_ref, send_ref, window_ref, ids_ref, full_ref, total_ref
+    where_ref, got_ref, other_ref, near_ref, far_ref, arrived_ref, send_ref, window_ref, ids_ref, full_ref, total_ref
 ):
+    del arrived_ref
+
     place, chip, core = where_ref[0], where_ref[1], where_ref[2]
 
     def grid(k):
@@ -264,16 +263,19 @@
     for w in range(WINDOW + 2):
         ids_ref[w] = full_ref[10, jnp.clip(2 * place + w - 5, 0, NAX - 1)].astype(jnp.int32)
     ids = ids.astype(jnp.int32)
-    high_of = ids >> 7
-    low_of = ids & (LANES - 1)
-    high_iota = lax.broadcasted_iota(jnp.int32, (HI, LANES), 0)
-    low_iota = lax.broadcasted_iota(jnp.int32, (LANES, LANES), 0)
-    counted = jnp.zeros((3 * HI, LANES), F32)
+    high_of = ids >> 6
+    low_of = ids & (HALF - 1)
+    high_iota = lax.broadcasted_iota(jnp.int32, (NC2 // HALF, LANES), 0)
+    low_iota = lax.broadcasted_iota(jnp.int32, (HALF, LANES), 0)
+    pieces = [piece.astype(F32) for piece in split3(residual)[:2]]
+    counted = jnp.zeros((2 * NC2 // HALF, HALF), F32)
     for x in range(NAX):
         left, right = [], []
         for k in range(YT):
-            picked = jnp.where(high_of[x, k : k + 1] == high_iota, residual[x, k : k + 1], 0.0)
-            left.append(jnp.concatenate(split3(picked), axis=0))
+            hit = high_of[x, k : k + 1] == high_iota
+            left.append(
+                jnp.concatenate([jnp.where(hit, piece[x, k : k + 1], 0.0).astype(BF16) for piece in pieces], axis=0)
+            )
             right.append(jnp.where(low_of[x, k : k + 1] == low_iota, 1.0, 0.0).astype(BF16))
         counted = counted + lax.dot_general(
             jnp.concatenate(left, axis=1),
@@ -281,18 +283,19 @@
             (((1,), (1,)), ((), ())),
             preferred_element_type=F32,
         )
-    target = counted[:HI] + counted[HI : 2 * HI] + counted[2 * HI :]
+    rows = NC2 // HALF
+    target = sum(counted[k * rows : (k + 1) * rows] for k in range(2))
+    target = [jnp.concatenate([target[2 * h : 2 * h + 1], target[2 * h + 1 : 2 * h + 2]], axis=1) for h in range(HI)]
     for ref, side in ((near_ref, core), (far_ref, 1 - core)):
         for k in range(4):
             total = jnp.zeros((HI, LANES), F32)
             for h in range(HI):
-                total = total + ref[k, :, h * LANES : (h + 1) * LANES] * target[h : h + 1]
+                total = total + ref[k, :, h * LANES : (h + 1) * LANES] * target[h]
             at = lax.rem(chip + 4 - k, 4) * 2 + side
             total_ref[pl.ds(pl.multiple_of(at * HI, HI), HI)] = total
     row = jnp.sum(total_ref[...].T, axis=0, keepdims=True)
-    tile = jnp.broadcast_to(row, (8, LANES))
     for i in range(GX):
-        send_ref[i] = tile
+        send_ref[i] = row
 
 
 def lane_take(table, index):
@@ -306,9 +309,9 @@
     ids_ref,
     near_ref,
     far_ref,
+    first_ref,
+    second_ref,
     u_hbm,
-    ul_ref,
-    ur_ref,
     out_ref,
     post_ref,
     a_ref,
@@ -329,7 +332,7 @@
         low_of = unknown & (LANES - 1)
         value = jnp.zeros((YT, LANES), F32)
         for k in range(HI):
-            table = jnp.broadcast_to(table_ref[k, 0:1], (YT, LANES))
+            table = jnp.broadcast_to(table_ref[k], (YT, LANES))
             value = jnp.where(high_of == k, lane_take(table, low_of), value)
         picked.append(value)
     coarsest = jnp.stack(picked[1:-1], axis=0)
@@ -341,9 +344,15 @@
         row = post[k + 2]
         post_ref[k] = row if gate is None else row * gate
 
-    for slab, first_tile in ((0, CX + 1), (1, 0), (2, 2 * CX + 1)):
+    odd = place & 1
+
+    def halo(slab, x):
+        first, second = first_ref[:, x], second_ref[:, x]
+        return jnp.where(odd == 1, first, second) if slab == 0 else jnp.where(odd == 1, second, first)
+
+    for slab in range(3):
         for x in range(CX):
-            ids = shared_ids(near_ref, far_ref, chip, core, first_tile + x)
+            ids = shared_ids(near_ref, far_ref, chip, core, x) if slab == 1 else halo(slab, x).astype(jnp.int32)
             for k in range(YT):
                 table0 = jnp.broadcast_to(post_ref[2 * slab, k : k + 1], (CY, LANES))
                 table1 = jnp.broadcast_to(post_ref[2 * slab + 1, k : k + 1], (CY, LANES))
@@ -358,8 +367,8 @@
     first, second, third = FINE_NODES
     u_copy.wait()
     relax_rows(a_ref, b_ref, 2, 1.0 / PROLONG, *gates, plus=u_ref)
-    for k, u, gate in ((EDGE - 3, ul_ref, keep_low), (EDGE + CX + 2, ur_ref, keep_high)):
-        b_ref[k] = (relax(a_ref[k - 1], a_ref[k], a_ref[k + 1], 1.0 / PROLONG) + u[...]) * gate
+    for k, slab, gate in ((EDGE - 3, 0, keep_low), (EDGE + CX + 2, 2, keep_high)):
+        b_ref[k] = (relax(a_ref[k - 1], a_ref[k], a_ref[k + 1], 1.0 / PROLONG) + halo(slab, CX)) * gate
     relax_rows(b_ref, a_ref, 2, first, *gates)
     relax_rows(a_ref, b_ref, 1, second, *gates)
     for x in range(CX):
@@ -385,8 +394,11 @@
     return run
 
 
-def shifted(value, step):
-    return lax.ppermute(value, "gx", [(k, (k + step) % GX) for k in range(GX)])
+def beside(first, second):
+    one = [(k, k ^ 1) for k in range(GX)]
+    two = [(k, ((k + 1) ^ 1) - 1) for k in range(GX)]
+    two = [(k, other % GX) for k, other in two]
+    return lax.ppermute(first, "gx", one), lax.ppermute(second, "gx", two)
 
 
 FINE_FLOPS = 3 * 10**10
@@ -394,6 +406,10 @@
 
 def chip_below(value, step):
     return lax.ppermute(value, "gy", [(j, (j + 2 * step) % GY) for j in range(GY)])
+
+
+def arrived_kernel(low_ref, high_ref, out_ref):
+    out_ref[...] = low_ref[0, CX, :, :LANES] + high_ref[0, CX, :, :LANES]
 
 
 def other_core(value):
@@ -404,7 +420,6 @@
     row = lax.axis_index("gy")
     place = jnp.stack([lax.axis_index("gx"), row // 2, row % 2]).astype(jnp.int32)
     cells = lax.all_to_all(right_side, "gy", 0, 0, tiled=True)
-    low, high = shifted(cells, 1), shifted(cells, -1)
 
     arguments = (fine_ids, coarse_diag, coarse_links, coarse_ids)
     tiles = call(
@@ -421,52 +436,56 @@
         0,
         dict.fromkeys(range(4), pltpu.HBM),
     )(*(pltpu.with_memory_space_constraint(value, pltpu.HBM) for value in arguments))
-    shared = call(share_kernel, pltpu.VMEM((SHARED, CY, CZ), F32), [], 10**8)(
-        tiles, shifted(tiles[:CX], 1), shifted(tiles[:CX], -1)
-    )
-    inverse = [coarsest_inverse, chip_below(coarsest_inverse, 1), None, chip_below(coarsest_inverse, 3)]
-    shared, inverse[1], inverse[3] = lax.optimization_barrier((shared, inverse[1], inverse[3]))
-    near = jnp.stack([shared, *(chip_below(shared, k) for k in range(1, 4))], axis=0)
+    slabs = [tiles, *(chip_below(tiles, k) for k in range(1, 4))]
+    cells, *slabs = lax.optimization_barrier((cells, *slabs))
+    near = jnp.stack(slabs, axis=0)
     far = other_core(near)
 
+    first, second = beside(cells, cells)
+
+    cells, inverse = lax.optimization_barrier((cells, coarsest_inverse))
+    chips = [chip_below(inverse, k) for k in range(1, 4)]
+
     field = (ROWS, YT, CY, CZ)
-    smooth, u, going_up, going_down = call(
+    smooth, u = call(
         down_kernel,
         [
             pltpu.VMEM((CX, YT, CY, CZ), F32),
             pltpu.VMEM((CX + 2 * U_EDGE, YT, CY, CZ), F32),
-            pltpu.VMEM((YT, CY, CZ), F32),
-            pltpu.VMEM((YT, CY, CZ), F32),
         ],
         [pltpu.VMEM(field, F32), pltpu.VMEM(field, F32)],
         FINE_FLOPS,
         1,
-    )(place, low, cells, high)
-    send = call(
+    )(place, first, cells, second, far)
+    send, *going = call(
         pool_kernel,
-        pltpu.VMEM((GX, 2 + FIELDS, YT, LANES), F32),
+        [
+            pltpu.VMEM((GX, 2 + FIELDS, YT, LANES), F32),
+            pltpu.VMEM((YT, CX + 1, CY, CZ), F32),
+            pltpu.VMEM((YT, CX + 1, CY, CZ), F32),
+        ],
         [pltpu.VMEM((GY, CY, CZ), F32)],
         2 * 10**9,
         1,
-    )(place, smooth, near, far)
-    send, inverse[0] = lax.optimization_barrier((send, inverse[0]))
-    inverse[2] = chip_below(inverse[0], 2)
-    inverse_near = jnp.stack(inverse, axis=0)
+    )(place, smooth, u, near, far)
+    send, inverse, *chips = lax.optimization_barrier((send, inverse, *chips))
+    inverse_near = jnp.stack([inverse, *chips], axis=0)
     inverse_far = other_core(inverse_near)
-    u_low, u_high = shifted(going_up, 1), shifted(going_down, -1)
+    first, second = beside(*going)
     got = lax.all_to_all(send, "gx", 0, 0, tiled=True)
-    got, u_low, u_high = lax.optimization_barrier((got, u_low, u_high))
+    arrived = call(arrived_kernel, pltpu.VMEM((CY, LANES), F32), [], 2 * 10**10)(first, second)
+    got, arrived = lax.optimization_barrier((got, arrived))
     send, window, unknowns = call(
         solve_kernel,
         [
-            pltpu.VMEM((GX, 8, LANES), F32),
+            pltpu.VMEM((GX, 1, LANES), F32),
             pltpu.VMEM((10, WINDOW, YT, LANES), F32),
             pltpu.VMEM((WINDOW + 2, YT, LANES), jnp.int32),
         ],
         [pltpu.VMEM((11, NAX, YT, LANES), F32), pltpu.VMEM((LANES, LANES), F32)],
-        3 * 10**9,
+        10**6,
         1,
-    )(place, got, other_core(got[:, 2:]), inverse_near, inverse_far)
+    )(place, got, other_core(got[:, 2:]), inverse_near, inverse_far, arrived)
     table = lax.all_to_all(send, "gx", 0, 0, tiled=True)
     out = call(
         up_kernel,
@@ -480,8 +499,8 @@
         ],
         4 * 10**9,
         1,
-        {6: pltpu.HBM},
-    )(place, table, window, unknowns, near, far, pltpu.with_memory_space_constraint(u, pltpu.HBM), u_low, u_high)
+        {8: pltpu.HBM},
+    )(place, table, window, unknowns, near, far, first, second, pltpu.with_memory_space_constraint(u, pltpu.HBM))
     return lax.all_to_all(out, "gy", 0, 0, tiled=True)
 
 

time: 86.3 us -> 79.8 us (0.925)
  starting transfers between devices: 37.6 us -> 33.6 us
  waiting for transfers between devices: 13.9 us -> 12.4 us
  Pallas kernels: 12.1 us -> 10.8 us
    all_to_all x1, waiting for transfers between devices: 0.01 us -> 6.35 us  [local(): got = lax.all_to_all(send, 'gx', 0, 0, tiled=True)]
    ppermute x6 -> x4, starting transfers between devices: 14.6 us -> 8.54 us  [beside(): return (lax.ppermute(first, 'gx', one), lax.ppermute(second, 'gx', two))]
    ppermute x6 -> x4, waiting for transfers between devices: 5.91 us -> 1.17 us  [beside(): return (lax.ppermute(first, 'gx', one), lax.ppermute(second, 'gx', two))]
    ppermute x3, starting transfers between devices: 5.63 us -> 8.77 us  [other_core(): return lax.ppermute(value, 'gy', [(j, j ^ 1) for j in range(GY)])]
    ppermute x6, waiting for transfers between devices: 6.68 us -> 3.65 us  [chip_below(): lax.ppermute(value, 'gy', [(j, (j + 2 * step) % GY) for j in range(GY)])]
    pallas_call x6, Pallas kernels: 12.1 us -> 10.8 us  [run(): pl.pallas_call(kernel, out_shape=out_shape, in_specs=[spec(k) for k in ra...]
    all_to_all x1, starting transfers between devices: 4.57 us -> 3.57 us  [local(): got = lax.all_to_all(send, 'gx', 0, 0, tiled=True)]
  transfers between devices with their start and end apart: 17 -> 15, of which waited for: 7 -> 7; matrix products, arithmetic and copies ran while one was open for 0% -> 0% of each run, Pallas kernels for 3% -> 6%
where the time goes in v4:
time: 79.8 us; the launch traced here: 79.3 us
  starting transfers between devices  33.6 us (42%)
  blocking collectives  21.6 us (27%)
  waiting for transfers between devices  12.4 us (16%)
  Pallas kernels  10.8 us (14%)
    all_to_all x1, blocking collectives, local(): return lax.all_to_all(out, 'gy', 0, 0, tiled=True)  11.5 us
    pallas_call x6, Pallas kernels, run(): pl.pallas_call(kernel, out_shape=out_shape, in_specs=[spec(k) for k in ra...  10.8 us
    all_to_all x1, blocking collectives, local(): table = lax.all_to_all(send, 'gx', 0, 0, tiled=True)  10 us
    ppermute x3, starting transfers between devices, other_core(): return lax.ppermute(value, 'gy', [(j, j ^ 1) for j in range(GY)])  8.77 us
    ppermute x4, starting transfers between devices, beside(): return (lax.ppermute(first, 'gx', one), lax.ppermute(second, 'gx', two))  8.54 us
    all_to_all x1, starting transfers between devices, local(): cells = lax.all_to_all(right_side, 'gy', 0, 0, tiled=True)  6.81 us
    all_to_all x1, waiting for transfers between devices, local(): got = lax.all_to_all(send, 'gx', 0, 0, tiled=True)  6.35 us
    ppermute x6, starting transfers between devices, chip_below(): lax.ppermute(value, 'gy', [(j, (j + 2 * step) % GY) for j in range(GY)])  5.88 us
  transfers between devices with their start and end apart: 15, of which 7 were waited for; matrix products, arithmetic and copies ran while one was open for 0% of the time, Pallas kernels for 6%

profile of v4, /device:TPU:1, one launch (start us, length us, event | category | flops | bytes accessed | tf_op | source)
XLA Modules:
  0.0 79.3 jit_solution(2384759503564412615)
XLA Ops:
  0.0 6.8 %all-to-all-start = ((f32[8,4,8,256]{3,2,1,0:T(8,128)}), f32[8,4,8,256]{3,2,1,0:T(8,128)S(1)}, u32[]{:S(2)}, u32[]{:S(2)}) async-start(f32[8,4,8,256]{3,2,1,0:T(8,128)} %param.6), calls=%async_computation | async-start | bytes 524288 | tf_op jit(solution)/shard_map/all_to_all | solution.py:422
  6.8 0.9 %shard_map.64 = f32[5,8,256]{2,1,0:T(8,128)S(1)} custom-call(s32[4,8,256]{2,1,0:T(8,128)} %ids_ref.1, f32[2,2,64]{2,1,0:T(2,128)} %diag_ref.1, f32[6,2,2,64]{3,2,1,0:T(2,128)} %links_ref.1, s32[2,2,64]{2,1,0:T(2,128)} %coarse_ids_ref.1), custom_call_target="tpu_custom_call" | custom-call | flops 100000000 | bytes 1048576 | tf_op jit(solution)/shard_map/pallas_call | solution.py:384
  7.7 2.7 %collective-permute-start.2 = (f32[5,8,256]{2,1,0:T(8,128)S(1)}, f32[5,8,256]{2,1,0:T(8,128)S(1)}, u32[]{:S(2)}, u32[]{:S(2)}) collective-permute-start(f32[5,8,256]{2,1,0:T(8,128)S(1)} %shard_map.64), channel_id=1, source_target_pairs={{0,6},{1,7},{2,0},{3,1},{4,2},{5,3},{6,4},{7,5},{8,14},{9,15},{10,... | collective-permute-start | bytes 122888 | tf_op jit(solution)/shard_map/ppermute | solution.py:408
  10.4 0.6 collective-permute-start.1
  10.9 0.6 collective-permute-start
  11.5 1.1 %collective-permute-done.2 = f32[5,8,256]{2,1,0:T(8,128)S(1)} collective-permute-done((f32[5,8,256]{2,1,0:T(8,128)S(1)}, f32[5,8,256]{2,1,0:T(8,128)S(1)}, u32[]{:S(2)}, u32[]{:S(2)}) %collective-permute-start.2) | collective-permute-done | bytes 40992 | tf_op jit(solution)/shard_map/ppermute | solution.py:408
  12.6 2.1 %collective-permute-done.1 = f32[5,8,256]{2,1,0:T(8,128)S(1)} collective-permute-done((f32[5,8,256]{2,1,0:T(8,128)S(1)}, f32[5,8,256]{2,1,0:T(8,128)S(1)}, u32[]{:S(2)}, u32[]{:S(2)}) %collective-permute-start.1) | collective-permute-done | bytes 40992 | tf_op jit(solution)/shard_map/ppermute | solution.py:408
  14.7 0.4 collective-permute-done
  15.2 0.0 all-to-all-done.to_ref
  15.2 4.9 %collective-permute-start.4 = (f32[8,4,8,256]{3,2,1,0:T(8,128)S(1)}, f32[8,4,8,256]{3,2,1,0:T(8,128)S(1)}, u32[]{:S(2)}, u32[]{:S(2)}) collective-permute-start(f32[8,4,8,256]{3,2,1,0:T(8,128)S(1)} %all-to-all-done.to_ref), channel_id=1, source_target_pairs={{0,120},{8,16},{16,8},{24,32},{32,24},{40,48},{48,40},{56,64},{64,... | collective-permute-start | bytes 786440 | tf_op jit(solution)/shard_map/ppermute | solution.py:401
  20.1 0.0 collective-permute-start.3
  20.1 0.0 copy-start.1
  20.1 2.3 %collective-permute-start.5 = (f32[4,5,8,256]{3,2,1,0:T(8,128)S(1)}, f32[4,5,8,256]{3,2,1,0:T(8,128)S(1)}, u32[]{:S(2)}, u32[]{:S(2)}) collective-permute-start(f32[4,5,8,256]{3,2,1,0:T(8,128)S(1)} %pad_maximum_fusion.1.near_ref), channel_id=1, source_target_pairs={{0,1},{1,0},{2,3},{3,2},{4,5},{5,4},{6,7},{7,6},{8,9},{9,8},{10,11... | collective-permute-start | bytes 491528 | tf_op jit(solution)/shard_map/ppermute | solution.py:416
  22.4 0.1 pad_add_fusion.where_ref
  22.5 0.0 copy-done.1
  22.5 0.2 collective-permute-start.8
  22.6 1.1 %collective-permute-start.7 = (f32[16,2048]{1,0:T(8,128)S(1)}, f32[16,2048]{1,0:T(8,128)S(1)}, u32[]{:S(2)}, u32[]{:S(2)}) collective-permute-start(f32[16,2048]{1,0:T(8,128)S(1)} %copy-done.1), channel_id=1, source_target_pairs={{0,4},{1,5},{2,6},{3,7},{4,0},{5,1},{6,2},{7,3},{8,12},{9,13},{10,... | collective-permute-start | bytes 393224 | tf_op jit(solution)/shard_map/ppermute | solution.py:408
  23.8 0.0 collective-permute-done.5.far_ref
  23.8 0.8 collective-permute-start.6
  24.5 0.1 collective-permute-done.4.t2_ref
  24.7 1.0 %collective-permute-done.3.t1_ref = f32[8,4,8,256]{3,2,1,0:T(8,128)S(1)} collective-permute-done((f32[8,4,8,256]{3,2,1,0:T(8,128)S(1)}, f32[8,4,8,256]{3,2,1,0:T(8,128)S(1)}, u32[]{:S(2)}, u32[]{:S(2)}) %collective-permute-start.3) | collective-permute-done | bytes 262176 | tf_op jit(solution)/shard_map/ppermute | solution.py:401
  25.7 1.7 %shard_map.65 = (f32[4,8,8,256]{3,2,1,0:T(8,128)S(1)}, f32[8,8,8,256]{3,2,1,0:T(8,128)S(1)}) custom-call(s32[3]{0:T(128)S(1)} %pad_add_fusion.where_ref, f32[8,4,8,256]{3,2,1,0:T(8,128)S(1)} %collective-permute-done.3.t1_ref, f32[8,4,8,256]{3,2,1,0:T(8,128)S(1)} %all-to-all-done.to_ref, f32[8,4,8,256]{3,2,1,0:T(8,128)S(1)} %collective-permute-done.4.t2_ref, ...), custom_call_target="tpu_custom_call" | custom-call | flops 30000001024 | bytes 1048576 | tf_op jit(solution)/shard_map/pallas_call | solution.py:384
  27.4 0.0 copy-start
  27.4 2.2 %shard_map.66 = (f32[16,7,8,128]{3,2,1,0:T(8,128)}, f32[8,5,8,256]{3,2,1,0:T(8,128)S(1)}, f32[8,5,8,256]{3,2,1,0:T(8,128)S(1)}) custom-call(s32[3]{0:T(128)S(1)} %pad_add_fusion.where_ref, f32[4,8,8,256]{3,2,1,0:T(8,128)S(1)} %get-tuple-element.33.smooth_ref, f32[8,8,8,256]{3,2,1,0:T(8,128)S(1)} %get-tuple-element.34.u_ref.u_hbm, ...), custom_call_target="tpu_custom_call" | custom-call | flops 2000000000 | bytes 1048576 | tf_op jit(solution)/shard_map/pallas_call | solution.py:384
  29.7 0.0 copy-done
  29.7 0.6 collective-permute-start.9
  30.3 3.0 %collective-permute-start.10 = (f32[8,5,8,256]{3,2,1,0:T(8,128)S(1)}, f32[8,5,8,256]{3,2,1,0:T(8,128)S(1)}, u32[]{:S(2)}, u32[]{:S(2)}) collective-permute-start(f32[8,5,8,256]{3,2,1,0:T(8,128)S(1)} %get-tuple-element.39), channel_id=1, source_target_pairs={{0,120},{8,16},{16,8},{24,32},{32,24},{40,48},{48,40},{56,64},{64,... | collective-permute-start | bytes 983048 | tf_op jit(solution)/shard_map/ppermute | solution.py:401
  33.3 0.0 collective-permute-done.8
  33.3 0.0 collective-permute-done.7
  33.3 0.0 collective-permute-done.6
  33.3 3.6 %all-to-all-start.1 = ((f32[16,7,8,128]{3,2,1,0:T(8,128)}), f32[16,7,8,128]{3,2,1,0:T(8,128)S(1)}, u32[]{:S(2)}, u32[]{:S(2)}) async-start(f32[16,7,8,128]{3,2,1,0:T(8,128)} %get-tuple-element.37), calls=%async_computation.1 | async-start | bytes 917504 | tf_op jit(solution)/shard_map/all_to_all | solution.py:475
  36.9 3.2 %collective-permute-start.12 = (f32[4,16,2048]{2,1,0:T(8,128)S(1)}, f32[4,16,2048]{2,1,0:T(8,128)S(1)}, u32[]{:S(2)}, u32[]{:S(2)}) collective-permute-start(f32[4,16,2048]{2,1,0:T(8,128)S(1)} %pad_maximum_fusion.near_ref), channel_id=1, source_target_pairs={{0,1},{1,0},{2,3},{3,2},{4,5},{5,4},{6,7},{7,6},{8,9},{9,8},{10,11... | collective-permute-start | bytes 1572872 | tf_op jit(solution)/shard_map/ppermute | solution.py:416
  40.1 0.0 collective-permute-done.9.low_ref.first_ref
  40.1 0.0 collective-permute-done.10.high_ref.second_ref
  40.1 6.3 %all-to-all-done.1.got_ref = f32[16,7,8,128]{3,2,1,0:T(8,128)S(1)} async-done(((f32[16,7,8,128]{3,2,1,0:T(8,128)}), f32[16,7,8,128]{3,2,1,0:T(8,128)S(1)}, u32[]{:S(2)}, u32[]{:S(2)}) %all-to-all-start.1) | async-done | bytes 458784 | tf_op jit(solution)/shard_map/all_to_all | solution.py:475
  46.5 3.3 %collective-permute-start.11 = (f32[16,5,8,128]{3,2,1,0:T(8,128)S(1)}, f32[16,5,8,128]{3,2,1,0:T(8,128)S(1)}, u32[]{:S(2)}, u32[]{:S(2)}) collective-permute-start(f32[16,5,8,128]{3,2,1,0:T(8,128)S(1)} %slice.3), channel_id=1, source_target_pairs={{0,1},{1,0},{2,3},{3,2},{4,5},{5,4},{6,7},{7,6},{8,9},{9,8},{10,11... | collective-permute-start | bytes 983048 | tf_op jit(solution)/shard_map/ppermute | solution.py:416
  49.8 0.0 collective-permute-done.12.far_ref
  49.8 1.3 %collective-permute-done.11.other_ref = f32[16,5,8,128]{3,2,1,0:T(8,128)S(1)} collective-permute-done((f32[16,5,8,128]{3,2,1,0:T(8,128)S(1)}, f32[16,5,8,128]{3,2,1,0:T(8,128)S(1)}, u32[]{:S(2)}, u32[]{:S(2)}) %collective-permute-start.11) | collective-permute-done | bytes 327712 | tf_op jit(solution)/shard_map/ppermute | solution.py:416
  51.1 2.7 %shard_map.68 = (f32[16,1,128]{2,1,0:T(1,128)S(1)}, f32[10,10,8,128]{3,2,1,0:T(8,128)S(1)}, s32[12,8,128]{2,1,0:T(8,128)S(1)}) custom-call(s32[3]{0:T(128)S(1)} %pad_add_fusion.where_ref, f32[16,7,8,128]{3,2,1,0:T(8,128)S(1)} %all-to-all-done.1.got_ref, f32[16,5,8,128]{3,2,1,0:T(8,128)S(1)} %collective-permute-done.11.other_ref, ...), custom_call_target="tpu_custom_call" | custom-call | flops 1000000 | bytes 1048576 | tf_op jit(solution)/shard_map/pallas_call | solution.py:384
  53.8 10.0 %all_to_all.20.table_ref = f32[16,1,128]{2,1,0:T(1,128)S(1)} all-to-all(f32[16,1,128]{2,1,0:T(1,128)S(1)} %get-tuple-element.46), channel_id=1, replica_groups=mesh['gx'=16,'gy'=8] {'gx'}, dimensions={0} | all-to-all | bytes 16384 | tf_op jit(solution)/shard_map/all_to_all | solution.py:489
  63.8 3.3 %shard_map.69 = f32[8,4,8,256]{3,2,1,0:T(8,128)S(1)} custom-call(s32[3]{0:T(128)S(1)} %pad_add_fusion.where_ref, f32[16,1,128]{2,1,0:T(1,128)S(1)} %all_to_all.20.table_ref, f32[10,10,8,128]{3,2,1,0:T(8,128)S(1)} %get-tuple-element.47.window_ref, s32[12,8,128]{2,1,0:T(8,128)S(1)} %get-tuple-element.48.ids_ref, ...), custom_call_target="tpu_custom_call" | custom-call | flops 4000000000 | bytes 1048576 | tf_op jit(solution)/shard_map/pallas_call | solution.py:384
  67.1 11.5 %all_to_all.21 = f32[8,4,8,256]{3,2,1,0:T(8,128)S(1)} all-to-all(f32[8,4,8,256]{3,2,1,0:T(8,128)S(1)} %shard_map.69), channel_id=1, replica_groups=mesh['gx'=16,'gy'=8] {'gy'}, dimensions={0} | all-to-all | bytes 524288 | tf_op jit(solution)/shard_map/all_to_all | solution.py:504
  78.6 0.7 copy.8
  (4 shorter events, 0.1 us)
Async XLA Ops:
  0.0 15.2 %all-to-all-start = ((f32[8,4,8,256]{3,2,1,0:T(8,128)}), f32[8,4,8,256]{3,2,1,0:T(8,128)S(1)}, u32[]{:S(2)}, u32[]{:S(2)}) async-start(f32[8,4,8,256]{3,2,1,0:T(8,128)} %param.6), calls=%async_computation | async-start | bytes 524288 | tf_op jit(solution)/shard_map/all_to_all | solution.py:422
  7.7 4.9 %collective-permute-start.2 = (f32[5,8,256]{2,1,0:T(8,128)S(1)}, f32[5,8,256]{2,1,0:T(8,128)S(1)}, u32[]{:S(2)}, u32[]{:S(2)}) collective-permute-start(f32[5,8,256]{2,1,0:T(8,128)S(1)} %shard_map.64), channel_id=1, source_target_pairs={{0,6},{1,7},{2,0},{3,1},{4,2},{5,3},{6,4},{7,5},{8,14},{9,15},{10,... | collective-permute-start | bytes 122888 | tf_op jit(solution)/shard_map/ppermute | solution.py:408
  10.4 4.4 %collective-permute-start.1 = (f32[5,8,256]{2,1,0:T(8,128)S(1)}, f32[5,8,256]{2,1,0:T(8,128)S(1)}, u32[]{:S(2)}, u32[]{:S(2)}) collective-permute-start(f32[5,8,256]{2,1,0:T(8,128)S(1)} %shard_map.64), channel_id=1, source_target_pairs={{0,4},{1,5},{2,6},{3,7},{4,0},{5,1},{6,2},{7,3},{8,12},{9,13},{10,... | collective-permute-start | bytes 122888 | tf_op jit(solution)/shard_map/ppermute | solution.py:408
  10.9 4.2 %collective-permute-start = (f32[5,8,256]{2,1,0:T(8,128)S(1)}, f32[5,8,256]{2,1,0:T(8,128)S(1)}, u32[]{:S(2)}, u32[]{:S(2)}) collective-permute-start(f32[5,8,256]{2,1,0:T(8,128)S(1)} %shard_map.64), channel_id=1, source_target_pairs={{0,2},{1,3},{2,4},{3,5},{4,6},{5,7},{6,0},{7,1},{8,10},{9,11},{10,... | collective-permute-start | bytes 122888 | tf_op jit(solution)/shard_map/ppermute | solution.py:408
  15.2 9.5 %collective-permute-start.4 = (f32[8,4,8,256]{3,2,1,0:T(8,128)S(1)}, f32[8,4,8,256]{3,2,1,0:T(8,128)S(1)}, u32[]{:S(2)}, u32[]{:S(2)}) collective-permute-start(f32[8,4,8,256]{3,2,1,0:T(8,128)S(1)} %all-to-all-done.to_ref), channel_id=1, source_target_pairs={{0,120},{8,16},{16,8},{24,32},{32,24},{40,48},{48,40},{56,64},{64,... | collective-permute-start | bytes 786440 | tf_op jit(solution)/shard_map/ppermute | solution.py:401
  20.1 5.6 %collective-permute-start.3 = (f32[8,4,8,256]{3,2,1,0:T(8,128)S(1)}, f32[8,4,8,256]{3,2,1,0:T(8,128)S(1)}, u32[]{:S(2)}, u32[]{:S(2)}) collective-permute-start(f32[8,4,8,256]{3,2,1,0:T(8,128)S(1)} %all-to-all-done.to_ref), channel_id=1, source_target_pairs={{0,8},{8,0},{16,24},{24,16},{32,40},{40,32},{48,56},{56,48},{64,72... | collective-permute-start | bytes 786440 | tf_op jit(solution)/shard_map/ppermute | solution.py:401
  20.1 2.4 %copy-start.1 = (f32[16,2048]{1,0:T(8,128)S(1)}, f32[16,2048]{1,0:T(8,128)}, u32[]{:S(2)}) copy-start(f32[16,2048]{1,0:T(8,128)} %param.11) | copy-start | bytes 393220
  20.1 3.6 %collective-permute-start.5 = (f32[4,5,8,256]{3,2,1,0:T(8,128)S(1)}, f32[4,5,8,256]{3,2,1,0:T(8,128)S(1)}, u32[]{:S(2)}, u32[]{:S(2)}) collective-permute-start(f32[4,5,8,256]{3,2,1,0:T(8,128)S(1)} %pad_maximum_fusion.1.near_ref), channel_id=1, source_target_pairs={{0,1},{1,0},{2,3},{3,2},{4,5},{5,4},{6,7},{7,6},{8,9},{9,8},{10,11... | collective-permute-start | bytes 491528 | tf_op jit(solution)/shard_map/ppermute | solution.py:416
  22.5 10.8 %collective-permute-start.8 = (f32[16,2048]{1,0:T(8,128)S(1)}, f32[16,2048]{1,0:T(8,128)S(1)}, u32[]{:S(2)}, u32[]{:S(2)}) collective-permute-start(f32[16,2048]{1,0:T(8,128)S(1)} %copy-done.1), channel_id=1, source_target_pairs={{0,6},{1,7},{2,0},{3,1},{4,2},{5,3},{6,4},{7,5},{8,14},{9,15},{10,... | collective-permute-start | bytes 393224 | tf_op jit(solution)/shard_map/ppermute | solution.py:408
  22.6 10.6 %collective-permute-start.7 = (f32[16,2048]{1,0:T(8,128)S(1)}, f32[16,2048]{1,0:T(8,128)S(1)}, u32[]{:S(2)}, u32[]{:S(2)}) collective-permute-start(f32[16,2048]{1,0:T(8,128)S(1)} %copy-done.1), channel_id=1, source_target_pairs={{0,4},{1,5},{2,6},{3,7},{4,0},{5,1},{6,2},{7,3},{8,12},{9,13},{10,... | collective-permute-start | bytes 393224 | tf_op jit(solution)/shard_map/ppermute | solution.py:408
  23.8 9.5 %collective-permute-start.6 = (f32[16,2048]{1,0:T(8,128)S(1)}, f32[16,2048]{1,0:T(8,128)S(1)}, u32[]{:S(2)}, u32[]{:S(2)}) collective-permute-start(f32[16,2048]{1,0:T(8,128)S(1)} %copy-done.1), channel_id=1, source_target_pairs={{0,2},{1,3},{2,4},{3,5},{4,6},{5,7},{6,0},{7,1},{8,10},{9,11},{10,... | collective-permute-start | bytes 393224 | tf_op jit(solution)/shard_map/ppermute | solution.py:408
  27.4 2.2 %copy-start = (f32[8,8,8,256]{3,2,1,0:T(8,128)}, f32[8,8,8,256]{3,2,1,0:T(8,128)S(1)}, u32[]{:S(2)}) copy-start(f32[8,8,8,256]{3,2,1,0:T(8,128)S(1)} %get-tuple-element.34.u_ref.u_hbm) | copy-start | bytes 1572868
  29.7 10.4 %collective-permute-start.9 = (f32[8,5,8,256]{3,2,1,0:T(8,128)S(1)}, f32[8,5,8,256]{3,2,1,0:T(8,128)S(1)}, u32[]{:S(2)}, u32[]{:S(2)}) collective-permute-start(f32[8,5,8,256]{3,2,1,0:T(8,128)S(1)} %get-tuple-element.38), channel_id=1, source_target_pairs={{0,8},{8,0},{16,24},{24,16},{32,40},{40,32},{48,56},{56,48},{64,72... | collective-permute-start | bytes 983048 | tf_op jit(solution)/shard_map/ppermute | solution.py:401
  30.3 9.9 %collective-permute-start.10 = (f32[8,5,8,256]{3,2,1,0:T(8,128)S(1)}, f32[8,5,8,256]{3,2,1,0:T(8,128)S(1)}, u32[]{:S(2)}, u32[]{:S(2)}) collective-permute-start(f32[8,5,8,256]{3,2,1,0:T(8,128)S(1)} %get-tuple-element.39), channel_id=1, source_target_pairs={{0,120},{8,16},{16,8},{24,32},{32,24},{40,48},{48,40},{56,64},{64,... | collective-permute-start | bytes 983048 | tf_op jit(solution)/shard_map/ppermute | solution.py:401
  33.3 13.2 %all-to-all-start.1 = ((f32[16,7,8,128]{3,2,1,0:T(8,128)}), f32[16,7,8,128]{3,2,1,0:T(8,128)S(1)}, u32[]{:S(2)}, u32[]{:S(2)}) async-start(f32[16,7,8,128]{3,2,1,0:T(8,128)} %get-tuple-element.37), calls=%async_computation.1 | async-start | bytes 917504 | tf_op jit(solution)/shard_map/all_to_all | solution.py:475
  36.9 12.9 %collective-permute-start.12 = (f32[4,16,2048]{2,1,0:T(8,128)S(1)}, f32[4,16,2048]{2,1,0:T(8,128)S(1)}, u32[]{:S(2)}, u32[]{:S(2)}) collective-permute-start(f32[4,16,2048]{2,1,0:T(8,128)S(1)} %pad_maximum_fusion.near_ref), channel_id=1, source_target_pairs={{0,1},{1,0},{2,3},{3,2},{4,5},{5,4},{6,7},{7,6},{8,9},{9,8},{10,11... | collective-permute-start | bytes 1572872 | tf_op jit(solution)/shard_map/ppermute | solution.py:416
  46.5 4.6 %collective-permute-start.11 = (f32[16,5,8,128]{3,2,1,0:T(8,128)S(1)}, f32[16,5,8,128]{3,2,1,0:T(8,128)S(1)}, u32[]{:S(2)}, u32[]{:S(2)}) collective-permute-start(f32[16,5,8,128]{3,2,1,0:T(8,128)S(1)} %slice.3), channel_id=1, source_target_pairs={{0,1},{1,0},{2,3},{3,2},{4,5},{5,4},{6,7},{7,6},{8,9},{9,8},{10,11... | collective-permute-start | bytes 983048 | tf_op jit(solution)/shard_map/ppermute | solution.py:416

commit v5 on v4

--- a/solution.py
+++ b/solution.py
@@ -166,9 +166,24 @@
         dst[k] = row if plus is None else row + plus[k - EDGE + U_EDGE]
 
 
-def down_kernel(where_ref, t1_ref, to_ref, t2_ref, far_ref, smooth_ref, u_ref, a_ref, b_ref):
-    del far_ref
-    place = where_ref[0]
+def down_kernel(
+    where_ref,
+    t1_ref,
+    to_ref,
+    t2_ref,
+    near_ref,
+    far_ref,
+    send_ref,
+    first_ref,
+    second_ref,
+    u_hbm,
+    a_ref,
+    b_ref,
+    tile_ref,
+    u_ref,
+    u_sem,
+):
+    place, chip, core = where_ref[0], where_ref[1], where_ref[2]
     odd = place & 1
     keep_low = jnp.where(place > 0, 1.0, 0.0).astype(F32)
     keep_high = jnp.where(place < GX - 1, 1.0, 0.0).astype(F32)
@@ -186,14 +201,14 @@
     relax_rows(b_ref, a_ref, 2, second, *gates)
     for k in range(CX + 2 * U_EDGE):
         u_ref[k] = u_ref[k] + (1.0 / third) * a_ref[k + shift]
+    u_copy = pltpu.make_async_copy(u_ref, u_hbm, u_sem)
+    u_copy.start()
     relax_rows(a_ref, b_ref, 1, third, *gates)
+    smooth = []
     for x in range(CX):
         k = EDGE + x
-        smooth_ref[x] = relax(b_ref[k - 1], b_ref[k], b_ref[k + 1], 1.0 / PROLONG)
-
-
-def pool_kernel(where_ref, smooth_ref, u_ref, near_ref, far_ref, send_ref, first_ref, second_ref, tile_ref):
-    chip, core = where_ref[1], where_ref[2]
+        smooth.append(relax(b_ref[k - 1], b_ref[k], b_ref[k + 1], 1.0 / PROLONG))
+
     shape = (YT, CY, CZ)
     home = lax.broadcasted_iota(jnp.int32, shape, 2) // 4
     codes = []
@@ -202,7 +217,6 @@
         first_ref[:, x] = ids.astype(F32)
         second_ref[:, x] = ids.astype(F32)
         codes.append((ids >> 6) * 3 + ((ids & 63) - home) + 1)
-    odd = where_ref[0] & 1
     first_ref[:, CX] = u_ref[U_EDGE + 1 + odd]
     second_ref[:, CX] = u_ref[U_EDGE + 2 - odd]
     pooled = []
@@ -211,7 +225,7 @@
         for k in range(6):
             total = jnp.zeros(shape, F32)
             for x in range(CX):
-                total = total + jnp.where(codes[x] == half * 6 + k, smooth_ref[x], 0.0)
+                total = total + jnp.where(codes[x] == half * 6 + k, smooth[x], 0.0)
             parts.append(jnp.sum(total, axis=1))
         pooled.append(jnp.concatenate(parts, axis=1))
     pooled = jnp.concatenate(pooled, axis=0)
@@ -230,6 +244,7 @@
     for i in range(GX):
         for k, tile in enumerate(tiles):
             send_ref[i, k] = tile
+    u_copy.wait()
 
 
 def solve_kernel(
@@ -307,8 +322,7 @@
     table_ref,
     window_ref,
     ids_ref,
-    near_ref,
-    far_ref,
+    own_ref,
     first_ref,
     second_ref,
     u_hbm,
@@ -321,7 +335,7 @@
 ):
     u_copy = pltpu.make_async_copy(u_hbm, u_ref, u_sem)
     u_copy.start()
-    place, chip, core = where_ref[0], where_ref[1], where_ref[2]
+    place = where_ref[0]
     keep_low = jnp.where(place > 0, 1.0, 0.0).astype(F32)
     keep_high = jnp.where(place < GX - 1, 1.0, 0.0).astype(F32)
     coefs = tuple(window_ref[k] for k in range(8))
@@ -352,7 +366,7 @@
 
     for slab in range(3):
         for x in range(CX):
-            ids = shared_ids(near_ref, far_ref, chip, core, x) if slab == 1 else halo(slab, x).astype(jnp.int32)
+            ids = (own_ref[:, x] if slab == 1 else halo(slab, x)).astype(jnp.int32)
             for k in range(YT):
                 table0 = jnp.broadcast_to(post_ref[2 * slab, k : k + 1], (CY, LANES))
                 table1 = jnp.broadcast_to(post_ref[2 * slab + 1, k : k + 1], (CY, LANES))
@@ -376,16 +390,22 @@
         out_ref[:, x] = relax(b_ref[k - 1], b_ref[k], b_ref[k + 1], third) + u_ref[U_EDGE + x]
 
 
-def call(kernel, out_shape, scratch, flops, scalars=0, spaces=None):
+def call(kernel, out_shape, scratch, flops, scalars=0, spaces=None, hbm_outs=()):
     def spec(k):
         return pl.BlockSpec(memory_space=pltpu.SMEM if k < scalars else (spaces or {}).get(k, pltpu.VMEM))
+
+    single = not isinstance(out_shape, list)
+    out_specs = [
+        pl.BlockSpec(memory_space=pltpu.HBM if k in hbm_outs else pltpu.VMEM)
+        for k in range(1 if single else len(out_shape))
+    ]
 
     def run(*args):
         return pl.pallas_call(
             kernel,
             out_shape=out_shape,
             in_specs=[spec(k) for k in range(len(args))],
-            out_specs=jax.tree.map(lambda _: pl.BlockSpec(memory_space=pltpu.VMEM), out_shape),
+            out_specs=out_specs[0] if single else out_specs,
             scratch_shapes=scratch,
             compiler_params=pltpu.CompilerParams(vmem_limit_bytes=24 * 1024 * 1024),
             cost_estimate=pl.CostEstimate(flops=flops, bytes_accessed=2**20, transcendentals=0),
@@ -437,7 +457,7 @@
         dict.fromkeys(range(4), pltpu.HBM),
     )(*(pltpu.with_memory_space_constraint(value, pltpu.HBM) for value in arguments))
     slabs = [tiles, *(chip_below(tiles, k) for k in range(1, 4))]
-    cells, *slabs = lax.optimization_barrier((cells, *slabs))
+    cells, slabs[3] = lax.optimization_barrier((cells, slabs[3]))
     near = jnp.stack(slabs, axis=0)
     far = other_core(near)
 
@@ -447,27 +467,25 @@
     chips = [chip_below(inverse, k) for k in range(1, 4)]
 
     field = (ROWS, YT, CY, CZ)
-    smooth, u = call(
+    send, *going, u = call(
         down_kernel,
-        [
-            pltpu.VMEM((CX, YT, CY, CZ), F32),
-            pltpu.VMEM((CX + 2 * U_EDGE, YT, CY, CZ), F32),
-        ],
-        [pltpu.VMEM(field, F32), pltpu.VMEM(field, F32)],
-        FINE_FLOPS,
-        1,
-    )(place, first, cells, second, far)
-    send, *going = call(
-        pool_kernel,
         [
             pltpu.VMEM((GX, 2 + FIELDS, YT, LANES), F32),
             pltpu.VMEM((YT, CX + 1, CY, CZ), F32),
             pltpu.VMEM((YT, CX + 1, CY, CZ), F32),
+            pltpu.HBM((CX + 2 * U_EDGE, YT, CY, CZ), F32),
         ],
-        [pltpu.VMEM((GY, CY, CZ), F32)],
-        2 * 10**9,
+        [
+            pltpu.VMEM(field, F32),
+            pltpu.VMEM(field, F32),
+            pltpu.VMEM((GY, CY, CZ), F32),
+            pltpu.VMEM((CX + 2 * U_EDGE, YT, CY, CZ), F32),
+            pltpu.SemaphoreType.DMA,
+        ],
+        FINE_FLOPS,
         1,
-    )(place, smooth, u, near, far)
+        hbm_outs=(3,),
+    )(place, first, cells, second, near, far)
     send, inverse, *chips = lax.optimization_barrier((send, inverse, *chips))
     inverse_near = jnp.stack([inverse, *chips], axis=0)
     inverse_far = other_core(inverse_near)
@@ -499,8 +517,8 @@
         ],
         4 * 10**9,
         1,
-        {8: pltpu.HBM},
-    )(place, table, window, unknowns, near, far, first, second, pltpu.with_memory_space_constraint(u, pltpu.HBM))
+        {7: pltpu.HBM},
+    )(place, table, window, unknowns, going[0], first, second, pltpu.with_memory_space_constraint(u, pltpu.HBM))
     return lax.all_to_all(out, "gy", 0, 0, tiled=True)
 
 

time: 79.8 us -> 78.5 us (0.984)
  waiting for transfers between devices: 12.4 us -> 10.7 us
  starting transfers between devices: 33.6 us -> 34.5 us
    ppermute x6, waiting for transfers between devices: 3.65 us -> 1.11 us  [chip_below(): lax.ppermute(value, 'gy', [(j, (j + 2 * step) % GY) for j in range(GY)])]
    ppermute x6, starting transfers between devices: 5.88 us -> 6.91 us  [chip_below(): lax.ppermute(value, 'gy', [(j, (j + 2 * step) % GY) for j in range(GY)])]
    pallas_call x6 -> x5, Pallas kernels: 10.8 us -> 10.4 us  [run(): pl.pallas_call(kernel, out_shape=out_shape, in_specs=[spec(k) for k in ra...]
  transfers between devices with their start and end apart: 15 -> 15, of which waited for: 7 -> 6; matrix products, arithmetic and copies ran while one was open for 0% -> 0% of each run, Pallas kernels for 6% -> 6%
where the time goes in v5:
time: 78.5 us; the launch traced here: 78 us
  starting transfers between devices  34.5 us (44%)
  blocking collectives  21.4 us (27%)
  waiting for transfers between devices  10.7 us (14%)
  Pallas kernels  10.4 us (13%)
    all_to_all x1, blocking collectives, local(): return lax.all_to_all(out, 'gy', 0, 0, tiled=True)  11.9 us
    pallas_call x5, Pallas kernels, run(): pl.pallas_call(kernel, out_shape=out_shape, in_specs=[spec(k) for k in ra...  10.4 us
    all_to_all x1, blocking collectives, local(): table = lax.all_to_all(send, 'gx', 0, 0, tiled=True)  9.52 us
    ppermute x4, starting transfers between devices, beside(): return (lax.ppermute(first, 'gx', one), lax.ppermute(second, 'gx', two))  8.62 us
    ppermute x3, starting transfers between devices, other_core(): return lax.ppermute(value, 'gy', [(j, j ^ 1) for j in range(GY)])  8.46 us
    ppermute x6, starting transfers between devices, chip_below(): lax.ppermute(value, 'gy', [(j, (j + 2 * step) % GY) for j in range(GY)])  6.91 us
    all_to_all x1, starting transfers between devices, local(): cells = lax.all_to_all(right_side, 'gy', 0, 0, tiled=True)  6.81 us
    all_to_all x1, waiting for transfers between devices, local(): got = lax.all_to_all(send, 'gx', 0, 0, tiled=True)  5.79 us
  transfers between devices with their start and end apart: 15, of which 6 were waited for; matrix products, arithmetic and copies ran while one was open for 0% of the time, Pallas kernels for 6%

profile of v5, /device:TPU:1, one launch (start us, length us, event | category | flops | bytes accessed | tf_op | source)
XLA Modules:
  0.0 78.0 jit_solution(3683248785686284446)
XLA Ops:
  0.0 6.8 %all-to-all-start = ((f32[8,4,8,256]{3,2,1,0:T(8,128)}), f32[8,4,8,256]{3,2,1,0:T(8,128)S(1)}, u32[]{:S(2)}, u32[]{:S(2)}) async-start(f32[8,4,8,256]{3,2,1,0:T(8,128)} %param.6), calls=%async_computation | async-start | bytes 524288 | tf_op jit(solution)/shard_map/all_to_all | solution.py:442
  6.8 0.9 %shard_map.64 = f32[5,8,256]{2,1,0:T(8,128)S(1)} custom-call(s32[4,8,256]{2,1,0:T(8,128)} %ids_ref.1, f32[2,2,64]{2,1,0:T(2,128)} %diag_ref.1, f32[6,2,2,64]{3,2,1,0:T(2,128)} %links_ref.1, s32[2,2,64]{2,1,0:T(2,128)} %coarse_ids_ref.1), custom_call_target="tpu_custom_call" | custom-call | flops 100000000 | bytes 1048576 | tf_op jit(solution)/shard_map/pallas_call | solution.py:404
  7.7 2.7 %collective-permute-start = (f32[5,8,256]{2,1,0:T(8,128)S(1)}, f32[5,8,256]{2,1,0:T(8,128)S(1)}, u32[]{:S(2)}, u32[]{:S(2)}) collective-permute-start(f32[5,8,256]{2,1,0:T(8,128)S(1)} %shard_map.64), channel_id=1, source_target_pairs={{0,6},{1,7},{2,0},{3,1},{4,2},{5,3},{6,4},{7,5},{8,14},{9,15},{10,... | collective-permute-start | bytes 122888 | tf_op jit(solution)/shard_map/ppermute | solution.py:428
  10.4 0.6 collective-permute-start.4
  10.9 0.6 collective-permute-start.3
  11.5 1.1 %collective-permute-done = f32[5,8,256]{2,1,0:T(8,128)S(1)} collective-permute-done((f32[5,8,256]{2,1,0:T(8,128)S(1)}, f32[5,8,256]{2,1,0:T(8,128)S(1)}, u32[]{:S(2)}, u32[]{:S(2)}) %collective-permute-start) | collective-permute-done | bytes 40992 | tf_op jit(solution)/shard_map/ppermute | solution.py:428
  12.6 0.7 all-to-all-done.to_ref
  13.3 4.9 %collective-permute-start.2 = (f32[8,4,8,256]{3,2,1,0:T(8,128)S(1)}, f32[8,4,8,256]{3,2,1,0:T(8,128)S(1)}, u32[]{:S(2)}, u32[]{:S(2)}) collective-permute-start(f32[8,4,8,256]{3,2,1,0:T(8,128)S(1)} %all-to-all-done.to_ref), channel_id=1, source_target_pairs={{0,120},{8,16},{16,8},{24,32},{32,24},{40,48},{48,40},{56,64},{64,... | collective-permute-start | bytes 786440 | tf_op jit(solution)/shard_map/ppermute | solution.py:421
  18.2 0.0 collective-permute-start.1
  18.3 0.0 collective-permute-done.4
  18.3 0.0 collective-permute-done.3
  18.3 0.0 copy-start
  18.3 1.4 %collective-permute-start.5 = (f32[4,5,8,256]{3,2,1,0:T(8,128)S(1)}, f32[4,5,8,256]{3,2,1,0:T(8,128)S(1)}, u32[]{:S(2)}, u32[]{:S(2)}) collective-permute-start(f32[4,5,8,256]{3,2,1,0:T(8,128)S(1)} %pad_maximum_fusion.1.near_ref), channel_id=1, source_target_pairs={{0,1},{1,0},{2,3},{3,2},{4,5},{5,4},{6,7},{7,6},{8,9},{9,8},{10,11... | collective-permute-start | bytes 491528 | tf_op jit(solution)/shard_map/ppermute | solution.py:436
  19.7 0.1 pad_add_fusion.where_ref
  19.8 0.0 copy-done
  19.8 2.2 %collective-permute-start.8 = (f32[16,2048]{1,0:T(8,128)S(1)}, f32[16,2048]{1,0:T(8,128)S(1)}, u32[]{:S(2)}, u32[]{:S(2)}) collective-permute-start(f32[16,2048]{1,0:T(8,128)S(1)} %copy-done), channel_id=1, source_target_pairs={{0,6},{1,7},{2,0},{3,1},{4,2},{5,3},{6,4},{7,5},{8,14},{9,15},{10,... | collective-permute-start | bytes 393224 | tf_op jit(solution)/shard_map/ppermute | solution.py:428
  22.0 0.3 collective-permute-start.7
  22.3 0.0 collective-permute-done.5.far_ref
  22.3 0.5 collective-permute-start.6
  22.9 0.8 %collective-permute-done.2.t2_ref = f32[8,4,8,256]{3,2,1,0:T(8,128)S(1)} collective-permute-done((f32[8,4,8,256]{3,2,1,0:T(8,128)S(1)}, f32[8,4,8,256]{3,2,1,0:T(8,128)S(1)}, u32[]{:S(2)}, u32[]{:S(2)}) %collective-permute-start.2) | collective-permute-done | bytes 262176 | tf_op jit(solution)/shard_map/ppermute | solution.py:421
  23.7 1.0 %collective-permute-done.1.t1_ref = f32[8,4,8,256]{3,2,1,0:T(8,128)S(1)} collective-permute-done((f32[8,4,8,256]{3,2,1,0:T(8,128)S(1)}, f32[8,4,8,256]{3,2,1,0:T(8,128)S(1)}, u32[]{:S(2)}, u32[]{:S(2)}) %collective-permute-start.1) | collective-permute-done | bytes 262176 | tf_op jit(solution)/shard_map/ppermute | solution.py:421
  24.7 3.5 %shard_map.65 = (f32[16,7,8,128]{3,2,1,0:T(8,128)}, f32[8,5,8,256]{3,2,1,0:T(8,128)S(1)}, f32[8,5,8,256]{3,2,1,0:T(8,128)S(1)}, f32[8,8,8,256]{3,2,1,0:T(8,128)}) custom-call(s32[3]{0:T(128)S(1)} %pad_add_fusion.where_ref, f32[8,4,8,256]{3,2,1,0:T(8,128)S(1)} %collective-permute-done.1.t1_ref, f32[8,4,8,256]{3,2,1,0:T(8,128)S(1)} %all-to-all-done.to_ref, ...), custom_call_target="tpu_custom_call" | custom-call | flops 30000001024 | bytes 1048576 | tf_op jit(solution)/shard_map/pallas_call | solution.py:404
  28.3 3.7 %collective-permute-start.10 = (f32[8,5,8,256]{3,2,1,0:T(8,128)S(1)}, f32[8,5,8,256]{3,2,1,0:T(8,128)S(1)}, u32[]{:S(2)}, u32[]{:S(2)}) collective-permute-start(f32[8,5,8,256]{3,2,1,0:T(8,128)S(1)} %get-tuple-element.30), channel_id=1, source_target_pairs={{0,120},{8,16},{16,8},{24,32},{32,24},{40,48},{48,40},{56,64},{64,... | collective-permute-start | bytes 983048 | tf_op jit(solution)/shard_map/ppermute | solution.py:421
  32.0 0.0 collective-permute-start.9
  32.0 0.0 collective-permute-done.8
  32.0 0.0 collective-permute-done.7
  32.0 0.0 collective-permute-done.6
  32.0 3.7 %all-to-all-start.1 = ((f32[16,7,8,128]{3,2,1,0:T(8,128)}), f32[16,7,8,128]{3,2,1,0:T(8,128)S(1)}, u32[]{:S(2)}, u32[]{:S(2)}) async-start(f32[16,7,8,128]{3,2,1,0:T(8,128)} %get-tuple-element.28), calls=%async_computation.1 | async-start | bytes 917504 | tf_op jit(solution)/shard_map/all_to_all | solution.py:493
  35.8 3.2 %collective-permute-start.12 = (f32[4,16,2048]{2,1,0:T(8,128)S(1)}, f32[4,16,2048]{2,1,0:T(8,128)S(1)}, u32[]{:S(2)}, u32[]{:S(2)}) collective-permute-start(f32[4,16,2048]{2,1,0:T(8,128)S(1)} %pad_maximum_fusion.near_ref), channel_id=1, source_target_pairs={{0,1},{1,0},{2,3},{3,2},{4,5},{5,4},{6,7},{7,6},{8,9},{9,8},{10,11... | collective-permute-start | bytes 1572872 | tf_op jit(solution)/shard_map/ppermute | solution.py:436
  39.0 0.0 collective-permute-done.10.high_ref.second_ref
  39.0 0.0 collective-permute-done.9.low_ref.first_ref
  39.0 5.8 %all-to-all-done.1.got_ref = f32[16,7,8,128]{3,2,1,0:T(8,128)S(1)} async-done(((f32[16,7,8,128]{3,2,1,0:T(8,128)}), f32[16,7,8,128]{3,2,1,0:T(8,128)S(1)}, u32[]{:S(2)}, u32[]{:S(2)}) %all-to-all-start.1) | async-done | bytes 458784 | tf_op jit(solution)/shard_map/all_to_all | solution.py:493
  44.8 3.9 %collective-permute-start.11 = (f32[16,5,8,128]{3,2,1,0:T(8,128)S(1)}, f32[16,5,8,128]{3,2,1,0:T(8,128)S(1)}, u32[]{:S(2)}, u32[]{:S(2)}) collective-permute-start(f32[16,5,8,128]{3,2,1,0:T(8,128)S(1)} %slice.3), channel_id=1, source_target_pairs={{0,1},{1,0},{2,3},{3,2},{4,5},{5,4},{6,7},{7,6},{8,9},{9,8},{10,11... | collective-permute-start | bytes 983048 | tf_op jit(solution)/shard_map/ppermute | solution.py:436
  48.7 0.0 collective-permute-done.12.far_ref
  48.7 1.3 %collective-permute-done.11.other_ref = f32[16,5,8,128]{3,2,1,0:T(8,128)S(1)} collective-permute-done((f32[16,5,8,128]{3,2,1,0:T(8,128)S(1)}, f32[16,5,8,128]{3,2,1,0:T(8,128)S(1)}, u32[]{:S(2)}, u32[]{:S(2)}) %collective-permute-start.11) | collective-permute-done | bytes 327712 | tf_op jit(solution)/shard_map/ppermute | solution.py:436
  49.9 2.7 %shard_map.67 = (f32[16,1,128]{2,1,0:T(1,128)S(1)}, f32[10,10,8,128]{3,2,1,0:T(8,128)S(1)}, s32[12,8,128]{2,1,0:T(8,128)S(1)}) custom-call(s32[3]{0:T(128)S(1)} %pad_add_fusion.where_ref, f32[16,7,8,128]{3,2,1,0:T(8,128)S(1)} %all-to-all-done.1.got_ref, f32[16,5,8,128]{3,2,1,0:T(8,128)S(1)} %collective-permute-done.11.other_ref, ...), custom_call_target="tpu_custom_call" | custom-call | flops 1000000 | bytes 1048576 | tf_op jit(solution)/shard_map/pallas_call | solution.py:404
  52.6 9.5 %all_to_all.20.table_ref = f32[16,1,128]{2,1,0:T(1,128)S(1)} all-to-all(f32[16,1,128]{2,1,0:T(1,128)S(1)} %get-tuple-element.37), channel_id=1, replica_groups=mesh['gx'=16,'gy'=8] {'gx'}, dimensions={0} | all-to-all | bytes 16384 | tf_op jit(solution)/shard_map/all_to_all | solution.py:507
  62.2 3.3 %shard_map.68 = f32[8,4,8,256]{3,2,1,0:T(8,128)S(1)} custom-call(s32[3]{0:T(128)S(1)} %pad_add_fusion.where_ref, f32[16,1,128]{2,1,0:T(1,128)S(1)} %all_to_all.20.table_ref, f32[10,10,8,128]{3,2,1,0:T(8,128)S(1)} %get-tuple-element.38.window_ref, s32[12,8,128]{2,1,0:T(8,128)S(1)} %get-tuple-element.39.ids_ref, ...), custom_call_target="tpu_custom_call" | custom-call | flops 4000000000 | bytes 1048576 | tf_op jit(solution)/shard_map/pallas_call | solution.py:404
  65.4 11.9 %all_to_all.21 = f32[8,4,8,256]{3,2,1,0:T(8,128)S(1)} all-to-all(f32[8,4,8,256]{3,2,1,0:T(8,128)S(1)} %shard_map.68), channel_id=1, replica_groups=mesh['gx'=16,'gy'=8] {'gy'}, dimensions={0} | all-to-all | bytes 524288 | tf_op jit(solution)/shard_map/all_to_all | solution.py:522
  77.3 0.7 copy.8
  (4 shorter events, 0.1 us)
Async XLA Ops:
  0.0 13.3 %all-to-all-start = ((f32[8,4,8,256]{3,2,1,0:T(8,128)}), f32[8,4,8,256]{3,2,1,0:T(8,128)S(1)}, u32[]{:S(2)}, u32[]{:S(2)}) async-start(f32[8,4,8,256]{3,2,1,0:T(8,128)} %param.6), calls=%async_computation | async-start | bytes 524288 | tf_op jit(solution)/shard_map/all_to_all | solution.py:442
  7.7 4.9 %collective-permute-start = (f32[5,8,256]{2,1,0:T(8,128)S(1)}, f32[5,8,256]{2,1,0:T(8,128)S(1)}, u32[]{:S(2)}, u32[]{:S(2)}) collective-permute-start(f32[5,8,256]{2,1,0:T(8,128)S(1)} %shard_map.64), channel_id=1, source_target_pairs={{0,6},{1,7},{2,0},{3,1},{4,2},{5,3},{6,4},{7,5},{8,14},{9,15},{10,... | collective-permute-start | bytes 122888 | tf_op jit(solution)/shard_map/ppermute | solution.py:428
  10.4 7.9 %collective-permute-start.4 = (f32[5,8,256]{2,1,0:T(8,128)S(1)}, f32[5,8,256]{2,1,0:T(8,128)S(1)}, u32[]{:S(2)}, u32[]{:S(2)}) collective-permute-start(f32[5,8,256]{2,1,0:T(8,128)S(1)} %shard_map.64), channel_id=1, source_target_pairs={{0,4},{1,5},{2,6},{3,7},{4,0},{5,1},{6,2},{7,3},{8,12},{9,13},{10,... | collective-permute-start | bytes 122888 | tf_op jit(solution)/shard_map/ppermute | solution.py:428
  10.9 7.3 %collective-permute-start.3 = (f32[5,8,256]{2,1,0:T(8,128)S(1)}, f32[5,8,256]{2,1,0:T(8,128)S(1)}, u32[]{:S(2)}, u32[]{:S(2)}) collective-permute-start(f32[5,8,256]{2,1,0:T(8,128)S(1)} %shard_map.64), channel_id=1, source_target_pairs={{0,2},{1,3},{2,4},{3,5},{4,6},{5,7},{6,0},{7,1},{8,10},{9,11},{10,... | collective-permute-start | bytes 122888 | tf_op jit(solution)/shard_map/ppermute | solution.py:428
  13.3 10.4 %collective-permute-start.2 = (f32[8,4,8,256]{3,2,1,0:T(8,128)S(1)}, f32[8,4,8,256]{3,2,1,0:T(8,128)S(1)}, u32[]{:S(2)}, u32[]{:S(2)}) collective-permute-start(f32[8,4,8,256]{3,2,1,0:T(8,128)S(1)} %all-to-all-done.to_ref), channel_id=1, source_target_pairs={{0,120},{8,16},{16,8},{24,32},{32,24},{40,48},{48,40},{56,64},{64,... | collective-permute-start | bytes 786440 | tf_op jit(solution)/shard_map/ppermute | solution.py:421
  18.2 6.5 %collective-permute-start.1 = (f32[8,4,8,256]{3,2,1,0:T(8,128)S(1)}, f32[8,4,8,256]{3,2,1,0:T(8,128)S(1)}, u32[]{:S(2)}, u32[]{:S(2)}) collective-permute-start(f32[8,4,8,256]{3,2,1,0:T(8,128)S(1)} %all-to-all-done.to_ref), channel_id=1, source_target_pairs={{0,8},{8,0},{16,24},{24,16},{32,40},{40,32},{48,56},{56,48},{64,72... | collective-permute-start | bytes 786440 | tf_op jit(solution)/shard_map/ppermute | solution.py:421
  18.3 1.5 %copy-start = (f32[16,2048]{1,0:T(8,128)S(1)}, f32[16,2048]{1,0:T(8,128)}, u32[]{:S(2)}) copy-start(f32[16,2048]{1,0:T(8,128)} %param.11) | copy-start | bytes 393220
  18.3 4.0 %collective-permute-start.5 = (f32[4,5,8,256]{3,2,1,0:T(8,128)S(1)}, f32[4,5,8,256]{3,2,1,0:T(8,128)S(1)}, u32[]{:S(2)}, u32[]{:S(2)}) collective-permute-start(f32[4,5,8,256]{3,2,1,0:T(8,128)S(1)} %pad_maximum_fusion.1.near_ref), channel_id=1, source_target_pairs={{0,1},{1,0},{2,3},{3,2},{4,5},{5,4},{6,7},{7,6},{8,9},{9,8},{10,11... | collective-permute-start | bytes 491528 | tf_op jit(solution)/shard_map/ppermute | solution.py:436
  19.8 12.2 %collective-permute-start.8 = (f32[16,2048]{1,0:T(8,128)S(1)}, f32[16,2048]{1,0:T(8,128)S(1)}, u32[]{:S(2)}, u32[]{:S(2)}) collective-permute-start(f32[16,2048]{1,0:T(8,128)S(1)} %copy-done), channel_id=1, source_target_pairs={{0,6},{1,7},{2,0},{3,1},{4,2},{5,3},{6,4},{7,5},{8,14},{9,15},{10,... | collective-permute-start | bytes 393224 | tf_op jit(solution)/shard_map/ppermute | solution.py:428
  22.0 10.0 %collective-permute-start.7 = (f32[16,2048]{1,0:T(8,128)S(1)}, f32[16,2048]{1,0:T(8,128)S(1)}, u32[]{:S(2)}, u32[]{:S(2)}) collective-permute-start(f32[16,2048]{1,0:T(8,128)S(1)} %copy-done), channel_id=1, source_target_pairs={{0,4},{1,5},{2,6},{3,7},{4,0},{5,1},{6,2},{7,3},{8,12},{9,13},{10,... | collective-permute-start | bytes 393224 | tf_op jit(solution)/shard_map/ppermute | solution.py:428
  22.3 9.7 %collective-permute-start.6 = (f32[16,2048]{1,0:T(8,128)S(1)}, f32[16,2048]{1,0:T(8,128)S(1)}, u32[]{:S(2)}, u32[]{:S(2)}) collective-permute-start(f32[16,2048]{1,0:T(8,128)S(1)} %copy-done), channel_id=1, source_target_pairs={{0,2},{1,3},{2,4},{3,5},{4,6},{5,7},{6,0},{7,1},{8,10},{9,11},{10,... | collective-permute-start | bytes 393224 | tf_op jit(solution)/shard_map/ppermute | solution.py:428
  28.3 10.7 %collective-permute-start.10 = (f32[8,5,8,256]{3,2,1,0:T(8,128)S(1)}, f32[8,5,8,256]{3,2,1,0:T(8,128)S(1)}, u32[]{:S(2)}, u32[]{:S(2)}) collective-permute-start(f32[8,5,8,256]{3,2,1,0:T(8,128)S(1)} %get-tuple-element.30), channel_id=1, source_target_pairs={{0,120},{8,16},{16,8},{24,32},{32,24},{40,48},{48,40},{56,64},{64,... | collective-permute-start | bytes 983048 | tf_op jit(solution)/shard_map/ppermute | solution.py:421
  32.0 7.0 %collective-permute-start.9 = (f32[8,5,8,256]{3,2,1,0:T(8,128)S(1)}, f32[8,5,8,256]{3,2,1,0:T(8,128)S(1)}, u32[]{:S(2)}, u32[]{:S(2)}) collective-permute-start(f32[8,5,8,256]{3,2,1,0:T(8,128)S(1)} %get-tuple-element.29.own_ref), channel_id=1, source_target_pairs={{0,8},{8,0},{16,24},{24,16},{32,40},{40,32},{48,56},{56,48},{64,72... | collective-permute-start | bytes 983048 | tf_op jit(solution)/shard_map/ppermute | solution.py:421
  32.0 12.8 %all-to-all-start.1 = ((f32[16,7,8,128]{3,2,1,0:T(8,128)}), f32[16,7,8,128]{3,2,1,0:T(8,128)S(1)}, u32[]{:S(2)}, u32[]{:S(2)}) async-start(f32[16,7,8,128]{3,2,1,0:T(8,128)} %get-tuple-element.28), calls=%async_computation.1 | async-start | bytes 917504 | tf_op jit(solution)/shard_map/all_to_all | solution.py:493
  35.8 12.9 %collective-permute-start.12 = (f32[4,16,2048]{2,1,0:T(8,128)S(1)}, f32[4,16,2048]{2,1,0:T(8,128)S(1)}, u32[]{:S(2)}, u32[]{:S(2)}) collective-permute-start(f32[4,16,2048]{2,1,0:T(8,128)S(1)} %pad_maximum_fusion.near_ref), channel_id=1, source_target_pairs={{0,1},{1,0},{2,3},{3,2},{4,5},{5,4},{6,7},{7,6},{8,9},{9,8},{10,11... | collective-permute-start | bytes 1572872 | tf_op jit(solution)/shard_map/ppermute | solution.py:436
  44.8 5.1 %collective-permute-start.11 = (f32[16,5,8,128]{3,2,1,0:T(8,128)S(1)}, f32[16,5,8,128]{3,2,1,0:T(8,128)S(1)}, u32[]{:S(2)}, u32[]{:S(2)}) collective-permute-start(f32[16,5,8,128]{3,2,1,0:T(8,128)S(1)} %slice.3), channel_id=1, source_target_pairs={{0,1},{1,0},{2,3},{3,2},{4,5},{5,4},{6,7},{7,6},{8,9},{9,8},{10,11... | collective-permute-start | bytes 983048 | tf_op jit(solution)/shard_map/ppermute | solution.py:436

commit v6 on v5

--- a/solution.py
+++ b/solution.py
@@ -106,12 +106,15 @@
     return first, second, third
 
 
-def tiles_kernel(ids_ref, diag_ref, links_ref, coarse_ids_ref, out_ref, id_buf, diag_buf, link_buf, cid_buf, sems):
+def tiles_kernel(
+    where_ref, ids_ref, diag_ref, links_ref, coarse_ids_ref, inverse_hbm, out_ref, inverse_ref, id_buf, diag_buf, link_buf, cid_buf, sems
+):
     pairs = ((ids_ref, id_buf), (diag_ref, diag_buf), (links_ref, link_buf), (coarse_ids_ref, cid_buf))
     copies = [pltpu.make_async_copy(src, dst, sems.at[k]) for k, (src, dst) in enumerate(pairs)]
+    copies.append(pltpu.make_async_copy(inverse_hbm, inverse_ref, sems.at[4]))
     for copy in copies:
         copy.start()
-    for copy in copies:
+    for copy in copies[:4]:
         copy.wait()
     fields = (
         diag_buf[...],
@@ -128,6 +131,7 @@
     for x in range(CX):
         out_ref[x] = id_buf[x].astype(F32)
     out_ref[CX] = jnp.concatenate(rows, axis=0)
+    copies[4].wait()
 
 
 def shared_tile(near_ref, far_ref, chip, core, j, tile):
@@ -229,10 +233,10 @@
             parts.append(jnp.sum(total, axis=1))
         pooled.append(jnp.concatenate(parts, axis=1))
     pooled = jnp.concatenate(pooled, axis=0)
-    pieces = jnp.concatenate(split3(pooled), axis=0)
+    pieces = jnp.concatenate(split3(pooled)[:2], axis=0)
     sums = jnp.dot(pieces, pool_matrix(), preferred_element_type=F32)
     rows = 2 * YT
-    target = sums[:rows] + sums[rows : 2 * rows] + sums[2 * rows :]
+    target = sums[:rows] + sums[rows:]
     tiles = [target[:YT], target[YT:]]
     for j in range(GY):
         tile_ref[j] = shared_tile(near_ref, far_ref, chip, core, j, CX)
@@ -441,21 +445,21 @@
     place = jnp.stack([lax.axis_index("gx"), row // 2, row % 2]).astype(jnp.int32)
     cells = lax.all_to_all(right_side, "gy", 0, 0, tiled=True)
 
-    arguments = (fine_ids, coarse_diag, coarse_links, coarse_ids)
-    tiles = call(
+    arguments = (fine_ids, coarse_diag, coarse_links, coarse_ids, coarsest_inverse)
+    tiles, inverse = call(
         tiles_kernel,
-        pltpu.VMEM((CX + 1, CY, CZ), F32),
+        [pltpu.VMEM((CX + 1, CY, CZ), F32), pltpu.VMEM((HI, NC2), F32)],
         [
             pltpu.VMEM((CX, CY, CZ), jnp.int32),
             pltpu.VMEM((2, 2, 64), F32),
             pltpu.VMEM((6, 2, 2, 64), F32),
             pltpu.VMEM((2, 2, 64), jnp.int32),
-            pltpu.SemaphoreType.DMA((4,)),
+            pltpu.SemaphoreType.DMA((5,)),
         ],
         10**8,
-        0,
-        dict.fromkeys(range(4), pltpu.HBM),
-    )(*(pltpu.with_memory_space_constraint(value, pltpu.HBM) for value in arguments))
+        1,
+        dict.fromkeys(range(1, 6), pltpu.HBM),
+    )(place, *(pltpu.with_memory_space_constraint(value, pltpu.HBM) for value in arguments))
     slabs = [tiles, *(chip_below(tiles, k) for k in range(1, 4))]
     cells, slabs[3] = lax.optimization_barrier((cells, slabs[3]))
     near = jnp.stack(slabs, axis=0)
@@ -463,7 +467,7 @@
 
     first, second = beside(cells, cells)
 
-    cells, inverse = lax.optimization_barrier((cells, coarsest_inverse))
+    cells, inverse = lax.optimization_barrier((cells, inverse))
     chips = [chip_below(inverse, k) for k in range(1, 4)]
 
     field = (ROWS, YT, CY, CZ)
@@ -486,7 +490,7 @@
         1,
         hbm_outs=(3,),
     )(place, first, cells, second, near, far)
-    send, inverse, *chips = lax.optimization_barrier((send, inverse, *chips))
+    send, chips[0], chips[2] = lax.optimization_barrier((send, chips[0], chips[2]))
     inverse_near = jnp.stack([inverse, *chips], axis=0)
     inverse_far = other_core(inverse_near)
     first, second = beside(*going)

time: 78.5 us -> 77.9 us (level)
  waiting for transfers between devices: 10.7 us -> 9.46 us
  transfers between devices with their start and end apart: 15 -> 15, of which waited for: 6 -> 6; matrix products, arithmetic and copies ran while one was open for 0% -> 0% of each run, Pallas kernels for 6% -> 7%
where the time goes in v6:
time: 77.9 us; the launch traced here: 77.5 us
  starting transfers between devices  35.1 us (45%)
  blocking collectives  20.8 us (27%)
  Pallas kernels  11.1 us (14%)
  waiting for transfers between devices  9.46 us (12%)
    all_to_all x1, blocking collectives, local(): return lax.all_to_all(out, 'gy', 0, 0, tiled=True)  11.3 us
    pallas_call x5, Pallas kernels, run(): pl.pallas_call(kernel, out_shape=out_shape, in_specs=[spec(k) for k in ra...  11.1 us
    all_to_all x1, blocking collectives, local(): table = lax.all_to_all(send, 'gx', 0, 0, tiled=True)  9.53 us
    ppermute x4, starting transfers between devices, beside(): return (lax.ppermute(first, 'gx', one), lax.ppermute(second, 'gx', two))  8.62 us
    ppermute x3, starting transfers between devices, other_core(): return lax.ppermute(value, 'gy', [(j, j ^ 1) for j in range(GY)])  8.44 us
    ppermute x6, starting transfers between devices, chip_below(): lax.ppermute(value, 'gy', [(j, (j + 2 * step) % GY) for j in range(GY)])  7.51 us
    all_to_all x1, starting transfers between devices, local(): cells = lax.all_to_all(right_side, 'gy', 0, 0, tiled=True)  6.81 us
    all_to_all x1, waiting for transfers between devices, local(): got = lax.all_to_all(send, 'gx', 0, 0, tiled=True)  5.8 us
  transfers between devices with their start and end apart: 15, of which 6 were waited for; matrix products, arithmetic and copies ran while one was open for 0% of the time, Pallas kernels for 7%

profile of v6, /device:TPU:1, one launch (start us, length us, event | category | flops | bytes accessed | tf_op | source)
XLA Modules:
  0.0 77.5 jit_solution(9999566932727609889)
XLA Ops:
  0.0 6.8 %all-to-all-start = ((f32[8,4,8,256]{3,2,1,0:T(8,128)}), f32[8,4,8,256]{3,2,1,0:T(8,128)S(1)}, u32[]{:S(2)}, u32[]{:S(2)}) async-start(f32[8,4,8,256]{3,2,1,0:T(8,128)} %param.6), calls=%async_computation | async-start | bytes 524288 | tf_op jit(solution)/shard_map/all_to_all | solution.py:446
  6.8 0.1 pad_add_fusion.where_ref
  6.9 1.6 %shard_map.64 = (f32[5,8,256]{2,1,0:T(8,128)S(1)}, f32[16,2048]{1,0:T(8,128)S(1)}) custom-call(s32[3]{0:T(128)S(1)} %pad_add_fusion.where_ref, s32[4,8,256]{2,1,0:T(8,128)} %ids_ref.1, f32[2,2,64]{2,1,0:T(2,128)} %diag_ref.1, f32[6,2,2,64]{3,2,1,0:T(2,128)} %links_ref.1, s32[2,2,64]{2,1,0:T(2,128)} %coarse_ids_ref.1, f32[16,2048]{1,0:T(8,128)} %inverse_hbm.1), custom_call_target="tpu_custom_call" | custom-call | flops 100000000 | bytes 1048576 | tf_op jit(solution)/shard_map/pallas_call | solution.py:408
  8.5 2.7 %collective-permute-start = (f32[5,8,256]{2,1,0:T(8,128)S(1)}, f32[5,8,256]{2,1,0:T(8,128)S(1)}, u32[]{:S(2)}, u32[]{:S(2)}) collective-permute-start(f32[5,8,256]{2,1,0:T(8,128)S(1)} %get-tuple-element.23), channel_id=1, source_target_pairs={{0,6},{1,7},{2,0},{3,1},{4,2},{5,3},{6,4},{7,5},{8,14},{9,15},{10,... | collective-permute-start | bytes 122888 | tf_op jit(solution)/shard_map/ppermute | solution.py:432
  11.1 0.6 collective-permute-start.4
  11.7 0.6 collective-permute-start.3
  12.3 0.3 collective-permute-done
  12.6 0.7 all-to-all-done.to_ref
  13.3 4.9 %collective-permute-start.2 = (f32[8,4,8,256]{3,2,1,0:T(8,128)S(1)}, f32[8,4,8,256]{3,2,1,0:T(8,128)S(1)}, u32[]{:S(2)}, u32[]{:S(2)}) collective-permute-start(f32[8,4,8,256]{3,2,1,0:T(8,128)S(1)} %all-to-all-done.to_ref), channel_id=1, source_target_pairs={{0,120},{8,16},{16,8},{24,32},{32,24},{40,48},{48,40},{56,64},{64,... | collective-permute-start | bytes 786440 | tf_op jit(solution)/shard_map/ppermute | solution.py:425
  18.2 0.0 collective-permute-start.1
  18.3 0.0 collective-permute-done.4
  18.3 0.0 collective-permute-done.3
  18.3 1.4 %collective-permute-start.5 = (f32[4,5,8,256]{3,2,1,0:T(8,128)S(1)}, f32[4,5,8,256]{3,2,1,0:T(8,128)S(1)}, u32[]{:S(2)}, u32[]{:S(2)}) collective-permute-start(f32[4,5,8,256]{3,2,1,0:T(8,128)S(1)} %pad_maximum_fusion.1.near_ref), channel_id=1, source_target_pairs={{0,1},{1,0},{2,3},{3,2},{4,5},{5,4},{6,7},{7,6},{8,9},{9,8},{10,11... | collective-permute-start | bytes 491528 | tf_op jit(solution)/shard_map/ppermute | solution.py:440
  19.7 2.2 %collective-permute-start.11 = (f32[16,2048]{1,0:T(8,128)S(1)}, f32[16,2048]{1,0:T(8,128)S(1)}, u32[]{:S(2)}, u32[]{:S(2)}) collective-permute-start(f32[16,2048]{1,0:T(8,128)S(1)} %get-tuple-element.29), channel_id=1, source_target_pairs={{0,4},{1,5},{2,6},{3,7},{4,0},{5,1},{6,2},{7,3},{8,12},{9,13},{10,... | collective-permute-start | bytes 393224 | tf_op jit(solution)/shard_map/ppermute | solution.py:432
  21.9 0.9 %collective-permute-start.7 = (f32[16,2048]{1,0:T(8,128)S(1)}, f32[16,2048]{1,0:T(8,128)S(1)}, u32[]{:S(2)}, u32[]{:S(2)}) collective-permute-start(f32[16,2048]{1,0:T(8,128)S(1)} %get-tuple-element.29), channel_id=1, source_target_pairs={{0,6},{1,7},{2,0},{3,1},{4,2},{5,3},{6,4},{7,5},{8,14},{9,15},{10,... | collective-permute-start | bytes 393224 | tf_op jit(solution)/shard_map/ppermute | solution.py:432
  22.8 0.0 collective-permute-done.5.far_ref
  22.9 0.5 collective-permute-start.6
  23.4 0.3 collective-permute-done.2.t2_ref
  23.7 1.0 %collective-permute-done.1.t1_ref = f32[8,4,8,256]{3,2,1,0:T(8,128)S(1)} collective-permute-done((f32[8,4,8,256]{3,2,1,0:T(8,128)S(1)}, f32[8,4,8,256]{3,2,1,0:T(8,128)S(1)}, u32[]{:S(2)}, u32[]{:S(2)}) %collective-permute-start.1) | collective-permute-done | bytes 262176 | tf_op jit(solution)/shard_map/ppermute | solution.py:425
  24.7 3.6 %shard_map.65 = (f32[16,7,8,128]{3,2,1,0:T(8,128)}, f32[8,5,8,256]{3,2,1,0:T(8,128)S(1)}, f32[8,5,8,256]{3,2,1,0:T(8,128)S(1)}, f32[8,8,8,256]{3,2,1,0:T(8,128)}) custom-call(s32[3]{0:T(128)S(1)} %pad_add_fusion.where_ref, f32[8,4,8,256]{3,2,1,0:T(8,128)S(1)} %collective-permute-done.1.t1_ref, f32[8,4,8,256]{3,2,1,0:T(8,128)S(1)} %all-to-all-done.to_ref, ...), custom_call_target="tpu_custom_call" | custom-call | flops 30000001024 | bytes 1048576 | tf_op jit(solution)/shard_map/pallas_call | solution.py:408
  28.3 3.7 %collective-permute-start.9 = (f32[8,5,8,256]{3,2,1,0:T(8,128)S(1)}, f32[8,5,8,256]{3,2,1,0:T(8,128)S(1)}, u32[]{:S(2)}, u32[]{:S(2)}) collective-permute-start(f32[8,5,8,256]{3,2,1,0:T(8,128)S(1)} %get-tuple-element.32), channel_id=1, source_target_pairs={{0,120},{8,16},{16,8},{24,32},{32,24},{40,48},{48,40},{56,64},{64,... | collective-permute-start | bytes 983048 | tf_op jit(solution)/shard_map/ppermute | solution.py:425
  32.0 0.0 collective-permute-start.8
  32.0 0.0 collective-permute-done.7
  32.0 0.0 collective-permute-done.6
  32.0 3.7 %all-to-all-start.1 = ((f32[16,7,8,128]{3,2,1,0:T(8,128)}), f32[16,7,8,128]{3,2,1,0:T(8,128)S(1)}, u32[]{:S(2)}, u32[]{:S(2)}) async-start(f32[16,7,8,128]{3,2,1,0:T(8,128)} %get-tuple-element.30), calls=%async_computation.1 | async-start | bytes 917504 | tf_op jit(solution)/shard_map/all_to_all | solution.py:497
  35.7 0.0 collective-permute-done.11
  35.8 3.2 %collective-permute-start.12 = (f32[4,16,2048]{2,1,0:T(8,128)S(1)}, f32[4,16,2048]{2,1,0:T(8,128)S(1)}, u32[]{:S(2)}, u32[]{:S(2)}) collective-permute-start(f32[4,16,2048]{2,1,0:T(8,128)S(1)} %pad_maximum_fusion.near_ref), channel_id=1, source_target_pairs={{0,1},{1,0},{2,3},{3,2},{4,5},{5,4},{6,7},{7,6},{8,9},{9,8},{10,11... | collective-permute-start | bytes 1572872 | tf_op jit(solution)/shard_map/ppermute | solution.py:440
  39.0 0.0 collective-permute-done.9.high_ref.second_ref
  39.0 0.0 collective-permute-done.8.low_ref.first_ref
  39.0 5.8 %all-to-all-done.1.got_ref = f32[16,7,8,128]{3,2,1,0:T(8,128)S(1)} async-done(((f32[16,7,8,128]{3,2,1,0:T(8,128)}), f32[16,7,8,128]{3,2,1,0:T(8,128)S(1)}, u32[]{:S(2)}, u32[]{:S(2)}) %all-to-all-start.1) | async-done | bytes 458784 | tf_op jit(solution)/shard_map/all_to_all | solution.py:497
  44.8 3.9 %collective-permute-start.10 = (f32[16,5,8,128]{3,2,1,0:T(8,128)S(1)}, f32[16,5,8,128]{3,2,1,0:T(8,128)S(1)}, u32[]{:S(2)}, u32[]{:S(2)}) collective-permute-start(f32[16,5,8,128]{3,2,1,0:T(8,128)S(1)} %slice.3), channel_id=1, source_target_pairs={{0,1},{1,0},{2,3},{3,2},{4,5},{5,4},{6,7},{7,6},{8,9},{9,8},{10,11... | collective-permute-start | bytes 983048 | tf_op jit(solution)/shard_map/ppermute | solution.py:440
  48.7 0.0 collective-permute-done.12.far_ref
  48.7 1.3 %collective-permute-done.10.other_ref = f32[16,5,8,128]{3,2,1,0:T(8,128)S(1)} collective-permute-done((f32[16,5,8,128]{3,2,1,0:T(8,128)S(1)}, f32[16,5,8,128]{3,2,1,0:T(8,128)S(1)}, u32[]{:S(2)}, u32[]{:S(2)}) %collective-permute-start.10) | collective-permute-done | bytes 327712 | tf_op jit(solution)/shard_map/ppermute | solution.py:440
  49.9 2.7 %shard_map.67 = (f32[16,1,128]{2,1,0:T(1,128)S(1)}, f32[10,10,8,128]{3,2,1,0:T(8,128)S(1)}, s32[12,8,128]{2,1,0:T(8,128)S(1)}) custom-call(s32[3]{0:T(128)S(1)} %pad_add_fusion.where_ref, f32[16,7,8,128]{3,2,1,0:T(8,128)S(1)} %all-to-all-done.1.got_ref, f32[16,5,8,128]{3,2,1,0:T(8,128)S(1)} %collective-permute-done.10.other_ref, ...), custom_call_target="tpu_custom_call" | custom-call | flops 1000000 | bytes 1048576 | tf_op jit(solution)/shard_map/pallas_call | solution.py:408
  52.6 9.5 %all_to_all.20.table_ref = f32[16,1,128]{2,1,0:T(1,128)S(1)} all-to-all(f32[16,1,128]{2,1,0:T(1,128)S(1)} %get-tuple-element.37), channel_id=1, replica_groups=mesh['gx'=16,'gy'=8] {'gx'}, dimensions={0} | all-to-all | bytes 16384 | tf_op jit(solution)/shard_map/all_to_all | solution.py:511
  62.2 3.3 %shard_map.68 = f32[8,4,8,256]{3,2,1,0:T(8,128)S(1)} custom-call(s32[3]{0:T(128)S(1)} %pad_add_fusion.where_ref, f32[16,1,128]{2,1,0:T(1,128)S(1)} %all_to_all.20.table_ref, f32[10,10,8,128]{3,2,1,0:T(8,128)S(1)} %get-tuple-element.38.window_ref, s32[12,8,128]{2,1,0:T(8,128)S(1)} %get-tuple-element.39.ids_ref, ...), custom_call_target="tpu_custom_call" | custom-call | flops 4000000000 | bytes 1048576 | tf_op jit(solution)/shard_map/pallas_call | solution.py:408
  65.5 11.3 %all_to_all.21 = f32[8,4,8,256]{3,2,1,0:T(8,128)S(1)} all-to-all(f32[8,4,8,256]{3,2,1,0:T(8,128)S(1)} %shard_map.68), channel_id=1, replica_groups=mesh['gx'=16,'gy'=8] {'gy'}, dimensions={0} | all-to-all | bytes 524288 | tf_op jit(solution)/shard_map/all_to_all | solution.py:526
  76.8 0.7 copy.8
  (4 shorter events, 0.1 us)
Async XLA Ops:
  0.0 13.3 %all-to-all-start = ((f32[8,4,8,256]{3,2,1,0:T(8,128)}), f32[8,4,8,256]{3,2,1,0:T(8,128)S(1)}, u32[]{:S(2)}, u32[]{:S(2)}) async-start(f32[8,4,8,256]{3,2,1,0:T(8,128)} %param.6), calls=%async_computation | async-start | bytes 524288 | tf_op jit(solution)/shard_map/all_to_all | solution.py:446
  8.5 4.2 %collective-permute-start = (f32[5,8,256]{2,1,0:T(8,128)S(1)}, f32[5,8,256]{2,1,0:T(8,128)S(1)}, u32[]{:S(2)}, u32[]{:S(2)}) collective-permute-start(f32[5,8,256]{2,1,0:T(8,128)S(1)} %get-tuple-element.23), channel_id=1, source_target_pairs={{0,6},{1,7},{2,0},{3,1},{4,2},{5,3},{6,4},{7,5},{8,14},{9,15},{10,... | collective-permute-start | bytes 122888 | tf_op jit(solution)/shard_map/ppermute | solution.py:432
  11.1 7.1 %collective-permute-start.4 = (f32[5,8,256]{2,1,0:T(8,128)S(1)}, f32[5,8,256]{2,1,0:T(8,128)S(1)}, u32[]{:S(2)}, u32[]{:S(2)}) collective-permute-start(f32[5,8,256]{2,1,0:T(8,128)S(1)} %get-tuple-element.23), channel_id=1, source_target_pairs={{0,4},{1,5},{2,6},{3,7},{4,0},{5,1},{6,2},{7,3},{8,12},{9,13},{10,... | collective-permute-start | bytes 122888 | tf_op jit(solution)/shard_map/ppermute | solution.py:432
  11.7 6.6 %collective-permute-start.3 = (f32[5,8,256]{2,1,0:T(8,128)S(1)}, f32[5,8,256]{2,1,0:T(8,128)S(1)}, u32[]{:S(2)}, u32[]{:S(2)}) collective-permute-start(f32[5,8,256]{2,1,0:T(8,128)S(1)} %get-tuple-element.23), channel_id=1, source_target_pairs={{0,2},{1,3},{2,4},{3,5},{4,6},{5,7},{6,0},{7,1},{8,10},{9,11},{10,... | collective-permute-start | bytes 122888 | tf_op jit(solution)/shard_map/ppermute | solution.py:432
  13.3 10.4 %collective-permute-start.2 = (f32[8,4,8,256]{3,2,1,0:T(8,128)S(1)}, f32[8,4,8,256]{3,2,1,0:T(8,128)S(1)}, u32[]{:S(2)}, u32[]{:S(2)}) collective-permute-start(f32[8,4,8,256]{3,2,1,0:T(8,128)S(1)} %all-to-all-done.to_ref), channel_id=1, source_target_pairs={{0,120},{8,16},{16,8},{24,32},{32,24},{40,48},{48,40},{56,64},{64,... | collective-permute-start | bytes 786440 | tf_op jit(solution)/shard_map/ppermute | solution.py:425
  18.2 6.5 %collective-permute-start.1 = (f32[8,4,8,256]{3,2,1,0:T(8,128)S(1)}, f32[8,4,8,256]{3,2,1,0:T(8,128)S(1)}, u32[]{:S(2)}, u32[]{:S(2)}) collective-permute-start(f32[8,4,8,256]{3,2,1,0:T(8,128)S(1)} %all-to-all-done.to_ref), channel_id=1, source_target_pairs={{0,8},{8,0},{16,24},{24,16},{32,40},{40,32},{48,56},{56,48},{64,72... | collective-permute-start | bytes 786440 | tf_op jit(solution)/shard_map/ppermute | solution.py:425
  18.3 4.6 %collective-permute-start.5 = (f32[4,5,8,256]{3,2,1,0:T(8,128)S(1)}, f32[4,5,8,256]{3,2,1,0:T(8,128)S(1)}, u32[]{:S(2)}, u32[]{:S(2)}) collective-permute-start(f32[4,5,8,256]{3,2,1,0:T(8,128)S(1)} %pad_maximum_fusion.1.near_ref), channel_id=1, source_target_pairs={{0,1},{1,0},{2,3},{3,2},{4,5},{5,4},{6,7},{7,6},{8,9},{9,8},{10,11... | collective-permute-start | bytes 491528 | tf_op jit(solution)/shard_map/ppermute | solution.py:440
  19.7 16.1 %collective-permute-start.11 = (f32[16,2048]{1,0:T(8,128)S(1)}, f32[16,2048]{1,0:T(8,128)S(1)}, u32[]{:S(2)}, u32[]{:S(2)}) collective-permute-start(f32[16,2048]{1,0:T(8,128)S(1)} %get-tuple-element.29), channel_id=1, source_target_pairs={{0,4},{1,5},{2,6},{3,7},{4,0},{5,1},{6,2},{7,3},{8,12},{9,13},{10,... | collective-permute-start | bytes 393224 | tf_op jit(solution)/shard_map/ppermute | solution.py:432
  21.9 10.1 %collective-permute-start.7 = (f32[16,2048]{1,0:T(8,128)S(1)}, f32[16,2048]{1,0:T(8,128)S(1)}, u32[]{:S(2)}, u32[]{:S(2)}) collective-permute-start(f32[16,2048]{1,0:T(8,128)S(1)} %get-tuple-element.29), channel_id=1, source_target_pairs={{0,6},{1,7},{2,0},{3,1},{4,2},{5,3},{6,4},{7,5},{8,14},{9,15},{10,... | collective-permute-start | bytes 393224 | tf_op jit(solution)/shard_map/ppermute | solution.py:432
  22.9 9.1 %collective-permute-start.6 = (f32[16,2048]{1,0:T(8,128)S(1)}, f32[16,2048]{1,0:T(8,128)S(1)}, u32[]{:S(2)}, u32[]{:S(2)}) collective-permute-start(f32[16,2048]{1,0:T(8,128)S(1)} %get-tuple-element.29), channel_id=1, source_target_pairs={{0,2},{1,3},{2,4},{3,5},{4,6},{5,7},{6,0},{7,1},{8,10},{9,11},{10,... | collective-permute-start | bytes 393224 | tf_op jit(solution)/shard_map/ppermute | solution.py:432
  28.3 10.7 %collective-permute-start.9 = (f32[8,5,8,256]{3,2,1,0:T(8,128)S(1)}, f32[8,5,8,256]{3,2,1,0:T(8,128)S(1)}, u32[]{:S(2)}, u32[]{:S(2)}) collective-permute-start(f32[8,5,8,256]{3,2,1,0:T(8,128)S(1)} %get-tuple-element.32), channel_id=1, source_target_pairs={{0,120},{8,16},{16,8},{24,32},{32,24},{40,48},{48,40},{56,64},{64,... | collective-permute-start | bytes 983048 | tf_op jit(solution)/shard_map/ppermute | solution.py:425
  32.0 7.0 %collective-permute-start.8 = (f32[8,5,8,256]{3,2,1,0:T(8,128)S(1)}, f32[8,5,8,256]{3,2,1,0:T(8,128)S(1)}, u32[]{:S(2)}, u32[]{:S(2)}) collective-permute-start(f32[8,5,8,256]{3,2,1,0:T(8,128)S(1)} %get-tuple-element.31.own_ref), channel_id=1, source_target_pairs={{0,8},{8,0},{16,24},{24,16},{32,40},{40,32},{48,56},{56,48},{64,72... | collective-permute-start | bytes 983048 | tf_op jit(solution)/shard_map/ppermute | solution.py:425
  32.0 12.8 %all-to-all-start.1 = ((f32[16,7,8,128]{3,2,1,0:T(8,128)}), f32[16,7,8,128]{3,2,1,0:T(8,128)S(1)}, u32[]{:S(2)}, u32[]{:S(2)}) async-start(f32[16,7,8,128]{3,2,1,0:T(8,128)} %get-tuple-element.30), calls=%async_computation.1 | async-start | bytes 917504 | tf_op jit(solution)/shard_map/all_to_all | solution.py:497
  35.8 12.9 %collective-permute-start.12 = (f32[4,16,2048]{2,1,0:T(8,128)S(1)}, f32[4,16,2048]{2,1,0:T(8,128)S(1)}, u32[]{:S(2)}, u32[]{:S(2)}) collective-permute-start(f32[4,16,2048]{2,1,0:T(8,128)S(1)} %pad_maximum_fusion.near_ref), channel_id=1, source_target_pairs={{0,1},{1,0},{2,3},{3,2},{4,5},{5,4},{6,7},{7,6},{8,9},{9,8},{10,11... | collective-permute-start | bytes 1572872 | tf_op jit(solution)/shard_map/ppermute | solution.py:440
  44.8 5.1 %collective-permute-start.10 = (f32[16,5,8,128]{3,2,1,0:T(8,128)S(1)}, f32[16,5,8,128]{3,2,1,0:T(8,128)S(1)}, u32[]{:S(2)}, u32[]{:S(2)}) collective-permute-start(f32[16,5,8,128]{3,2,1,0:T(8,128)S(1)} %slice.3), channel_id=1, source_target_pairs={{0,1},{1,0},{2,3},{3,2},{4,5},{5,4},{6,7},{7,6},{8,9},{9,8},{10,11... | collective-permute-start | bytes 983048 | tf_op jit(solution)/shard_map/ppermute | solution.py:440

commit v7 on v6

--- a/solution.py
+++ b/solution.py
@@ -288,9 +288,9 @@
     low_iota = lax.broadcasted_iota(jnp.int32, (HALF, LANES), 0)
     pieces = [piece.astype(F32) for piece in split3(residual)[:2]]
     counted = jnp.zeros((2 * NC2 // HALF, HALF), F32)
-    for x in range(NAX):
+    for start in range(0, NAX, 4):
         left, right = [], []
-        for k in range(YT):
+        for x, k in [(x, k) for x in range(start, start + 4) for k in range(YT)]:
             hit = high_of[x, k : k + 1] == high_iota
             left.append(
                 jnp.concatenate([jnp.where(hit, piece[x, k : k + 1], 0.0).astype(BF16) for piece in pieces], axis=0)

time: 77.9 us -> 77.9 us (level)
  no operation moved by 1% of the time
where the time goes in v7:
time: 77.9 us; the launch traced here: 77.5 us
  starting transfers between devices  35.1 us (45%)
  blocking collectives  20.8 us (27%)
  Pallas kernels  11.2 us (14%)
  waiting for transfers between devices  9.46 us (12%)
    all_to_all x1, blocking collectives, local(): return lax.all_to_all(out, 'gy', 0, 0, tiled=True)  11.3 us
    pallas_call x5, Pallas kernels, run(): pl.pallas_call(kernel, out_shape=out_shape, in_specs=[spec(k) for k in ra...  11.2 us
    all_to_all x1, blocking collectives, local(): table = lax.all_to_all(send, 'gx', 0, 0, tiled=True)  9.53 us
    ppermute x4, starting transfers between devices, beside(): return (lax.ppermute(first, 'gx', one), lax.ppermute(second, 'gx', two))  8.62 us
    ppermute x3, starting transfers between devices, other_core(): return lax.ppermute(value, 'gy', [(j, j ^ 1) for j in range(GY)])  8.44 us
    ppermute x6, starting transfers between devices, chip_below(): lax.ppermute(value, 'gy', [(j, (j + 2 * step) % GY) for j in range(GY)])  7.51 us
    all_to_all x1, starting transfers between devices, local(): cells = lax.all_to_all(right_side, 'gy', 0, 0, tiled=True)  6.81 us
    all_to_all x1, waiting for transfers between devices, local(): got = lax.all_to_all(send, 'gx', 0, 0, tiled=True)  5.8 us
  transfers between devices with their start and end apart: 15, of which 6 were waited for; matrix products, arithmetic and copies ran while one was open for 0% of the time, Pallas kernels for 7%

profile of v7, /device:TPU:1, one launch (start us, length us, event | category | flops | bytes accessed | tf_op | source)
XLA Modules:
  0.0 77.5 jit_solution(3651381513596094233)
XLA Ops:
  0.0 6.8 %all-to-all-start = ((f32[8,4,8,256]{3,2,1,0:T(8,128)}), f32[8,4,8,256]{3,2,1,0:T(8,128)S(1)}, u32[]{:S(2)}, u32[]{:S(2)}) async-start(f32[8,4,8,256]{3,2,1,0:T(8,128)} %param.6), calls=%async_computation | async-start | bytes 524288 | tf_op jit(solution)/shard_map/all_to_all | solution.py:446
  6.8 0.1 pad_add_fusion.where_ref
  6.9 1.6 %shard_map.64 = (f32[5,8,256]{2,1,0:T(8,128)S(1)}, f32[16,2048]{1,0:T(8,128)S(1)}) custom-call(s32[3]{0:T(128)S(1)} %pad_add_fusion.where_ref, s32[4,8,256]{2,1,0:T(8,128)} %ids_ref.1, f32[2,2,64]{2,1,0:T(2,128)} %diag_ref.1, f32[6,2,2,64]{3,2,1,0:T(2,128)} %links_ref.1, s32[2,2,64]{2,1,0:T(2,128)} %coarse_ids_ref.1, f32[16,2048]{1,0:T(8,128)} %inverse_hbm.1), custom_call_target="tpu_custom_call" | custom-call | flops 100000000 | bytes 1048576 | tf_op jit(solution)/shard_map/pallas_call | solution.py:408
  8.5 2.7 %collective-permute-start = (f32[5,8,256]{2,1,0:T(8,128)S(1)}, f32[5,8,256]{2,1,0:T(8,128)S(1)}, u32[]{:S(2)}, u32[]{:S(2)}) collective-permute-start(f32[5,8,256]{2,1,0:T(8,128)S(1)} %get-tuple-element.23), channel_id=1, source_target_pairs={{0,6},{1,7},{2,0},{3,1},{4,2},{5,3},{6,4},{7,5},{8,14},{9,15},{10,... | collective-permute-start | bytes 122888 | tf_op jit(solution)/shard_map/ppermute | solution.py:432
  11.1 0.6 collective-permute-start.4
  11.7 0.6 collective-permute-start.3
  12.3 0.3 collective-permute-done
  12.6 0.7 all-to-all-done.to_ref
  13.3 4.9 %collective-permute-start.2 = (f32[8,4,8,256]{3,2,1,0:T(8,128)S(1)}, f32[8,4,8,256]{3,2,1,0:T(8,128)S(1)}, u32[]{:S(2)}, u32[]{:S(2)}) collective-permute-start(f32[8,4,8,256]{3,2,1,0:T(8,128)S(1)} %all-to-all-done.to_ref), channel_id=1, source_target_pairs={{0,120},{8,16},{16,8},{24,32},{32,24},{40,48},{48,40},{56,64},{64,... | collective-permute-start | bytes 786440 | tf_op jit(solution)/shard_map/ppermute | solution.py:425
  18.2 0.0 collective-permute-start.1
  18.3 0.0 collective-permute-done.4
  18.3 0.0 collective-permute-done.3
  18.3 1.4 %collective-permute-start.5 = (f32[4,5,8,256]{3,2,1,0:T(8,128)S(1)}, f32[4,5,8,256]{3,2,1,0:T(8,128)S(1)}, u32[]{:S(2)}, u32[]{:S(2)}) collective-permute-start(f32[4,5,8,256]{3,2,1,0:T(8,128)S(1)} %pad_maximum_fusion.1.near_ref), channel_id=1, source_target_pairs={{0,1},{1,0},{2,3},{3,2},{4,5},{5,4},{6,7},{7,6},{8,9},{9,8},{10,11... | collective-permute-start | bytes 491528 | tf_op jit(solution)/shard_map/ppermute | solution.py:440
  19.7 2.2 %collective-permute-start.11 = (f32[16,2048]{1,0:T(8,128)S(1)}, f32[16,2048]{1,0:T(8,128)S(1)}, u32[]{:S(2)}, u32[]{:S(2)}) collective-permute-start(f32[16,2048]{1,0:T(8,128)S(1)} %get-tuple-element.29), channel_id=1, source_target_pairs={{0,4},{1,5},{2,6},{3,7},{4,0},{5,1},{6,2},{7,3},{8,12},{9,13},{10,... | collective-permute-start | bytes 393224 | tf_op jit(solution)/shard_map/ppermute | solution.py:432
  21.9 0.9 %collective-permute-start.7 = (f32[16,2048]{1,0:T(8,128)S(1)}, f32[16,2048]{1,0:T(8,128)S(1)}, u32[]{:S(2)}, u32[]{:S(2)}) collective-permute-start(f32[16,2048]{1,0:T(8,128)S(1)} %get-tuple-element.29), channel_id=1, source_target_pairs={{0,6},{1,7},{2,0},{3,1},{4,2},{5,3},{6,4},{7,5},{8,14},{9,15},{10,... | collective-permute-start | bytes 393224 | tf_op jit(solution)/shard_map/ppermute | solution.py:432
  22.8 0.0 collective-permute-done.5.far_ref
  22.9 0.5 collective-permute-start.6
  23.4 0.3 collective-permute-done.2.t2_ref
  23.7 1.0 %collective-permute-done.1.t1_ref = f32[8,4,8,256]{3,2,1,0:T(8,128)S(1)} collective-permute-done((f32[8,4,8,256]{3,2,1,0:T(8,128)S(1)}, f32[8,4,8,256]{3,2,1,0:T(8,128)S(1)}, u32[]{:S(2)}, u32[]{:S(2)}) %collective-permute-start.1) | collective-permute-done | bytes 262176 | tf_op jit(solution)/shard_map/ppermute | solution.py:425
  24.7 3.6 %shard_map.65 = (f32[16,7,8,128]{3,2,1,0:T(8,128)}, f32[8,5,8,256]{3,2,1,0:T(8,128)S(1)}, f32[8,5,8,256]{3,2,1,0:T(8,128)S(1)}, f32[8,8,8,256]{3,2,1,0:T(8,128)}) custom-call(s32[3]{0:T(128)S(1)} %pad_add_fusion.where_ref, f32[8,4,8,256]{3,2,1,0:T(8,128)S(1)} %collective-permute-done.1.t1_ref, f32[8,4,8,256]{3,2,1,0:T(8,128)S(1)} %all-to-all-done.to_ref, ...), custom_call_target="tpu_custom_call" | custom-call | flops 30000001024 | bytes 1048576 | tf_op jit(solution)/shard_map/pallas_call | solution.py:408
  28.3 3.7 %collective-permute-start.9 = (f32[8,5,8,256]{3,2,1,0:T(8,128)S(1)}, f32[8,5,8,256]{3,2,1,0:T(8,128)S(1)}, u32[]{:S(2)}, u32[]{:S(2)}) collective-permute-start(f32[8,5,8,256]{3,2,1,0:T(8,128)S(1)} %get-tuple-element.32), channel_id=1, source_target_pairs={{0,120},{8,16},{16,8},{24,32},{32,24},{40,48},{48,40},{56,64},{64,... | collective-permute-start | bytes 983048 | tf_op jit(solution)/shard_map/ppermute | solution.py:425
  32.0 0.0 collective-permute-start.8
  32.0 0.0 collective-permute-done.7
  32.0 0.0 collective-permute-done.6
  32.0 3.7 %all-to-all-start.1 = ((f32[16,7,8,128]{3,2,1,0:T(8,128)}), f32[16,7,8,128]{3,2,1,0:T(8,128)S(1)}, u32[]{:S(2)}, u32[]{:S(2)}) async-start(f32[16,7,8,128]{3,2,1,0:T(8,128)} %get-tuple-element.30), calls=%async_computation.1 | async-start | bytes 917504 | tf_op jit(solution)/shard_map/all_to_all | solution.py:497
  35.7 0.0 collective-permute-done.11
  35.8 3.2 %collective-permute-start.12 = (f32[4,16,2048]{2,1,0:T(8,128)S(1)}, f32[4,16,2048]{2,1,0:T(8,128)S(1)}, u32[]{:S(2)}, u32[]{:S(2)}) collective-permute-start(f32[4,16,2048]{2,1,0:T(8,128)S(1)} %pad_maximum_fusion.near_ref), channel_id=1, source_target_pairs={{0,1},{1,0},{2,3},{3,2},{4,5},{5,4},{6,7},{7,6},{8,9},{9,8},{10,11... | collective-permute-start | bytes 1572872 | tf_op jit(solution)/shard_map/ppermute | solution.py:440
  39.0 0.0 collective-permute-done.9.high_ref.second_ref
  39.0 0.0 collective-permute-done.8.low_ref.first_ref
  39.0 5.8 %all-to-all-done.1.got_ref = f32[16,7,8,128]{3,2,1,0:T(8,128)S(1)} async-done(((f32[16,7,8,128]{3,2,1,0:T(8,128)}), f32[16,7,8,128]{3,2,1,0:T(8,128)S(1)}, u32[]{:S(2)}, u32[]{:S(2)}) %all-to-all-start.1) | async-done | bytes 458784 | tf_op jit(solution)/shard_map/all_to_all | solution.py:497
  44.8 3.9 %collective-permute-start.10 = (f32[16,5,8,128]{3,2,1,0:T(8,128)S(1)}, f32[16,5,8,128]{3,2,1,0:T(8,128)S(1)}, u32[]{:S(2)}, u32[]{:S(2)}) collective-permute-start(f32[16,5,8,128]{3,2,1,0:T(8,128)S(1)} %slice.3), channel_id=1, source_target_pairs={{0,1},{1,0},{2,3},{3,2},{4,5},{5,4},{6,7},{7,6},{8,9},{9,8},{10,11... | collective-permute-start | bytes 983048 | tf_op jit(solution)/shard_map/ppermute | solution.py:440
  48.7 0.0 collective-permute-done.12.far_ref
  48.7 1.3 %collective-permute-done.10.other_ref = f32[16,5,8,128]{3,2,1,0:T(8,128)S(1)} collective-permute-done((f32[16,5,8,128]{3,2,1,0:T(8,128)S(1)}, f32[16,5,8,128]{3,2,1,0:T(8,128)S(1)}, u32[]{:S(2)}, u32[]{:S(2)}) %collective-permute-start.10) | collective-permute-done | bytes 327712 | tf_op jit(solution)/shard_map/ppermute | solution.py:440
  49.9 2.7 %shard_map.67 = (f32[16,1,128]{2,1,0:T(1,128)S(1)}, f32[10,10,8,128]{3,2,1,0:T(8,128)S(1)}, s32[12,8,128]{2,1,0:T(8,128)S(1)}) custom-call(s32[3]{0:T(128)S(1)} %pad_add_fusion.where_ref, f32[16,7,8,128]{3,2,1,0:T(8,128)S(1)} %all-to-all-done.1.got_ref, f32[16,5,8,128]{3,2,1,0:T(8,128)S(1)} %collective-permute-done.10.other_ref, ...), custom_call_target="tpu_custom_call" | custom-call | flops 1000000 | bytes 1048576 | tf_op jit(solution)/shard_map/pallas_call | solution.py:408
  52.7 9.5 %all_to_all.20.table_ref = f32[16,1,128]{2,1,0:T(1,128)S(1)} all-to-all(f32[16,1,128]{2,1,0:T(1,128)S(1)} %get-tuple-element.37), channel_id=1, replica_groups=mesh['gx'=16,'gy'=8] {'gx'}, dimensions={0} | all-to-all | bytes 16384 | tf_op jit(solution)/shard_map/all_to_all | solution.py:511
  62.2 3.3 %shard_map.68 = f32[8,4,8,256]{3,2,1,0:T(8,128)S(1)} custom-call(s32[3]{0:T(128)S(1)} %pad_add_fusion.where_ref, f32[16,1,128]{2,1,0:T(1,128)S(1)} %all_to_all.20.table_ref, f32[10,10,8,128]{3,2,1,0:T(8,128)S(1)} %get-tuple-element.38.window_ref, s32[12,8,128]{2,1,0:T(8,128)S(1)} %get-tuple-element.39.ids_ref, ...), custom_call_target="tpu_custom_call" | custom-call | flops 4000000000 | bytes 1048576 | tf_op jit(solution)/shard_map/pallas_call | solution.py:408
  65.5 11.3 %all_to_all.21 = f32[8,4,8,256]{3,2,1,0:T(8,128)S(1)} all-to-all(f32[8,4,8,256]{3,2,1,0:T(8,128)S(1)} %shard_map.68), channel_id=1, replica_groups=mesh['gx'=16,'gy'=8] {'gy'}, dimensions={0} | all-to-all | bytes 524288 | tf_op jit(solution)/shard_map/all_to_all | solution.py:526
  76.8 0.7 copy.8
  (4 shorter events, 0.1 us)
Async XLA Ops:
  0.0 13.3 %all-to-all-start = ((f32[8,4,8,256]{3,2,1,0:T(8,128)}), f32[8,4,8,256]{3,2,1,0:T(8,128)S(1)}, u32[]{:S(2)}, u32[]{:S(2)}) async-start(f32[8,4,8,256]{3,2,1,0:T(8,128)} %param.6), calls=%async_computation | async-start | bytes 524288 | tf_op jit(solution)/shard_map/all_to_all | solution.py:446
  8.5 4.2 %collective-permute-start = (f32[5,8,256]{2,1,0:T(8,128)S(1)}, f32[5,8,256]{2,1,0:T(8,128)S(1)}, u32[]{:S(2)}, u32[]{:S(2)}) collective-permute-start(f32[5,8,256]{2,1,0:T(8,128)S(1)} %get-tuple-element.23), channel_id=1, source_target_pairs={{0,6},{1,7},{2,0},{3,1},{4,2},{5,3},{6,4},{7,5},{8,14},{9,15},{10,... | collective-permute-start | bytes 122888 | tf_op jit(solution)/shard_map/ppermute | solution.py:432
  11.1 7.1 %collective-permute-start.4 = (f32[5,8,256]{2,1,0:T(8,128)S(1)}, f32[5,8,256]{2,1,0:T(8,128)S(1)}, u32[]{:S(2)}, u32[]{:S(2)}) collective-permute-start(f32[5,8,256]{2,1,0:T(8,128)S(1)} %get-tuple-element.23), channel_id=1, source_target_pairs={{0,4},{1,5},{2,6},{3,7},{4,0},{5,1},{6,2},{7,3},{8,12},{9,13},{10,... | collective-permute-start | bytes 122888 | tf_op jit(solution)/shard_map/ppermute | solution.py:432
  11.7 6.6 %collective-permute-start.3 = (f32[5,8,256]{2,1,0:T(8,128)S(1)}, f32[5,8,256]{2,1,0:T(8,128)S(1)}, u32[]{:S(2)}, u32[]{:S(2)}) collective-permute-start(f32[5,8,256]{2,1,0:T(8,128)S(1)} %get-tuple-element.23), channel_id=1, source_target_pairs={{0,2},{1,3},{2,4},{3,5},{4,6},{5,7},{6,0},{7,1},{8,10},{9,11},{10,... | collective-permute-start | bytes 122888 | tf_op jit(solution)/shard_map/ppermute | solution.py:432
  13.3 10.4 %collective-permute-start.2 = (f32[8,4,8,256]{3,2,1,0:T(8,128)S(1)}, f32[8,4,8,256]{3,2,1,0:T(8,128)S(1)}, u32[]{:S(2)}, u32[]{:S(2)}) collective-permute-start(f32[8,4,8,256]{3,2,1,0:T(8,128)S(1)} %all-to-all-done.to_ref), channel_id=1, source_target_pairs={{0,120},{8,16},{16,8},{24,32},{32,24},{40,48},{48,40},{56,64},{64,... | collective-permute-start | bytes 786440 | tf_op jit(solution)/shard_map/ppermute | solution.py:425
  18.2 6.5 %collective-permute-start.1 = (f32[8,4,8,256]{3,2,1,0:T(8,128)S(1)}, f32[8,4,8,256]{3,2,1,0:T(8,128)S(1)}, u32[]{:S(2)}, u32[]{:S(2)}) collective-permute-start(f32[8,4,8,256]{3,2,1,0:T(8,128)S(1)} %all-to-all-done.to_ref), channel_id=1, source_target_pairs={{0,8},{8,0},{16,24},{24,16},{32,40},{40,32},{48,56},{56,48},{64,72... | collective-permute-start | bytes 786440 | tf_op jit(solution)/shard_map/ppermute | solution.py:425
  18.3 4.6 %collective-permute-start.5 = (f32[4,5,8,256]{3,2,1,0:T(8,128)S(1)}, f32[4,5,8,256]{3,2,1,0:T(8,128)S(1)}, u32[]{:S(2)}, u32[]{:S(2)}) collective-permute-start(f32[4,5,8,256]{3,2,1,0:T(8,128)S(1)} %pad_maximum_fusion.1.near_ref), channel_id=1, source_target_pairs={{0,1},{1,0},{2,3},{3,2},{4,5},{5,4},{6,7},{7,6},{8,9},{9,8},{10,11... | collective-permute-start | bytes 491528 | tf_op jit(solution)/shard_map/ppermute | solution.py:440
  19.7 16.1 %collective-permute-start.11 = (f32[16,2048]{1,0:T(8,128)S(1)}, f32[16,2048]{1,0:T(8,128)S(1)}, u32[]{:S(2)}, u32[]{:S(2)}) collective-permute-start(f32[16,2048]{1,0:T(8,128)S(1)} %get-tuple-element.29), channel_id=1, source_target_pairs={{0,4},{1,5},{2,6},{3,7},{4,0},{5,1},{6,2},{7,3},{8,12},{9,13},{10,... | collective-permute-start | bytes 393224 | tf_op jit(solution)/shard_map/ppermute | solution.py:432
  21.9 10.1 %collective-permute-start.7 = (f32[16,2048]{1,0:T(8,128)S(1)}, f32[16,2048]{1,0:T(8,128)S(1)}, u32[]{:S(2)}, u32[]{:S(2)}) collective-permute-start(f32[16,2048]{1,0:T(8,128)S(1)} %get-tuple-element.29), channel_id=1, source_target_pairs={{0,6},{1,7},{2,0},{3,1},{4,2},{5,3},{6,4},{7,5},{8,14},{9,15},{10,... | collective-permute-start | bytes 393224 | tf_op jit(solution)/shard_map/ppermute | solution.py:432
  22.9 9.1 %collective-permute-start.6 = (f32[16,2048]{1,0:T(8,128)S(1)}, f32[16,2048]{1,0:T(8,128)S(1)}, u32[]{:S(2)}, u32[]{:S(2)}) collective-permute-start(f32[16,2048]{1,0:T(8,128)S(1)} %get-tuple-element.29), channel_id=1, source_target_pairs={{0,2},{1,3},{2,4},{3,5},{4,6},{5,7},{6,0},{7,1},{8,10},{9,11},{10,... | collective-permute-start | bytes 393224 | tf_op jit(solution)/shard_map/ppermute | solution.py:432
  28.3 10.7 %collective-permute-start.9 = (f32[8,5,8,256]{3,2,1,0:T(8,128)S(1)}, f32[8,5,8,256]{3,2,1,0:T(8,128)S(1)}, u32[]{:S(2)}, u32[]{:S(2)}) collective-permute-start(f32[8,5,8,256]{3,2,1,0:T(8,128)S(1)} %get-tuple-element.32), channel_id=1, source_target_pairs={{0,120},{8,16},{16,8},{24,32},{32,24},{40,48},{48,40},{56,64},{64,... | collective-permute-start | bytes 983048 | tf_op jit(solution)/shard_map/ppermute | solution.py:425
  32.0 7.0 %collective-permute-start.8 = (f32[8,5,8,256]{3,2,1,0:T(8,128)S(1)}, f32[8,5,8,256]{3,2,1,0:T(8,128)S(1)}, u32[]{:S(2)}, u32[]{:S(2)}) collective-permute-start(f32[8,5,8,256]{3,2,1,0:T(8,128)S(1)} %get-tuple-element.31.own_ref), channel_id=1, source_target_pairs={{0,8},{8,0},{16,24},{24,16},{32,40},{40,32},{48,56},{56,48},{64,72... | collective-permute-start | bytes 983048 | tf_op jit(solution)/shard_map/ppermute | solution.py:425
  32.0 12.8 %all-to-all-start.1 = ((f32[16,7,8,128]{3,2,1,0:T(8,128)}), f32[16,7,8,128]{3,2,1,0:T(8,128)S(1)}, u32[]{:S(2)}, u32[]{:S(2)}) async-start(f32[16,7,8,128]{3,2,1,0:T(8,128)} %get-tuple-element.30), calls=%async_computation.1 | async-start | bytes 917504 | tf_op jit(solution)/shard_map/all_to_all | solution.py:497
  35.8 12.9 %collective-permute-start.12 = (f32[4,16,2048]{2,1,0:T(8,128)S(1)}, f32[4,16,2048]{2,1,0:T(8,128)S(1)}, u32[]{:S(2)}, u32[]{:S(2)}) collective-permute-start(f32[4,16,2048]{2,1,0:T(8,128)S(1)} %pad_maximum_fusion.near_ref), channel_id=1, source_target_pairs={{0,1},{1,0},{2,3},{3,2},{4,5},{5,4},{6,7},{7,6},{8,9},{9,8},{10,11... | collective-permute-start | bytes 1572872 | tf_op jit(solution)/shard_map/ppermute | solution.py:440
  44.8 5.1 %collective-permute-start.10 = (f32[16,5,8,128]{3,2,1,0:T(8,128)S(1)}, f32[16,5,8,128]{3,2,1,0:T(8,128)S(1)}, u32[]{:S(2)}, u32[]{:S(2)}) collective-permute-start(f32[16,5,8,128]{3,2,1,0:T(8,128)S(1)} %slice.3), channel_id=1, source_target_pairs={{0,1},{1,0},{2,3},{3,2},{4,5},{5,4},{6,7},{7,6},{8,9},{9,8},{10,11... | collective-permute-start | bytes 983048 | tf_op jit(solution)/shard_map/ppermute | solution.py:440
